TPU v7x, 32 devices: a whole 2x2x4 slice. The times are simulated.
32 devices in a mesh: edp: 4 (over z), ep: 8 (over y, x, core).
Axes of the slice: x: 2, y: 2, z: 4, core: 2. Of those that a mesh axis runs over, the one named last changes fastest.
Arguments:
- token_acts: bfloat16 [4, 8, 2, 64, 1024], P('edp', 'ep'), may hold values from -6 to 6
- out_grad: bfloat16 [4, 8, 3584, 128], P('edp', 'ep'), may hold values from -0.59765625 to 0.59765625
- counts: int32 [4, 8, 2], P('edp', 'ep'), may hold values from 1 to 64, as said below
- params: float32 [8, 3584, 1024], P('ep', 'edp'), may hold values from -3 to 3
- first_moment: bfloat16 [8, 3584, 1024], P('ep', 'edp'), may hold values from -3 to 3
- second_moment: bfloat16 [8, 3584, 1024], P('ep', 'edp'), may hold values from 0.049804688 to 2
- old_expert: int32 [8], replicated, may hold values from 0 to 7, each once
- replica_of: int32 [8], replicated, may hold values from 0 to 7
- new_expert: int32 [8], replicated, may hold values from 0 to 7, each once
Outputs:
- update_step: float32 [8, 3584, 1024], P('ep', 'edp')
- new_first: bfloat16 [8, 3584, 1024], P('ep', 'edp')
- new_second: bfloat16 [8, 3584, 1024], P('ep', 'edp')
Inputs may be any that keep to these rules, and one draw needn't show every extreme that they name: `counts`: every slot has at least one live token; some slot is full and some slot has exactly one live token in every draw. `old_expert`: each expert appears exactly once. `new_expert`: each expert appears exactly once. `replica_of`: any expert may be served by any number of replica slots, its owner's included.
All inputs are finite; a program needn't handle non-finite values.
Results may differ from a plain program's by a relative error of at most 0.015.
Values may be sent and summed in bfloat16 or wider, within the bound.
No kernel may reach another device: no remote copies, remote signals or barrier semaphores. Data moves between devices by JAX's collectives and lax.ppermute only.
A program may use at most 128 MiB of HBM per device.

v0:
```python
import functools

import jax
import jax.numpy as jnp
from jax import lax
from jax.experimental import pallas as pl
from jax.experimental.pallas import tpu as pltpu
from jax.sharding import PartitionSpec as P

beta_one = 0.9
beta_two = 0.95
bias_one = 0.9999734386011124
bias_two = 0.994079470779666
decay_rate = 0.1
adam_eps = 1e-08

BF = jnp.bfloat16
F32 = jnp.float32
CHUNK = 16
LIMIT = 56 * 1024 * 1024


def adam_update(weights, first_old, second_old, gradient):
    first_new = beta_one * first_old.astype(F32) + (1.0 - beta_one) * gradient
    second_new = beta_two * second_old.astype(F32) + (1.0 - beta_two) * gradient * gradient
    scaled = first_new / bias_one / (jnp.sqrt(second_new / bias_two) + adam_eps)
    step_new = -(scaled + decay_rate * weights)
    return step_new, first_new, second_new


def mask_kernel(counts, acts, out):
    slots, tok, _ = acts.shape
    row = lax.broadcasted_iota(jnp.int32, (tok, 1), 0)
    for s in range(slots):
        out[s] = jnp.where(row < counts[s], acts[s], jnp.zeros_like(acts[s]))


def pack_kernel(me, params, first, second, *outs):
    at = pl.program_id(0)
    for j, out in enumerate(outs):

        @pl.when(at == j)
        def _(out=out):
            out[0] = params[...].astype(BF)
            out[1] = first[...]
            out[2] = second[...]


def grad_kernel(me, grads, acts, *refs):
    outs, table = refs[:-1], refs[-1]
    at = pl.program_id(0)
    groups, slots, tok, hidden = acts.shape

    @pl.when(at == 0)
    def _():
        zero = jnp.zeros((tok, hidden), BF)
        for g in range(groups):
            for t in range(slots):
                for s in range(slots):
                    rows = pl.ds((g * slots + t) * tok, tok)
                    table[rows, pl.ds(s * hidden, hidden)] = acts[g, s] if s == t else zero

    left = jnp.concatenate([grads[g] for g in range(groups)], axis=1)
    total = jnp.dot(left, table[...], preferred_element_type=F32).astype(BF)
    for j, out in enumerate(outs):

        @pl.when(at == j)
        def _(out=out):
            for s in range(slots):
                out[s] = total[:, s * hidden : (s + 1) * hidden]


def update_kernel(n, me_ref, old, rep, new, *refs):
    params, first, second = refs[:3]
    state = refs[3 : 3 + n - 1]
    grads = refs[2 + n : 2 + 2 * n]
    outs = refs[2 + 2 * n : 2 + 3 * n]
    sums, placed, owner, target = refs[2 + 3 * n :]
    me = me_ref[0]
    for e in range(n):
        owner[old[e]] = e
        target[new[e]] = e
    for k in range(n):
        sums[k] = grads[k][0].astype(F32)
    for k in range(n):
        at = me ^ owner[rep[me ^ k]]
        sums[at] = sums[at] + grads[k][1].astype(F32)
    for k in range(n):
        if k == 0:
            old_state = (params[...], first[...], second[...])
        else:
            old_state = (state[k - 1][0].astype(F32), state[k - 1][1], state[k - 1][2])
        step_new, first_new, second_new = adam_update(*old_state, sums[k])
        to = me ^ target[old[me ^ k]]
        placed[to, 0] = step_new.astype(BF)
        placed[to, 1] = first_new.astype(BF)
        placed[to, 2] = second_new.astype(BF)
    for k in range(n):
        outs[k][...] = placed[k]


def unpack_kernel(me, *refs):
    pieces, (step, first, second) = refs[:-3], refs[-3:]
    at = pl.program_id(0)
    for j, piece in enumerate(pieces):

        @pl.when(at == j)
        def _(piece=piece):
            step[...] = piece[0].astype(F32)
            first[...] = piece[1]
            second[...] = piece[2]


def call(kernel, prefetch, grid, in_specs, out_specs, out_shape, scratch=()):
    return pl.pallas_call(
        kernel,
        grid_spec=pltpu.PrefetchScalarGridSpec(
            num_scalar_prefetch=prefetch,
            grid=grid,
            in_specs=in_specs,
            out_specs=out_specs,
            scratch_shapes=scratch,
        ),
        out_shape=out_shape,
        compiler_params=pltpu.CompilerParams(vmem_limit_bytes=LIMIT),
    )


def swap(array, k, n):
    return lax.ppermute(array, "ep", [(i, i ^ k) for i in range(n)])


def fast_local(
    token_acts, out_grad, counts, params, first_moment, second_moment, old_expert, replica_of, new_expert
):
    groups = lax.axis_size("edp")
    n = lax.axis_size("ep")
    model_width, columns = out_grad.shape[2:]
    slots, tok, hidden = token_acts.shape[2:]
    rows = model_width // groups
    piece = rows // n
    me = lax.axis_index("ep").astype(jnp.int32).reshape(1)
    params, first, second = params[0], first_moment[0], second_moment[0]
    whole = lambda *shape: pl.BlockSpec(shape, lambda i, *_: (0,) * len(shape))

    by_k = lambda i, me: (me[0] ^ (i + 1), 0)
    packed = call(
        pack_kernel,
        1,
        (n - 1,),
        [pl.BlockSpec((piece, hidden), by_k)] * 3,
        [whole(3, piece, hidden)] * (n - 1),
        [jax.ShapeDtypeStruct((3, piece, hidden), BF)] * (n - 1),
    )(me, params, first, second)
    state = [swap(packed[k - 1], k, n) for k in range(1, n)]

    acts = call(
        mask_kernel,
        1,
        (1,),
        [whole(slots, tok, hidden)],
        whole(slots, tok, hidden),
        jax.ShapeDtypeStruct((slots, tok, hidden), BF),
    )(counts[0, 0], token_acts[0, 0])
    all_acts = lax.all_gather(acts, "edp", axis=0)
    all_grads = lax.all_to_all(
        out_grad[0, 0].reshape(groups, rows, columns), "edp", split_axis=0, concat_axis=0, tiled=True
    )
    grads = call(
        grad_kernel,
        1,
        (n,),
        [
            pl.BlockSpec((groups, piece, columns), lambda i, me: (0, me[0] ^ i, 0)),
            whole(groups, slots, tok, hidden),
        ],
        [whole(slots, piece, hidden)] * n,
        [jax.ShapeDtypeStruct((slots, piece, hidden), BF)] * n,
        [pltpu.VMEM((groups * slots * tok, slots * hidden), BF)],
    )(me, all_grads, all_acts)
    grads = [grads[0]] + [swap(grads[k], k, n) for k in range(1, n)]

    chunks = piece // CHUNK
    mine = pl.BlockSpec((CHUNK, hidden), lambda i, me, *_: (me[0] * chunks + i, 0))
    part = lambda count: pl.BlockSpec((count, CHUNK, hidden), lambda i, *_: (0, i, 0))
    placed = call(
        functools.partial(update_kernel, n),
        4,
        (chunks,),
        [mine] * 3 + [part(3)] * (n - 1) + [part(slots)] * n,
        [part(3)] * n,
        [jax.ShapeDtypeStruct((3, piece, hidden), BF)] * n,
        [
            pltpu.VMEM((n, CHUNK, hidden), F32),
            pltpu.VMEM((n, 3, CHUNK, hidden), BF),
            pltpu.SMEM((n,), jnp.int32),
            pltpu.SMEM((n,), jnp.int32),
        ],
    )(me, old_expert, replica_of, new_expert, params, first, second, *state, *grads)

    final = [placed[0]] + [swap(placed[k], k, n) for k in range(1, n)]
    out = pl.BlockSpec((piece, hidden), lambda i, me: (me[0] ^ i, 0))
    step, first, second = call(
        unpack_kernel,
        1,
        (n,),
        [whole(3, piece, hidden)] * n,
        [out] * 3,
        [jax.ShapeDtypeStruct((rows, hidden), d) for d in (F32, BF, BF)],
    )(me, *final)
    return step[None], first[None], second[None]


def plain_local(
    token_acts, out_grad, counts, params, first_moment, second_moment, old_expert, replica_of, new_expert
):
    groups = lax.axis_size("edp")
    owners = lax.axis_size("ep")
    model_width = out_grad.shape[2]
    slots, tok, hidden = token_acts.shape[2:]
    rows = model_width // groups
    piece = rows * hidden // owners
    exchange = functools.partial(lax.all_to_all, axis_name="ep", split_axis=0, concat_axis=0, tiled=True)
    row = jnp.arange(tok, dtype=jnp.int32)
    live = row[None, :] < counts[0, 0][:, None]
    acts = jnp.where(live[:, :, None], token_acts[0, 0], jnp.zeros_like(token_acts[0, 0]))
    all_acts = lax.all_gather(acts, "edp", axis=0)
    all_grads = lax.all_to_all(
        out_grad[0, 0].reshape(groups, rows, slots * tok), "edp", split_axis=0, concat_axis=0, tiled=True
    ).reshape(groups, rows, slots, tok)
    slot_grads = jnp.einsum("adst,astf->sdf", all_grads, all_acts, preferred_element_type=F32)
    pieces = lambda array: exchange(array.astype(BF).reshape(owners, piece))
    own, replica = pieces(slot_grads[0]), pieces(slot_grads[1])
    sum_matrix = (replica_of[None, :] == old_expert[:, None]).astype(BF)
    move_matrix = (old_expert[None, :] == new_expert[:, None]).astype(BF)
    total = own.astype(F32) + jnp.dot(sum_matrix, replica, preferred_element_type=F32)
    updated = adam_update(
        pieces(params[0]).astype(F32), pieces(first_moment[0]), pieces(second_moment[0]), total
    )
    result = []
    for array, kind in zip(updated, (F32, BF, BF)):
        placed = jnp.dot(move_matrix, array.astype(BF), preferred_element_type=F32)
        result.append(exchange(placed.astype(BF)).astype(kind).reshape(1, rows, hidden))
    return tuple(result)


def local(token_acts, out_grad, *others):
    groups, n = lax.axis_size("edp"), lax.axis_size("ep")
    rows = out_grad.shape[2] // groups
    fast = n & (n - 1) == 0 and rows % (n * CHUNK) == 0
    return (fast_local if fast else plain_local)(token_acts, out_grad, *others)


def solution(mesh):
    return jax.shard_map(
        local,
        mesh=mesh,
        in_specs=(
            P("edp", "ep", None, None, None),
            P("edp", "ep", None, None),
            P("edp", "ep", None),
            P("ep", "edp", None),
            P("ep", "edp", None),
            P("ep", "edp", None),
            P(),
            P(),
            P(),
        ),
        out_specs=(P("ep", "edp", None), P("ep", "edp", None), P("ep", "edp", None)),
        check_vma=False,
    )
```

profile of v0, /device:TPU:17, one launch (start us, length us, event | category | flops | bytes accessed | tf_op | source)
XLA Modules:
  0.0 219.6 jit_solution(2313018678526846980)
XLA Ops:
  7.2 0.0 all-gather.3.cloned.1.call-start
  7.2 2.3 %shard_map.113 = bf16[2,64,1024]{2,1,0:T(8,128)(2,1)} custom-call(s32[2]{0:T(128)} %bitcast.20, bf16[2,64,1024]{2,1,0:T(8,128)(2,1)} %bitcast.19), custom_call_target="tpu_custom_call" | custom-call | tf_op jit(solution)/shard_map/pallas_call | solution.py:157
  9.5 0.0 all-gather.3.cloned.1.call-update
  9.6 4.7 %all-to-all-start = ((bf16[4,896,128]{2,1,0:T(8,128)(2,1)}), bf16[4,896,128]{2,1,0:T(8,128)(2,1)S(1)}, u32[]{:S(2)}, u32[]{:S(2)}) async-start(bf16[4,896,128]{2,1,0:T(8,128)(2,1)} %bitcast.18), calls=%async_computation | async-start | bytes 1835008 | tf_op jit(solution)/shard_map/all_to_all | solution.py:166
  14.2 7.4 %shard_map.112 = (bf16[3,112,1024]{2,1,0:T(8,128)(2,1)}, bf16[3,112,1024]{2,1,0:T(8,128)(2,1)}, bf16[3,112,1024]{2,1,0:T(8,128)(2,1)}, bf16[3,112,1024]{2,1,0:T(...) custom-call(s32[1]{0:T(128)} %bitcast.me.me_ref, ...), custom_call_target="tpu_custom_call" | custom-call | tf_op jit(solution)/shard_map/pallas_call | solution.py:147
  21.7 1.3 collective-permute-start
  23.0 1.2 collective-permute-start.1
  24.2 0.4 collective-permute-start.2
  24.6 1.2 collective-permute-start.3
  25.8 0.6 collective-permute-start.4
  26.5 2.1 collective-permute-start.5
  28.6 11.7 %collective-permute-done.1.refs_4_ = bf16[3,112,1024]{2,1,0:T(8,128)(2,1)S(1)} collective-permute-done((bf16[3,112,1024]{2,1,0:T(8,128)(2,1)}, bf16[3,112,1024]{2,1,0:T(8,128)(2,1)S(1)}, u32[]{:S(2)}, u32[]{:S(2)}) %collective-permute-start.1) | collective-permute-done | bytes 688160 | tf_op jit(solution)/shard_map/ppermute | solution.py:130
  40.4 3.1 %collective-permute-start.6 = (bf16[3,112,1024]{2,1,0:T(8,128)(2,1)}, bf16[3,112,1024]{2,1,0:T(8,128)(2,1)}, u32[]{:S(2)}, u32[]{:S(2)}) collective-permute-start(bf16[3,112,1024]{2,1,0:T(8,128)(2,1)} %get-tuple-element.35), channel_id=1, source_target_pairs={{0,7},{1,6},{2,5},{3,4},{4,3},{5,2},{6,1},{7,0},{8,15},{9,14},{10,... | collective-permute-start | bytes 2064392 | tf_op jit(solution)/shard_map/ppermute | solution.py:130
  43.4 5.0 %all-to-all-done.grads = bf16[4,896,128]{2,1,0:T(8,128)(2,1)S(1)} async-done(((bf16[4,896,128]{2,1,0:T(8,128)(2,1)}), bf16[4,896,128]{2,1,0:T(8,128)(2,1)S(1)}, u32[]{:S(2)}, u32[]{:S(2)}) %all-to-all-start) | async-done | bytes 917536 | tf_op jit(solution)/shard_map/all_to_all | solution.py:166
  48.5 4.0 %all-gather.3.cloned.1.call-done = bf16[8,64,1024]{2,1,0:T(8,128)(2,1)} async-done(((bf16[2,64,1024]{2,1,0:T(8,128)(2,1)}), bf16[8,64,1024]{2,1,0:T(8,128)(2,1)}) %all-gather.3.cloned.1.call-update) | async-done | bytes 1048592 | tf_op jit(solution)/shard_map/all_gather | solution.py:165
  52.5 8.8 %shard_map.114 = (bf16[2,112,1024]{2,1,0:T(8,128)(2,1)}, bf16[2,112,1024]{2,1,0:T(8,128)(2,1)}, bf16[2,112,1024]{2,1,0:T(8,128)(2,1)}, bf16[2,112,1024]{2,1,0:T(...) custom-call(s32[1]{0:T(128)} %bitcast.me.me_ref, ...), custom_call_target="tpu_custom_call" | custom-call | tf_op jit(solution)/shard_map/pallas_call | solution.py:169
  61.3 0.0 collective-permute-done.2.refs_5_
  61.3 1.1 collective-permute-start.7
  62.4 1.3 collective-permute-start.8
  63.6 22.9 %collective-permute-done.4.refs_7_ = bf16[3,112,1024]{2,1,0:T(8,128)(2,1)} collective-permute-done((bf16[3,112,1024]{2,1,0:T(8,128)(2,1)}, bf16[3,112,1024]{2,1,0:T(8,128)(2,1)}, u32[]{:S(2)}, u32[]{:S(2)}) %collective-permute-start.4) | collective-permute-done | bytes 688160 | tf_op jit(solution)/shard_map/ppermute | solution.py:130
  86.5 0.6 collective-permute-start.9
  87.1 0.0 collective-permute-done.5.refs_8_
  87.1 1.6 collective-permute-start.10
  88.7 1.1 collective-permute-start.11
  89.7 0.0 collective-permute-done.7.refs_11_
  89.7 1.2 collective-permute-start.12
  90.9 3.4 %collective-permute-done.8.refs_12_ = bf16[2,112,1024]{2,1,0:T(8,128)(2,1)S(1)} collective-permute-done((bf16[2,112,1024]{2,1,0:T(8,128)(2,1)}, bf16[2,112,1024]{2,1,0:T(8,128)(2,1)S(1)}, u32[]{:S(2)}, u32[]{:S(2)}) %collective-permute-start.8) | collective-permute-done | bytes 458784 | tf_op jit(solution)/shard_map/ppermute | solution.py:130
  94.4 3.2 %collective-permute-start.13 = (bf16[2,112,1024]{2,1,0:T(8,128)(2,1)}, bf16[2,112,1024]{2,1,0:T(8,128)(2,1)S(1)}, u32[]{:S(2)}, u32[]{:S(2)}) collective-permute-start(bf16[2,112,1024]{2,1,0:T(8,128)(2,1)} %get-tuple-element.43), channel_id=1, source_target_pairs={{0,7},{1,6},{2,5},{3,4},{4,3},{5,2},{6,1},{7,0},{8,15},{9,14},{10,... | collective-permute-start | bytes 1376264 | tf_op jit(solution)/shard_map/ppermute | solution.py:130
  97.6 7.4 %collective-permute-done.9.refs_13_ = bf16[2,112,1024]{2,1,0:T(8,128)(2,1)S(1)} collective-permute-done((bf16[2,112,1024]{2,1,0:T(8,128)(2,1)}, bf16[2,112,1024]{2,1,0:T(8,128)(2,1)S(1)}, u32[]{:S(2)}, u32[]{:S(2)}) %collective-permute-start.9) | collective-permute-done | bytes 458784 | tf_op jit(solution)/shard_map/ppermute | solution.py:130
  105.0 0.0 collective-permute-done.10.refs_14_
  105.0 24.2 %collective-permute-done.11.refs_15_ = bf16[2,112,1024]{2,1,0:T(8,128)(2,1)S(1)} collective-permute-done((bf16[2,112,1024]{2,1,0:T(8,128)(2,1)}, bf16[2,112,1024]{2,1,0:T(8,128)(2,1)S(1)}, u32[]{:S(2)}, u32[]{:S(2)}) %collective-permute-start.11) | collective-permute-done | bytes 458784 | tf_op jit(solution)/shard_map/ppermute | solution.py:130
  129.2 0.7 copy-done.15
  130.0 0.1 copy-done.16
  130.1 0.2 copy-done.17
  130.3 10.4 %shard_map.115 = (bf16[3,112,1024]{2,1,0:T(8,128)(2,1)}, bf16[3,112,1024]{2,1,0:T(8,128)(2,1)}, bf16[3,112,1024]{2,1,0:T(8,128)(2,1)}, bf16[3,112,1024]{2,1,0:T(...) custom-call(s32[1]{0:T(128)} %bitcast.me.me_ref, ...), custom_call_target="tpu_custom_call" | custom-call | tf_op jit(solution)/shard_map/pallas_call | solution.py:186
  140.7 0.1 collective-permute-start.14
  140.8 0.5 collective-permute-start.15
  141.3 1.6 collective-permute-start.16
  142.9 1.5 collective-permute-start.17
  144.4 1.5 collective-permute-start.19
  145.8 11.8 %collective-permute-done.15.refs_2_ = bf16[3,112,1024]{2,1,0:T(8,128)(2,1)S(1)} collective-permute-done((bf16[3,112,1024]{2,1,0:T(8,128)(2,1)}, bf16[3,112,1024]{2,1,0:T(8,128)(2,1)S(1)}, u32[]{:S(2)}, u32[]{:S(2)}) %collective-permute-start.15) | collective-permute-done | bytes 688160 | tf_op jit(solution)/shard_map/ppermute | solution.py:130
  157.6 3.5 %collective-permute-start.20 = (bf16[3,112,1024]{2,1,0:T(8,128)(2,1)}, bf16[3,112,1024]{2,1,0:T(8,128)(2,1)S(1)}, u32[]{:S(2)}, u32[]{:S(2)}) collective-permute-start(bf16[3,112,1024]{2,1,0:T(8,128)(2,1)} %get-tuple-element.51), channel_id=1, source_target_pairs={{0,7},{1,6},{2,5},{3,4},{4,3},{5,2},{6,1},{7,0},{8,15},{9,14},{10,... | collective-permute-start | bytes 2064392 | tf_op jit(solution)/shard_map/ppermute | solution.py:130
  161.1 13.0 %collective-permute-done.16.refs_3_ = bf16[3,112,1024]{2,1,0:T(8,128)(2,1)S(1)} collective-permute-done((bf16[3,112,1024]{2,1,0:T(8,128)(2,1)}, bf16[3,112,1024]{2,1,0:T(8,128)(2,1)S(1)}, u32[]{:S(2)}, u32[]{:S(2)}) %collective-permute-start.16) | collective-permute-done | bytes 688160 | tf_op jit(solution)/shard_map/ppermute | solution.py:130
  174.1 30.4 %collective-permute-done.18.refs_5_ = bf16[3,112,1024]{2,1,0:T(8,128)(2,1)S(1)} collective-permute-done((bf16[3,112,1024]{2,1,0:T(8,128)(2,1)}, bf16[3,112,1024]{2,1,0:T(8,128)(2,1)S(1)}, u32[]{:S(2)}, u32[]{:S(2)}) %collective-permute-start.18) | collective-permute-done | bytes 688160 | tf_op jit(solution)/shard_map/ppermute | solution.py:130
  204.6 0.8 copy-done.8
  205.4 0.2 copy-done.9
  205.6 0.3 copy-done.10
  205.9 6.8 %shard_map.116 = (f32[896,1024]{1,0:T(8,128)}, bf16[896,1024]{1,0:T(8,128)(2,1)}, bf16[896,1024]{1,0:T(8,128)(2,1)}) custom-call(s32[1]{0:T(128)} %bitcast.me.me_ref, bf16[3,112,1024]{2,1,0:T(8,128)(2,1)} %get-tuple-element.44.refs_0_, bf16[3,112,1024]{2,1,0:T(8,128)(2,1)} %copy-done.4, bf16[3,112,1024]{2,1,0:T(8,128)(2,1)} %copy-done.5, ...), custom_call_target="tpu_custom_call" | custom-call | tf_op jit(solution)/shard_map/pallas_call | solution.py:203
  (40 shorter events, 0.1 us)
Async XLA Ops:
  7.2 45.3 %all-gather.3.cloned.1.call-start = ((), (), s32[]{:S(2)}) async-start(), calls=%async_computation.1 | async-start | bytes 1310720 | tf_op jit(solution)/shard_map/all_gather | solution.py:165
  9.6 38.9 %all-to-all-start = ((bf16[4,896,128]{2,1,0:T(8,128)(2,1)}), bf16[4,896,128]{2,1,0:T(8,128)(2,1)S(1)}, u32[]{:S(2)}, u32[]{:S(2)}) async-start(bf16[4,896,128]{2,1,0:T(8,128)(2,1)} %bitcast.18), calls=%async_computation | async-start | bytes 1835008 | tf_op jit(solution)/shard_map/all_to_all | solution.py:166
  21.7 4.8 %collective-permute-start = (bf16[3,112,1024]{2,1,0:T(8,128)(2,1)}, bf16[3,112,1024]{2,1,0:T(8,128)(2,1)S(1)}, u32[]{:S(2)}, u32[]{:S(2)}) collective-permute-start(bf16[3,112,1024]{2,1,0:T(8,128)(2,1)} %get-tuple-element.29), channel_id=1, source_target_pairs={{0,1},{1,0},{2,3},{3,2},{4,5},{5,4},{6,7},{7,6},{8,9},{9,8},{10,11... | collective-permute-start | bytes 2064392 | tf_op jit(solution)/shard_map/ppermute | solution.py:130
  23.0 17.4 %collective-permute-start.1 = (bf16[3,112,1024]{2,1,0:T(8,128)(2,1)}, bf16[3,112,1024]{2,1,0:T(8,128)(2,1)S(1)}, u32[]{:S(2)}, u32[]{:S(2)}) collective-permute-start(bf16[3,112,1024]{2,1,0:T(8,128)(2,1)} %get-tuple-element.30), channel_id=1, source_target_pairs={{0,2},{1,3},{2,0},{3,1},{4,6},{5,7},{6,4},{7,5},{8,10},{9,11},{10,... | collective-permute-start | bytes 2064392 | tf_op jit(solution)/shard_map/ppermute | solution.py:130
  24.2 37.1 %collective-permute-start.2 = (bf16[3,112,1024]{2,1,0:T(8,128)(2,1)}, bf16[3,112,1024]{2,1,0:T(8,128)(2,1)S(1)}, u32[]{:S(2)}, u32[]{:S(2)}) collective-permute-start(bf16[3,112,1024]{2,1,0:T(8,128)(2,1)} %get-tuple-element.31), channel_id=1, source_target_pairs={{0,3},{1,2},{2,1},{3,0},{4,7},{5,6},{6,5},{7,4},{8,11},{9,10},{10,... | collective-permute-start | bytes 2064392 | tf_op jit(solution)/shard_map/ppermute | solution.py:130
  24.6 37.8 %collective-permute-start.3 = (bf16[3,112,1024]{2,1,0:T(8,128)(2,1)}, bf16[3,112,1024]{2,1,0:T(8,128)(2,1)}, u32[]{:S(2)}, u32[]{:S(2)}) collective-permute-start(bf16[3,112,1024]{2,1,0:T(8,128)(2,1)} %get-tuple-element.32), channel_id=1, source_target_pairs={{0,4},{1,5},{2,6},{3,7},{4,0},{5,1},{6,2},{7,3},{8,12},{9,13},{10,... | collective-permute-start | bytes 2064392 | tf_op jit(solution)/shard_map/ppermute | solution.py:130
  25.8 60.7 %collective-permute-start.4 = (bf16[3,112,1024]{2,1,0:T(8,128)(2,1)}, bf16[3,112,1024]{2,1,0:T(8,128)(2,1)}, u32[]{:S(2)}, u32[]{:S(2)}) collective-permute-start(bf16[3,112,1024]{2,1,0:T(8,128)(2,1)} %get-tuple-element.33), channel_id=1, source_target_pairs={{0,5},{1,4},{2,7},{3,6},{4,1},{5,0},{6,3},{7,2},{8,13},{9,12},{10,... | collective-permute-start | bytes 2064392 | tf_op jit(solution)/shard_map/ppermute | solution.py:130
  26.5 102.7 %copy-start.1 = (bf16[3,112,1024]{2,1,0:T(8,128)(2,1)}, bf16[3,112,1024]{2,1,0:T(8,128)(2,1)S(1)}, u32[]{:S(2)}) copy-start(bf16[3,112,1024]{2,1,0:T(8,128)(2,1)S(1)} %collective-permute-done.refs_3_) | copy-start | bytes 2064388
  26.5 60.6 %collective-permute-start.5 = (bf16[3,112,1024]{2,1,0:T(8,128)(2,1)}, bf16[3,112,1024]{2,1,0:T(8,128)(2,1)}, u32[]{:S(2)}, u32[]{:S(2)}) collective-permute-start(bf16[3,112,1024]{2,1,0:T(8,128)(2,1)} %get-tuple-element.34), channel_id=1, source_target_pairs={{0,6},{1,7},{2,4},{3,5},{4,2},{5,3},{6,0},{7,1},{8,14},{9,15},{10,... | collective-permute-start | bytes 2064392 | tf_op jit(solution)/shard_map/ppermute | solution.py:130
  40.3 88.8 %copy-start.2 = (bf16[3,112,1024]{2,1,0:T(8,128)(2,1)}, bf16[3,112,1024]{2,1,0:T(8,128)(2,1)S(1)}, u32[]{:S(2)}) copy-start(bf16[3,112,1024]{2,1,0:T(8,128)(2,1)S(1)} %collective-permute-done.1.refs_4_) | copy-start | bytes 2064388
  40.4 48.3 %collective-permute-start.6 = (bf16[3,112,1024]{2,1,0:T(8,128)(2,1)}, bf16[3,112,1024]{2,1,0:T(8,128)(2,1)}, u32[]{:S(2)}, u32[]{:S(2)}) collective-permute-start(bf16[3,112,1024]{2,1,0:T(8,128)(2,1)} %get-tuple-element.35), channel_id=1, source_target_pairs={{0,7},{1,6},{2,5},{3,4},{4,3},{5,2},{6,1},{7,0},{8,15},{9,14},{10,... | collective-permute-start | bytes 2064392 | tf_op jit(solution)/shard_map/ppermute | solution.py:130
  48.5 4.0 %copy-start = (bf16[4,896,128]{2,1,0:T(8,128)(2,1)}, bf16[4,896,128]{2,1,0:T(8,128)(2,1)S(1)}, u32[]{:S(2)}) copy-start(bf16[4,896,128]{2,1,0:T(8,128)(2,1)S(1)} %all-to-all-done.grads) | copy-start | bytes 2752516
  61.3 67.9 %copy-start.3 = (bf16[3,112,1024]{2,1,0:T(8,128)(2,1)}, bf16[3,112,1024]{2,1,0:T(8,128)(2,1)S(1)}, u32[]{:S(2)}) copy-start(bf16[3,112,1024]{2,1,0:T(8,128)(2,1)S(1)} %collective-permute-done.2.refs_5_) | copy-start | bytes 2064388
  61.3 28.4 %collective-permute-start.7 = (bf16[2,112,1024]{2,1,0:T(8,128)(2,1)}, bf16[2,112,1024]{2,1,0:T(8,128)(2,1)S(1)}, u32[]{:S(2)}, u32[]{:S(2)}) collective-permute-start(bf16[2,112,1024]{2,1,0:T(8,128)(2,1)} %get-tuple-element.37), channel_id=1, source_target_pairs={{0,1},{1,0},{2,3},{3,2},{4,5},{5,4},{6,7},{7,6},{8,9},{9,8},{10,11... | collective-permute-start | bytes 1376264 | tf_op jit(solution)/shard_map/ppermute | solution.py:130
  62.4 32.0 %collective-permute-start.8 = (bf16[2,112,1024]{2,1,0:T(8,128)(2,1)}, bf16[2,112,1024]{2,1,0:T(8,128)(2,1)S(1)}, u32[]{:S(2)}, u32[]{:S(2)}) collective-permute-start(bf16[2,112,1024]{2,1,0:T(8,128)(2,1)} %get-tuple-element.38), channel_id=1, source_target_pairs={{0,2},{1,3},{2,0},{3,1},{4,6},{5,7},{6,4},{7,5},{8,10},{9,11},{10,... | collective-permute-start | bytes 1376264 | tf_op jit(solution)/shard_map/ppermute | solution.py:130
  86.5 18.5 %collective-permute-start.9 = (bf16[2,112,1024]{2,1,0:T(8,128)(2,1)}, bf16[2,112,1024]{2,1,0:T(8,128)(2,1)S(1)}, u32[]{:S(2)}, u32[]{:S(2)}) collective-permute-start(bf16[2,112,1024]{2,1,0:T(8,128)(2,1)} %get-tuple-element.39), channel_id=1, source_target_pairs={{0,3},{1,2},{2,1},{3,0},{4,7},{5,6},{6,5},{7,4},{8,11},{9,10},{10,... | collective-permute-start | bytes 1376264 | tf_op jit(solution)/shard_map/ppermute | solution.py:130
  87.1 17.9 %collective-permute-start.10 = (bf16[2,112,1024]{2,1,0:T(8,128)(2,1)}, bf16[2,112,1024]{2,1,0:T(8,128)(2,1)S(1)}, u32[]{:S(2)}, u32[]{:S(2)}) collective-permute-start(bf16[2,112,1024]{2,1,0:T(8,128)(2,1)} %get-tuple-element.40), channel_id=1, source_target_pairs={{0,4},{1,5},{2,6},{3,7},{4,0},{5,1},{6,2},{7,3},{8,12},{9,13},{10,... | collective-permute-start | bytes 1376264 | tf_op jit(solution)/shard_map/ppermute | solution.py:130
  88.7 40.5 %collective-permute-start.11 = (bf16[2,112,1024]{2,1,0:T(8,128)(2,1)}, bf16[2,112,1024]{2,1,0:T(8,128)(2,1)S(1)}, u32[]{:S(2)}, u32[]{:S(2)}) collective-permute-start(bf16[2,112,1024]{2,1,0:T(8,128)(2,1)} %get-tuple-element.41), channel_id=1, source_target_pairs={{0,5},{1,4},{2,7},{3,6},{4,1},{5,0},{6,3},{7,2},{8,13},{9,12},{10,... | collective-permute-start | bytes 1376264 | tf_op jit(solution)/shard_map/ppermute | solution.py:130
  89.7 39.5 %copy-start.11 = (bf16[2,112,1024]{2,1,0:T(8,128)(2,1)}, bf16[2,112,1024]{2,1,0:T(8,128)(2,1)S(1)}, u32[]{:S(2)}) copy-start(bf16[2,112,1024]{2,1,0:T(8,128)(2,1)S(1)} %collective-permute-done.7.refs_11_) | copy-start | bytes 1376260
  89.7 39.4 %collective-permute-start.12 = (bf16[2,112,1024]{2,1,0:T(8,128)(2,1)}, bf16[2,112,1024]{2,1,0:T(8,128)(2,1)S(1)}, u32[]{:S(2)}, u32[]{:S(2)}) collective-permute-start(bf16[2,112,1024]{2,1,0:T(8,128)(2,1)} %get-tuple-element.42), channel_id=1, source_target_pairs={{0,6},{1,7},{2,4},{3,5},{4,2},{5,3},{6,0},{7,1},{8,14},{9,15},{10,... | collective-permute-start | bytes 1376264 | tf_op jit(solution)/shard_map/ppermute | solution.py:130
  94.4 34.9 %copy-start.12 = (bf16[2,112,1024]{2,1,0:T(8,128)(2,1)}, bf16[2,112,1024]{2,1,0:T(8,128)(2,1)S(1)}, u32[]{:S(2)}) copy-start(bf16[2,112,1024]{2,1,0:T(8,128)(2,1)S(1)} %collective-permute-done.8.refs_12_) | copy-start | bytes 1376260
  94.4 34.8 %collective-permute-start.13 = (bf16[2,112,1024]{2,1,0:T(8,128)(2,1)}, bf16[2,112,1024]{2,1,0:T(8,128)(2,1)S(1)}, u32[]{:S(2)}, u32[]{:S(2)}) collective-permute-start(bf16[2,112,1024]{2,1,0:T(8,128)(2,1)} %get-tuple-element.43), channel_id=1, source_target_pairs={{0,7},{1,6},{2,5},{3,4},{4,3},{5,2},{6,1},{7,0},{8,15},{9,14},{10,... | collective-permute-start | bytes 1376264 | tf_op jit(solution)/shard_map/ppermute | solution.py:130
  105.0 24.3 %copy-start.13 = (bf16[2,112,1024]{2,1,0:T(8,128)(2,1)}, bf16[2,112,1024]{2,1,0:T(8,128)(2,1)S(1)}, u32[]{:S(2)}) copy-start(bf16[2,112,1024]{2,1,0:T(8,128)(2,1)S(1)} %collective-permute-done.9.refs_13_) | copy-start | bytes 1376260
  105.0 24.3 %copy-start.14 = (bf16[2,112,1024]{2,1,0:T(8,128)(2,1)}, bf16[2,112,1024]{2,1,0:T(8,128)(2,1)S(1)}, u32[]{:S(2)}) copy-start(bf16[2,112,1024]{2,1,0:T(8,128)(2,1)S(1)} %collective-permute-done.10.refs_14_) | copy-start | bytes 1376260
  129.2 0.8 copy-start.15
  129.2 0.9 copy-start.16
  129.2 1.1 copy-start.17
  140.7 3.7 %collective-permute-start.14 = (bf16[3,112,1024]{2,1,0:T(8,128)(2,1)}, bf16[3,112,1024]{2,1,0:T(8,128)(2,1)S(1)}, u32[]{:S(2)}, u32[]{:S(2)}) collective-permute-start(bf16[3,112,1024]{2,1,0:T(8,128)(2,1)} %get-tuple-element.45), channel_id=1, source_target_pairs={{0,1},{1,0},{2,3},{3,2},{4,5},{5,4},{6,7},{7,6},{8,9},{9,8},{10,11... | collective-permute-start | bytes 2064392 | tf_op jit(solution)/shard_map/ppermute | solution.py:130
  140.8 16.8 %collective-permute-start.15 = (bf16[3,112,1024]{2,1,0:T(8,128)(2,1)}, bf16[3,112,1024]{2,1,0:T(8,128)(2,1)S(1)}, u32[]{:S(2)}, u32[]{:S(2)}) collective-permute-start(bf16[3,112,1024]{2,1,0:T(8,128)(2,1)} %get-tuple-element.46), channel_id=1, source_target_pairs={{0,2},{1,3},{2,0},{3,1},{4,6},{5,7},{6,4},{7,5},{8,10},{9,11},{10,... | collective-permute-start | bytes 2064392 | tf_op jit(solution)/shard_map/ppermute | solution.py:130
  141.3 32.8 %collective-permute-start.16 = (bf16[3,112,1024]{2,1,0:T(8,128)(2,1)}, bf16[3,112,1024]{2,1,0:T(8,128)(2,1)S(1)}, u32[]{:S(2)}, u32[]{:S(2)}) collective-permute-start(bf16[3,112,1024]{2,1,0:T(8,128)(2,1)} %get-tuple-element.47), channel_id=1, source_target_pairs={{0,3},{1,2},{2,1},{3,0},{4,7},{5,6},{6,5},{7,4},{8,11},{9,10},{10,... | collective-permute-start | bytes 2064392 | tf_op jit(solution)/shard_map/ppermute | solution.py:130
  142.9 31.2 %collective-permute-start.17 = (bf16[3,112,1024]{2,1,0:T(8,128)(2,1)}, bf16[3,112,1024]{2,1,0:T(8,128)(2,1)S(1)}, u32[]{:S(2)}, u32[]{:S(2)}) collective-permute-start(bf16[3,112,1024]{2,1,0:T(8,128)(2,1)} %get-tuple-element.48), channel_id=1, source_target_pairs={{0,4},{1,5},{2,6},{3,7},{4,0},{5,1},{6,2},{7,3},{8,12},{9,13},{10,... | collective-permute-start | bytes 2064392 | tf_op jit(solution)/shard_map/ppermute | solution.py:130
  144.4 60.2 %collective-permute-start.18 = (bf16[3,112,1024]{2,1,0:T(8,128)(2,1)}, bf16[3,112,1024]{2,1,0:T(8,128)(2,1)S(1)}, u32[]{:S(2)}, u32[]{:S(2)}) collective-permute-start(bf16[3,112,1024]{2,1,0:T(8,128)(2,1)} %get-tuple-element.49), channel_id=1, source_target_pairs={{0,5},{1,4},{2,7},{3,6},{4,1},{5,0},{6,3},{7,2},{8,13},{9,12},{10,... | collective-permute-start | bytes 2064392 | tf_op jit(solution)/shard_map/ppermute | solution.py:130
  144.4 60.2 %copy-start.4 = (bf16[3,112,1024]{2,1,0:T(8,128)(2,1)}, bf16[3,112,1024]{2,1,0:T(8,128)(2,1)S(1)}, u32[]{:S(2)}) copy-start(bf16[3,112,1024]{2,1,0:T(8,128)(2,1)S(1)} %collective-permute-done.14.refs_1_) | copy-start | bytes 2064388
  144.4 60.2 %collective-permute-start.19 = (bf16[3,112,1024]{2,1,0:T(8,128)(2,1)}, bf16[3,112,1024]{2,1,0:T(8,128)(2,1)S(1)}, u32[]{:S(2)}, u32[]{:S(2)}) collective-permute-start(bf16[3,112,1024]{2,1,0:T(8,128)(2,1)} %get-tuple-element.50), channel_id=1, source_target_pairs={{0,6},{1,7},{2,4},{3,5},{4,2},{5,3},{6,0},{7,1},{8,14},{9,15},{10,... | collective-permute-start | bytes 2064392 | tf_op jit(solution)/shard_map/ppermute | solution.py:130
  157.6 47.0 %copy-start.5 = (bf16[3,112,1024]{2,1,0:T(8,128)(2,1)}, bf16[3,112,1024]{2,1,0:T(8,128)(2,1)S(1)}, u32[]{:S(2)}) copy-start(bf16[3,112,1024]{2,1,0:T(8,128)(2,1)S(1)} %collective-permute-done.15.refs_2_) | copy-start | bytes 2064388
  157.6 46.9 %collective-permute-start.20 = (bf16[3,112,1024]{2,1,0:T(8,128)(2,1)}, bf16[3,112,1024]{2,1,0:T(8,128)(2,1)S(1)}, u32[]{:S(2)}, u32[]{:S(2)}) collective-permute-start(bf16[3,112,1024]{2,1,0:T(8,128)(2,1)} %get-tuple-element.51), channel_id=1, source_target_pairs={{0,7},{1,6},{2,5},{3,4},{4,3},{5,2},{6,1},{7,0},{8,15},{9,14},{10,... | collective-permute-start | bytes 2064392 | tf_op jit(solution)/shard_map/ppermute | solution.py:130
  174.1 30.5 %copy-start.6 = (bf16[3,112,1024]{2,1,0:T(8,128)(2,1)}, bf16[3,112,1024]{2,1,0:T(8,128)(2,1)S(1)}, u32[]{:S(2)}) copy-start(bf16[3,112,1024]{2,1,0:T(8,128)(2,1)S(1)} %collective-permute-done.16.refs_3_) | copy-start | bytes 2064388
  174.1 30.5 %copy-start.7 = (bf16[3,112,1024]{2,1,0:T(8,128)(2,1)}, bf16[3,112,1024]{2,1,0:T(8,128)(2,1)S(1)}, u32[]{:S(2)}) copy-start(bf16[3,112,1024]{2,1,0:T(8,128)(2,1)S(1)} %collective-permute-done.17.refs_4_) | copy-start | bytes 2064388
  204.5 0.9 copy-start.8
  204.5 1.1 copy-start.9
  204.5 1.3 copy-start.10
Sparse Core Ops, SparseCore 0:
  9.7 42.7 all-gather.2
where the time goes:
time: 221 us; the launch traced here: 220 us
  waiting for transfers between devices  134 us (61%)
  Pallas kernels  35.8 us (16%)
  starting transfers between devices  33.3 us (15%)
  between operations  14.2 us (6%)
  local copies, waits for them, and re-layouts  2.38 us (1%)
    ppermute x21, waiting for transfers between devices, swap(): return lax.ppermute(array, 'ep', [(i, i ^ k) for i in range(n)])  125 us
    ppermute x21, starting transfers between devices, swap(): return lax.ppermute(array, 'ep', [(i, i ^ k) for i in range(n)])  28.6 us
    pallas_call x1, Pallas kernels, fast_local(): call(functools.partial(update_kernel, n), 4, (chunks,), [mine] * 3 + [par...  10.4 us
    pallas_call x1, Pallas kernels, fast_local(): call(grad_kernel, 1, (n,), [pl.BlockSpec((groups, piece, columns), lambda...  8.83 us
    pallas_call x1, Pallas kernels, fast_local(): call(pack_kernel, 1, (n - 1,), [pl.BlockSpec((piece, hidden), by_k)] * 3,...  7.45 us
    pallas_call x1, Pallas kernels, fast_local(): call(unpack_kernel, 1, (n,), [whole(3, piece, hidden)] * n, [out] * 3, [j...  6.82 us
    all_to_all x1, waiting for transfers between devices, fast_local(): lax.all_to_all(out_grad[0, 0].reshape(groups, rows, columns), 'edp', spli...  5.02 us
    all_to_all x1, starting transfers between devices, fast_local(): lax.all_to_all(out_grad[0, 0].reshape(groups, rows, columns), 'edp', spli...  4.66 us
  transfers between devices with their start and end apart: 23, of which 10 were waited for; matrix products, arithmetic and copies ran while one was open for 0% of the time, Pallas kernels for 7%

commit v1 on v0

--- a/solution.py
+++ b/solution.py
@@ -17,6 +17,7 @@
 BF = jnp.bfloat16
 F32 = jnp.float32
 CHUNK = 16
+PARTS = 2
 LIMIT = 56 * 1024 * 1024
 
 
@@ -28,11 +29,21 @@
     return step_new, first_new, second_new
 
 
-def mask_kernel(counts, acts, out):
-    slots, tok, _ = acts.shape
+def spread_kernel(me, counts, grads, acts, *outs):
+    at = pl.program_id(0)
+    slots, tok, hidden = acts.shape
+    rows, columns = grads.shape
     row = lax.broadcasted_iota(jnp.int32, (tok, 1), 0)
-    for s in range(slots):
-        out[s] = jnp.where(row < counts[s], acts[s], jnp.zeros_like(acts[s]))
+    for j, out in enumerate(outs):
+
+        @pl.when(at == j)
+        def _(out=out):
+            out[:rows] = grads[...]
+            for s in range(slots):
+                live = jnp.where(row < counts[s], acts[s], jnp.zeros_like(acts[s]))
+                for b in range(hidden // columns):
+                    to = rows + b * columns + s * tok
+                    out[to : to + tok] = live[:, b * columns : (b + 1) * columns]
 
 
 def pack_kernel(me, params, first, second, *outs):
@@ -46,28 +57,39 @@
             out[2] = second[...]
 
 
-def grad_kernel(me, grads, acts, *refs):
-    outs, table = refs[:-1], refs[-1]
+def grad_kernel(rows, slots, tok, hidden, me, *refs):
     at = pl.program_id(0)
-    groups, slots, tok, hidden = acts.shape
+    groups = lax.axis_size("edp")
+    given, outs, table = refs[:groups], refs[groups:-1], refs[-1]
+    n = lax.axis_size("ep")
+    parts = len(outs) // n
+    columns = given[0].shape[1]
+    piece = outs[0].shape[1]
+    width = hidden // parts
 
     @pl.when(at == 0)
     def _():
-        zero = jnp.zeros((tok, hidden), BF)
+        table[...] = jnp.zeros_like(table)
         for g in range(groups):
-            for t in range(slots):
+            for s in range(slots):
+                for b in range(hidden // columns):
+                    source = rows + b * columns + s * tok
+                    table[
+                        g * columns + s * tok : g * columns + (s + 1) * tok,
+                        s * hidden + b * columns : s * hidden + (b + 1) * columns,
+                    ] = given[g][source : source + tok]
+
+    here = pl.ds(pl.multiple_of((me[0] ^ at) * piece, CHUNK), piece)
+    left = jnp.concatenate([given[g][here] for g in range(groups)], axis=1)
+    total = jnp.dot(left, table[...], preferred_element_type=F32).astype(BF)
+    for j in range(n):
+
+        @pl.when(at == j)
+        def _(j=j):
+            for p in range(parts):
                 for s in range(slots):
-                    rows = pl.ds((g * slots + t) * tok, tok)
-                    table[rows, pl.ds(s * hidden, hidden)] = acts[g, s] if s == t else zero
-
-    left = jnp.concatenate([grads[g] for g in range(groups)], axis=1)
-    total = jnp.dot(left, table[...], preferred_element_type=F32).astype(BF)
-    for j, out in enumerate(outs):
-
-        @pl.when(at == j)
-        def _(out=out):
-            for s in range(slots):
-                out[s] = total[:, s * hidden : (s + 1) * hidden]
+                    start = s * hidden + p * width
+                    outs[p * n + j][s] = total[:, start : start + width]
 
 
 def update_kernel(n, me_ref, old, rep, new, *refs):
@@ -99,8 +121,8 @@
         outs[k][...] = placed[k]
 
 
-def unpack_kernel(me, *refs):
-    pieces, (step, first, second) = refs[:-3], refs[-3:]
+def unpack_kernel(n, me, *refs):
+    pieces, (step, first, second) = refs[:n], refs[-3:]
     at = pl.program_id(0)
     for j, piece in enumerate(pieces):
 
@@ -111,7 +133,7 @@
             second[...] = piece[2]
 
 
-def call(kernel, prefetch, grid, in_specs, out_specs, out_shape, scratch=()):
+def call(kernel, prefetch, grid, in_specs, out_specs, out_shape, scratch=(), aliases={}):
     return pl.pallas_call(
         kernel,
         grid_spec=pltpu.PrefetchScalarGridSpec(
@@ -122,12 +144,13 @@
             scratch_shapes=scratch,
         ),
         out_shape=out_shape,
+        input_output_aliases=aliases,
         compiler_params=pltpu.CompilerParams(vmem_limit_bytes=LIMIT),
     )
 
 
-def swap(array, k, n):
-    return lax.ppermute(array, "ep", [(i, i ^ k) for i in range(n)])
+def swap(array, k, axis):
+    return lax.ppermute(array, axis, [(i, i ^ k) for i in range(lax.axis_size(axis))])
 
 
 def fast_local(
@@ -139,75 +162,92 @@
     slots, tok, hidden = token_acts.shape[2:]
     rows = model_width // groups
     piece = rows // n
+    width = hidden // PARTS
     me = lax.axis_index("ep").astype(jnp.int32).reshape(1)
+    group = lax.axis_index("edp").astype(jnp.int32).reshape(1)
     params, first, second = params[0], first_moment[0], second_moment[0]
     whole = lambda *shape: pl.BlockSpec(shape, lambda i, *_: (0,) * len(shape))
-
-    by_k = lambda i, me: (me[0] ^ (i + 1), 0)
-    packed = call(
-        pack_kernel,
-        1,
-        (n - 1,),
-        [pl.BlockSpec((piece, hidden), by_k)] * 3,
-        [whole(3, piece, hidden)] * (n - 1),
-        [jax.ShapeDtypeStruct((3, piece, hidden), BF)] * (n - 1),
-    )(me, params, first, second)
-    state = [swap(packed[k - 1], k, n) for k in range(1, n)]
-
-    acts = call(
-        mask_kernel,
-        1,
-        (1,),
-        [whole(slots, tok, hidden)],
-        whole(slots, tok, hidden),
-        jax.ShapeDtypeStruct((slots, tok, hidden), BF),
-    )(counts[0, 0], token_acts[0, 0])
-    all_acts = lax.all_gather(acts, "edp", axis=0)
-    all_grads = lax.all_to_all(
-        out_grad[0, 0].reshape(groups, rows, columns), "edp", split_axis=0, concat_axis=0, tiled=True
-    )
-    grads = call(
-        grad_kernel,
+    others = range(1, n)
+
+    packed = {}
+    for ks in ([k for k in reversed(others) if k % 2 == 0], [k for k in reversed(others) if k % 2]):
+
+        def by_k(i, me, ks=ks):
+            k = ks[-1]
+            for j in range(len(ks) - 1):
+                k = jnp.where(i == j, ks[j], k)
+            return (me[0] ^ k, 0)
+
+        made = call(
+            pack_kernel,
+            1,
+            (len(ks),),
+            [pl.BlockSpec((piece, hidden), by_k)] * 3,
+            [whole(3, piece, hidden)] * len(ks),
+            [jax.ShapeDtypeStruct((3, piece, hidden), BF)] * len(ks),
+        )(me, params, first, second)
+        packed.update(zip(ks, made))
+    state = {k: swap(array, k, "ep") for k, array in packed.items()}
+
+    tall = rows + slots * tok * (hidden // columns)
+    spread = call(
+        spread_kernel,
+        2,
+        (groups,),
+        [pl.BlockSpec((rows, columns), lambda i, me, *_: (me[0] ^ i, 0)), whole(slots, tok, hidden)],
+        [whole(tall, columns)] * groups,
+        [jax.ShapeDtypeStruct((tall, columns), BF)] * groups,
+    )(group, counts[0, 0], out_grad[0, 0], token_acts[0, 0])
+    spread = [spread[0]] + [swap(spread[k], k, "edp") for k in range(1, groups)]
+    made = call(
+        functools.partial(grad_kernel, rows, slots, tok, hidden),
         1,
         (n,),
-        [
-            pl.BlockSpec((groups, piece, columns), lambda i, me: (0, me[0] ^ i, 0)),
-            whole(groups, slots, tok, hidden),
-        ],
-        [whole(slots, piece, hidden)] * n,
-        [jax.ShapeDtypeStruct((slots, piece, hidden), BF)] * n,
-        [pltpu.VMEM((groups * slots * tok, slots * hidden), BF)],
-    )(me, all_grads, all_acts)
-    grads = [grads[0]] + [swap(grads[k], k, n) for k in range(1, n)]
-
+        [whole(tall, columns)] * groups,
+        [whole(slots, piece, width)] * (n * PARTS),
+        [jax.ShapeDtypeStruct((slots, piece, width), BF)] * (n * PARTS),
+        [pltpu.VMEM((groups * columns, slots * hidden), BF)],
+    )(me, *spread)
+    grads = [
+        [made[p * n]] + [swap(made[p * n + k], k, "ep") for k in others] for p in range(PARTS)
+    ]
+
+    result = [None] * 3
     chunks = piece // CHUNK
-    mine = pl.BlockSpec((CHUNK, hidden), lambda i, me, *_: (me[0] * chunks + i, 0))
-    part = lambda count: pl.BlockSpec((count, CHUNK, hidden), lambda i, *_: (0, i, 0))
-    placed = call(
-        functools.partial(update_kernel, n),
-        4,
-        (chunks,),
-        [mine] * 3 + [part(3)] * (n - 1) + [part(slots)] * n,
-        [part(3)] * n,
-        [jax.ShapeDtypeStruct((3, piece, hidden), BF)] * n,
-        [
-            pltpu.VMEM((n, CHUNK, hidden), F32),
-            pltpu.VMEM((n, 3, CHUNK, hidden), BF),
-            pltpu.SMEM((n,), jnp.int32),
-            pltpu.SMEM((n,), jnp.int32),
-        ],
-    )(me, old_expert, replica_of, new_expert, params, first, second, *state, *grads)
-
-    final = [placed[0]] + [swap(placed[k], k, n) for k in range(1, n)]
-    out = pl.BlockSpec((piece, hidden), lambda i, me: (me[0] ^ i, 0))
-    step, first, second = call(
-        unpack_kernel,
-        1,
-        (n,),
-        [whole(3, piece, hidden)] * n,
-        [out] * 3,
-        [jax.ShapeDtypeStruct((rows, hidden), d) for d in (F32, BF, BF)],
-    )(me, *final)
+    for p in range(PARTS):
+        mine = pl.BlockSpec((CHUNK, width), lambda i, me, *_: (me[0] * chunks + i, p))
+        part = lambda count, at: pl.BlockSpec((count, CHUNK, width), lambda i, *_: (0, i, at))
+        placed = call(
+            functools.partial(update_kernel, n),
+            4,
+            (chunks,),
+            [mine] * 3 + [part(3, p)] * (n - 1) + [part(slots, 0)] * n,
+            [part(3, 0)] * n,
+            [jax.ShapeDtypeStruct((3, piece, width), BF)] * n,
+            [
+                pltpu.VMEM((n, CHUNK, width), F32),
+                pltpu.VMEM((n, 3, CHUNK, width), BF),
+                pltpu.SMEM((n,), jnp.int32),
+                pltpu.SMEM((n,), jnp.int32),
+            ],
+        )(
+            me, old_expert, replica_of, new_expert, params, first, second,
+            *[state[k] for k in others], *grads[p],
+        )
+
+        final = [placed[0]] + [swap(placed[k], k, "ep") for k in others]
+        out = pl.BlockSpec((piece, width), lambda i, me: (me[0] ^ i, p))
+        earlier = [] if p == 0 else result
+        result = call(
+            functools.partial(unpack_kernel, n),
+            1,
+            (n,),
+            [whole(3, piece, width)] * n + [pl.BlockSpec(memory_space=pl.ANY)] * len(earlier),
+            [out] * 3,
+            [jax.ShapeDtypeStruct((rows, hidden), d) for d in (F32, BF, BF)],
+            aliases={1 + n + j: j for j in range(len(earlier))},
+        )(me, *final, *earlier)
+    step, first, second = result
     return step[None], first[None], second[None]
 
 
@@ -246,8 +286,9 @@
 
 def local(token_acts, out_grad, *others):
     groups, n = lax.axis_size("edp"), lax.axis_size("ep")
-    rows = out_grad.shape[2] // groups
-    fast = n & (n - 1) == 0 and rows % (n * CHUNK) == 0
+    rows, columns = out_grad.shape[2] // groups, out_grad.shape[3]
+    fast = groups & (groups - 1) == 0 and n & (n - 1) == 0 and rows % (n * CHUNK) == 0
+    fast = fast and columns == 128 and token_acts.shape[4] % (128 * PARTS) == 0
     return (fast_local if fast else plain_local)(token_acts, out_grad, *others)
 
 

time: 221 us -> 205 us (0.928)
  waiting for transfers between devices: 134 us -> 91.8 us
  starting transfers between devices: 33.3 us -> 63.6 us
  between operations: 14.2 us -> 1 us
  Pallas kernels: 35.8 us -> 46.4 us
    ppermute x21 -> x38, starting transfers between devices: 28.6 us -> 63.6 us  [swap(): lax.ppermute(array, axis, [(i, i ^ k) for i in range(lax.axis_size(axis))])]
    ppermute x21 -> x38, waiting for transfers between devices: 125 us -> 91.8 us  [swap(): lax.ppermute(array, axis, [(i, i ^ k) for i in range(lax.axis_size(axis))])]
    pallas_call x4 -> x6, Pallas kernels: 25.4 us -> 31.1 us  [the longest x2 10.3 us: fast_local(): call(functools.partial(unpack_kernel, n), 1, (n,), [whole(3, piece, width...]
    all_to_all x1 -> x0, waiting for transfers between devices: 5.02 us -> none  [fast_local(): lax.all_to_all(out_grad[0, 0].reshape(groups, rows, columns), 'edp', spli...]
    pallas_call x1 -> x2, Pallas kernels: 10.4 us -> 15.3 us  [fast_local(): call(functools.partial(update_kernel, n), 4, (chunks,), [mine] * 3 + [par...]
    all_to_all x1 -> x0, starting transfers between devices: 4.66 us -> none  [fast_local(): lax.all_to_all(out_grad[0, 0].reshape(groups, rows, columns), 'edp', spli...]
    all_gather x1 -> x0, waiting for transfers between devices: 4 us -> none  [fast_local(): all_acts = lax.all_gather(acts, 'edp', axis=0)]
  transfers between devices with their start and end apart: 23 -> 38, of which waited for: 10 -> 18; matrix products, arithmetic and copies ran while one was open for 0% -> 0% of each run, Pallas kernels for 7% -> 18%
where the time goes in v1:
time: 205 us; the launch traced here: 204 us
  waiting for transfers between devices  91.8 us (45%)
  starting transfers between devices  63.6 us (31%)
  Pallas kernels  46.4 us (23%)
    ppermute x38, waiting for transfers between devices, swap(): lax.ppermute(array, axis, [(i, i ^ k) for i in range(lax.axis_size(axis))])  91.8 us
    ppermute x38, starting transfers between devices, swap(): lax.ppermute(array, axis, [(i, i ^ k) for i in range(lax.axis_size(axis))])  63.6 us
    pallas_call x2, Pallas kernels, fast_local(): call(functools.partial(update_kernel, n), 4, (chunks,), [mine] * 3 + [par...  15.3 us
    pallas_call x2, Pallas kernels, fast_local(): call(functools.partial(unpack_kernel, n), 1, (n,), [whole(3, piece, width...  10.3 us
    pallas_call x1, Pallas kernels, fast_local(): call(functools.partial(grad_kernel, rows, slots, tok, hidden), 1, (n,), [...  8.35 us
    pallas_call x2, Pallas kernels, fast_local(): call(pack_kernel, 1, (len(ks),), [pl.BlockSpec((piece, hidden), by_k)] *...  8.25 us
    pallas_call x1, Pallas kernels, fast_local(): call(spread_kernel, 2, (groups,), [pl.BlockSpec((rows, columns), lambda i...  4.24 us
  transfers between devices with their start and end apart: 38, of which 18 were waited for; matrix products, arithmetic and copies ran while one was open for 0% of the time, Pallas kernels for 18%

profile of v1, /device:TPU:17, one launch (start us, length us, event | category | flops | bytes accessed | tf_op | source)
XLA Modules:
  0.0 203.7 jit_solution(7554847661658736162)
XLA Ops:
  0.6 4.2 %shard_map.114 = (bf16[1920,128]{1,0:T(8,128)(2,1)}, bf16[1920,128]{1,0:T(8,128)(2,1)}, bf16[1920,128]{1,0:T(8,128)(2,1)}, bf16[1920,128]{1,0:T(8,128)(2,1)}) custom-call(s32[1]{0:T(128)} %bitcast.4.me, s32[2]{0:T(128)} %bitcast.28, bf16[3584,128]{1,0:T(8,128)(2,1)} %bitcast.26, bf16[2,64,1024]{2,1,0:T(8,128)(2,1)} %bitcast.27), custom_call_target="tpu_custom_call" | custom-call | tf_op jit(solution)/shard_map/pallas_call | solution.py:193
  4.9 1.3 collective-permute-start.7
  6.2 3.9 %shard_map.113 = (bf16[3,112,1024]{2,1,0:T(8,128)(2,1)}, bf16[3,112,1024]{2,1,0:T(8,128)(2,1)}, bf16[3,112,1024]{2,1,0:T(8,128)(2,1)}) custom-call(s32[1]{0:T(128)} %bitcast.me.me_ref, f32[896,1024]{1,0:T(8,128)} %bitcast.11, bf16[896,1024]{1,0:T(8,128)(2,1)} %bitcast.15, bf16[896,1024]{1,0:T(8,128)(2,1)} %bitcast.19), custom_call_target="tpu_custom_call" | custom-call | tf_op jit(solution)/shard_map/pallas_call | solution.py:181
  10.1 1.2 collective-permute-start.1
  11.3 1.2 collective-permute-start.3
  12.6 1.3 collective-permute-start.9
  13.9 4.4 %shard_map.112 = (bf16[3,112,1024]{2,1,0:T(8,128)(2,1)}, bf16[3,112,1024]{2,1,0:T(8,128)(2,1)}, bf16[3,112,1024]{2,1,0:T(8,128)(2,1)}, bf16[3,112,1024]{2,1,0:T(8,128)(2,1)}) custom-call(s32[1]{0:T(128)} %bitcast.me.me_ref, f32[896,1024]{1,0:T(8,128)} %bitcast.12, bf16[896,1024]{1,0:T(8,128)(2,1)} %bitcast.16, bf16[896,1024]{1,0:T(8,128)(2,1)} %bitcast.20), custom_call_target="tpu_custom_call" | custom-call | tf_op jit(solution)/shard_map/pallas_call | solution.py:181
  18.2 7.4 %collective-permute-done.7.refs_1_ = bf16[1920,128]{1,0:T(8,128)(2,1)S(1)} collective-permute-done((bf16[1920,128]{1,0:T(8,128)(2,1)}, bf16[1920,128]{1,0:T(8,128)(2,1)S(1)}, u32[]{:S(2)}, u32[]{:S(2)}) %collective-permute-start.7) | collective-permute-done | bytes 491552 | tf_op jit(solution)/shard_map/ppermute | solution.py:153
  25.6 2.2 %collective-permute-start.5 = (bf16[3,112,1024]{2,1,0:T(8,128)(2,1)S(1)}, bf16[3,112,1024]{2,1,0:T(8,128)(2,1)S(1)}, u32[]{:S(2)}, u32[]{:S(2)}) collective-permute-start(bf16[3,112,1024]{2,1,0:T(8,128)(2,1)S(1)} %copy-done.38), channel_id=1, source_target_pairs={{0,6},{1,7},{2,4},{3,5},{4,2},{5,3},{6,0},{7,1},{8,14},{9,15},{10,... | collective-permute-start | bytes 2064392 | tf_op jit(solution)/shard_map/ppermute | solution.py:153
  27.8 12.7 %collective-permute-start = (bf16[3,112,1024]{2,1,0:T(8,128)(2,1)}, bf16[3,112,1024]{2,1,0:T(8,128)(2,1)S(1)}, u32[]{:S(2)}, u32[]{:S(2)}) collective-permute-start(bf16[3,112,1024]{2,1,0:T(8,128)(2,1)} %get-tuple-element.52), channel_id=1, source_target_pairs={{0,1},{1,0},{2,3},{3,2},{4,5},{5,4},{6,7},{7,6},{8,9},{9,8},{10,11... | collective-permute-start | bytes 2064392 | tf_op jit(solution)/shard_map/ppermute | solution.py:153
  40.5 9.2 %collective-permute-done.9.refs_3_ = bf16[1920,128]{1,0:T(8,128)(2,1)S(1)} collective-permute-done((bf16[1920,128]{1,0:T(8,128)(2,1)S(1)}, bf16[1920,128]{1,0:T(8,128)(2,1)S(1)}, u32[]{:S(2)}, u32[]{:S(2)}) %collective-permute-start.9) | collective-permute-done | bytes 491552 | tf_op jit(solution)/shard_map/ppermute | solution.py:153
  49.7 2.9 %collective-permute-start.2 = (bf16[3,112,1024]{2,1,0:T(8,128)(2,1)}, bf16[3,112,1024]{2,1,0:T(8,128)(2,1)S(1)}, u32[]{:S(2)}, u32[]{:S(2)}) collective-permute-start(bf16[3,112,1024]{2,1,0:T(8,128)(2,1)} %get-tuple-element.54), channel_id=1, source_target_pairs={{0,3},{1,2},{2,1},{3,0},{4,7},{5,6},{6,5},{7,4},{8,11},{9,10},{10,... | collective-permute-start | bytes 2064392 | tf_op jit(solution)/shard_map/ppermute | solution.py:153
  52.8 1.6 collective-permute-start.6
  54.4 8.4 %shard_map.115 = (bf16[2,112,512]{2,1,0:T(8,128)(2,1)}, bf16[2,112,512]{2,1,0:T(8,128)(2,1)}, bf16[2,112,512]{2,1,0:T(8,128)(2,1)}, bf16[2,112,512]{2,1,0:T(8,12...) custom-call(s32[1]{0:T(128)} %bitcast.me.me_ref, ...), custom_call_target="tpu_custom_call" | custom-call | tf_op jit(solution)/shard_map/pallas_call | solution.py:202
  63.3 5.8 %collective-permute-done.2.refs_5_ = bf16[3,112,1024]{2,1,0:T(8,128)(2,1)S(1)} collective-permute-done((bf16[3,112,1024]{2,1,0:T(8,128)(2,1)}, bf16[3,112,1024]{2,1,0:T(8,128)(2,1)S(1)}, u32[]{:S(2)}, u32[]{:S(2)}) %collective-permute-start.2) | collective-permute-done | bytes 688160 | tf_op jit(solution)/shard_map/ppermute | solution.py:153
  69.1 1.0 collective-permute-done.4.refs_7_
  70.1 14.4 %collective-permute-start.26 = (bf16[2,112,512]{2,1,0:T(8,128)(2,1)}, bf16[2,112,512]{2,1,0:T(8,128)(2,1)S(1)}, u32[]{:S(2)}, u32[]{:S(2)}) collective-permute-start(bf16[2,112,512]{2,1,0:T(8,128)(2,1)} %get-tuple-element.82), channel_id=1, source_target_pairs={{0,3},{1,2},{2,1},{3,0},{4,7},{5,6},{6,5},{7,4},{8,11},{9,10},{10,... | collective-permute-start | bytes 688136 | tf_op jit(solution)/shard_map/ppermute | solution.py:153
  84.8 0.6 collective-permute-start.27
  85.4 1.5 collective-permute-start.28
  86.8 1.6 collective-permute-start.29
  88.8 0.9 collective-permute-start.30
  89.7 4.1 %collective-permute-done.26.refs_13_ = bf16[2,112,512]{2,1,0:T(8,128)(2,1)S(1)} collective-permute-done((bf16[2,112,512]{2,1,0:T(8,128)(2,1)}, bf16[2,112,512]{2,1,0:T(8,128)(2,1)S(1)}, u32[]{:S(2)}, u32[]{:S(2)}) %collective-permute-start.26) | collective-permute-done | bytes 229408 | tf_op jit(solution)/shard_map/ppermute | solution.py:153
  93.8 1.9 collective-permute-start.12
  95.7 11.6 %collective-permute-done.28.refs_15_ = bf16[2,112,512]{2,1,0:T(8,128)(2,1)S(1)} collective-permute-done((bf16[2,112,512]{2,1,0:T(8,128)(2,1)}, bf16[2,112,512]{2,1,0:T(8,128)(2,1)S(1)}, u32[]{:S(2)}, u32[]{:S(2)}) %collective-permute-start.28) | collective-permute-done | bytes 229408 | tf_op jit(solution)/shard_map/ppermute | solution.py:153
  108.5 1.3 collective-permute-start.15
  109.9 7.7 %shard_map.117 = (bf16[3,112,512]{2,1,0:T(8,128)(2,1)}, bf16[3,112,512]{2,1,0:T(8,128)(2,1)}, bf16[3,112,512]{2,1,0:T(8,128)(2,1)}, bf16[3,112,512]{2,1,0:T(8,12...) custom-call(s32[1]{0:T(128)} %bitcast.me.me_ref, ...), custom_call_target="tpu_custom_call" | custom-call | tf_op jit(solution)/shard_map/pallas_call | solution.py:220
  117.6 1.2 collective-permute-start.31
  119.2 0.9 collective-permute-done.13.refs_14_
  120.0 0.8 collective-permute-start.33
  120.8 4.1 %collective-permute-done.14.refs_15_ = bf16[2,112,512]{2,1,0:T(8,128)(2,1)S(1)} collective-permute-done((bf16[2,112,512]{2,1,0:T(8,128)(2,1)}, bf16[2,112,512]{2,1,0:T(8,128)(2,1)S(1)}, u32[]{:S(2)}, u32[]{:S(2)}) %collective-permute-start.14) | collective-permute-done | bytes 229408 | tf_op jit(solution)/shard_map/ppermute | solution.py:153
  125.0 1.9 collective-permute-start.16
  126.8 14.1 %collective-permute-done.16.refs_17_ = bf16[2,112,512]{2,1,0:T(8,128)(2,1)S(1)} collective-permute-done((bf16[2,112,512]{2,1,0:T(8,128)(2,1)S(1)}, bf16[2,112,512]{2,1,0:T(8,128)(2,1)S(1)}, u32[]{:S(2)}, u32[]{:S(2)}) %collective-permute-start.16) | collective-permute-done | bytes 229408 | tf_op jit(solution)/shard_map/ppermute | solution.py:153
  140.9 1.5 collective-permute-start.35
  142.5 7.7 %shard_map.116 = (bf16[3,112,512]{2,1,0:T(8,128)(2,1)}, bf16[3,112,512]{2,1,0:T(8,128)(2,1)}, bf16[3,112,512]{2,1,0:T(8,128)(2,1)}, bf16[3,112,512]{2,1,0:T(8,12...) custom-call(s32[1]{0:T(128)} %bitcast.me.me_ref, ...), custom_call_target="tpu_custom_call" | custom-call | tf_op jit(solution)/shard_map/pallas_call | solution.py:220
  150.2 1.0 collective-permute-start.36
  151.2 1.9 collective-permute-start.37
  153.6 1.7 collective-permute-start.19
  155.3 5.2 %collective-permute-done.36.refs_6_ = bf16[3,112,512]{2,1,0:T(8,128)(2,1)S(1)} collective-permute-done((bf16[3,112,512]{2,1,0:T(8,128)(2,1)S(1)}, bf16[3,112,512]{2,1,0:T(8,128)(2,1)S(1)}, u32[]{:S(2)}, u32[]{:S(2)}) %collective-permute-start.36) | collective-permute-done | bytes 344096 | tf_op jit(solution)/shard_map/ppermute | solution.py:153
  161.0 8.0 %collective-permute-done.37.refs_7_ = bf16[3,112,512]{2,1,0:T(8,128)(2,1)S(1)} collective-permute-done((bf16[3,112,512]{2,1,0:T(8,128)(2,1)S(1)}, bf16[3,112,512]{2,1,0:T(8,128)(2,1)S(1)}, u32[]{:S(2)}, u32[]{:S(2)}) %collective-permute-start.37) | collective-permute-done | bytes 344096 | tf_op jit(solution)/shard_map/ppermute | solution.py:153
  169.1 1.0 collective-permute-start.22
  170.1 4.6 %collective-permute-done.18.refs_2_ = bf16[3,112,512]{2,1,0:T(8,128)(2,1)S(1)} collective-permute-done((bf16[3,112,512]{2,1,0:T(8,128)(2,1)}, bf16[3,112,512]{2,1,0:T(8,128)(2,1)S(1)}, u32[]{:S(2)}, u32[]{:S(2)}) %collective-permute-start.18) | collective-permute-done | bytes 344096 | tf_op jit(solution)/shard_map/ppermute | solution.py:153
  174.6 2.7 %collective-permute-start.23 = (bf16[3,112,512]{2,1,0:T(8,128)(2,1)}, bf16[3,112,512]{2,1,0:T(8,128)(2,1)S(1)}, u32[]{:S(2)}, u32[]{:S(2)}) collective-permute-start(bf16[3,112,512]{2,1,0:T(8,128)(2,1)} %get-tuple-element.78), channel_id=1, source_target_pairs={{0,7},{1,6},{2,5},{3,4},{4,3},{5,2},{6,1},{7,0},{8,15},{9,14},{10,... | collective-permute-start | bytes 1032200 | tf_op jit(solution)/shard_map/ppermute | solution.py:153
  177.4 5.2 %shard_map.118 = (f32[896,1024]{1,0:T(8,128)}, bf16[896,1024]{1,0:T(8,128)(2,1)}, bf16[896,1024]{1,0:T(8,128)(2,1)}) custom-call(s32[1]{0:T(128)} %bitcast.me.me_ref, bf16[3,112,512]{2,1,0:T(8,128)(2,1)} %get-tuple-element.87.refs_0_, bf16[3,112,512]{2,1,0:T(8,128)(2,1)} %copy-done.17, bf16[3,112,512]{2,1,0:T(8,128)(2,1)} %copy-done.18, ...), custom_call_target="tpu_custom_call" | custom-call | tf_op jit(solution)/shard_map/pallas_call | solution.py:241
  182.6 0.7 collective-permute-done.19.refs_3_
  183.8 6.2 %collective-permute-done.22.refs_6_ = bf16[3,112,512]{2,1,0:T(8,128)(2,1)S(1)} collective-permute-done((bf16[3,112,512]{2,1,0:T(8,128)(2,1)}, bf16[3,112,512]{2,1,0:T(8,128)(2,1)S(1)}, u32[]{:S(2)}, u32[]{:S(2)}) %collective-permute-start.22) | collective-permute-done | bytes 344096 | tf_op jit(solution)/shard_map/ppermute | solution.py:153
  190.0 7.8 %collective-permute-done.23.refs_7_ = bf16[3,112,512]{2,1,0:T(8,128)(2,1)S(1)} collective-permute-done((bf16[3,112,512]{2,1,0:T(8,128)(2,1)}, bf16[3,112,512]{2,1,0:T(8,128)(2,1)S(1)}, u32[]{:S(2)}, u32[]{:S(2)}) %collective-permute-start.23) | collective-permute-done | bytes 344096 | tf_op jit(solution)/shard_map/ppermute | solution.py:153
  197.9 0.7 copy-done.16
  198.6 5.1 %shard_map.119 = (f32[896,1024]{1,0:T(8,128)}, bf16[896,1024]{1,0:T(8,128)(2,1)}, bf16[896,1024]{1,0:T(8,128)(2,1)}) custom-call(s32[1]{0:T(128)} %bitcast.me.me_ref, bf16[3,112,512]{2,1,0:T(8,128)(2,1)} %get-tuple-element.71.refs_0_, bf16[3,112,512]{2,1,0:T(8,128)(2,1)} %copy-done.10, ...), custom_call_target="tpu_custom_call", output_to_operand_aliasing={{0}: (9, {}), {1}: (10, {}), {2}: (11, {})} | custom-call | tf_op jit(solution)/shard_map/pallas_call | solution.py:241
  (122 shorter events, 4.6 us)
Async XLA Ops:
  4.9 20.7 %collective-permute-start.7 = (bf16[1920,128]{1,0:T(8,128)(2,1)}, bf16[1920,128]{1,0:T(8,128)(2,1)S(1)}, u32[]{:S(2)}, u32[]{:S(2)}) collective-permute-start(bf16[1920,128]{1,0:T(8,128)(2,1)} %get-tuple-element.60), channel_id=1, source_target_pairs={{0,8},{8,0},{16,24},{24,16},{1,9},{9,1},{17,25},{25,17},{2,10},{10... | collective-permute-start | bytes 1474568 | tf_op jit(solution)/shard_map/ppermute | solution.py:153
  6.2 21.6 %collective-permute-start.8 = (bf16[1920,128]{1,0:T(8,128)(2,1)}, bf16[1920,128]{1,0:T(8,128)(2,1)S(1)}, u32[]{:S(2)}, u32[]{:S(2)}) collective-permute-start(bf16[1920,128]{1,0:T(8,128)(2,1)} %get-tuple-element.61), channel_id=1, source_target_pairs={{0,16},{8,24},{16,0},{24,8},{1,17},{9,25},{17,1},{25,9},{2,18},{10... | collective-permute-start | bytes 1474568 | tf_op jit(solution)/shard_map/ppermute | solution.py:153
  10.1 42.5 %collective-permute-start.1 = (bf16[3,112,1024]{2,1,0:T(8,128)(2,1)}, bf16[3,112,1024]{2,1,0:T(8,128)(2,1)S(1)}, u32[]{:S(2)}, u32[]{:S(2)}) collective-permute-start(bf16[3,112,1024]{2,1,0:T(8,128)(2,1)} %get-tuple-element.53), channel_id=1, source_target_pairs={{0,2},{1,3},{2,0},{3,1},{4,6},{5,7},{6,4},{7,5},{8,10},{9,11},{10,... | collective-permute-start | bytes 2064392 | tf_op jit(solution)/shard_map/ppermute | solution.py:153
  11.3 41.4 %collective-permute-start.3 = (bf16[3,112,1024]{2,1,0:T(8,128)(2,1)}, bf16[3,112,1024]{2,1,0:T(8,128)(2,1)S(1)}, u32[]{:S(2)}, u32[]{:S(2)}) collective-permute-start(bf16[3,112,1024]{2,1,0:T(8,128)(2,1)} %get-tuple-element.55), channel_id=1, source_target_pairs={{0,4},{1,5},{2,6},{3,7},{4,0},{5,1},{6,2},{7,3},{8,12},{9,13},{10,... | collective-permute-start | bytes 2064392 | tf_op jit(solution)/shard_map/ppermute | solution.py:153
  12.6 37.2 %collective-permute-start.9 = (bf16[1920,128]{1,0:T(8,128)(2,1)S(1)}, bf16[1920,128]{1,0:T(8,128)(2,1)S(1)}, u32[]{:S(2)}, u32[]{:S(2)}) collective-permute-start(bf16[1920,128]{1,0:T(8,128)(2,1)S(1)} %copy-done.39), channel_id=1, source_target_pairs={{0,24},{8,16},{16,8},{24,0},{1,25},{9,17},{17,9},{25,1},{2,26},{10... | collective-permute-start | bytes 1474568 | tf_op jit(solution)/shard_map/ppermute | solution.py:153
  25.6 28.8 %copy-start.7 = (bf16[1920,128]{1,0:T(8,128)(2,1)}, bf16[1920,128]{1,0:T(8,128)(2,1)S(1)}, u32[]{:S(2)}) copy-start(bf16[1920,128]{1,0:T(8,128)(2,1)S(1)} %collective-permute-done.7.refs_1_) | copy-start | bytes 1474564
  25.6 37.1 %collective-permute-start.5 = (bf16[3,112,1024]{2,1,0:T(8,128)(2,1)S(1)}, bf16[3,112,1024]{2,1,0:T(8,128)(2,1)S(1)}, u32[]{:S(2)}, u32[]{:S(2)}) collective-permute-start(bf16[3,112,1024]{2,1,0:T(8,128)(2,1)S(1)} %copy-done.38), channel_id=1, source_target_pairs={{0,6},{1,7},{2,4},{3,5},{4,2},{5,3},{6,0},{7,1},{8,14},{9,15},{10,... | collective-permute-start | bytes 2064392 | tf_op jit(solution)/shard_map/ppermute | solution.py:153
  27.8 35.2 %collective-permute-start = (bf16[3,112,1024]{2,1,0:T(8,128)(2,1)}, bf16[3,112,1024]{2,1,0:T(8,128)(2,1)S(1)}, u32[]{:S(2)}, u32[]{:S(2)}) collective-permute-start(bf16[3,112,1024]{2,1,0:T(8,128)(2,1)} %get-tuple-element.52), channel_id=1, source_target_pairs={{0,1},{1,0},{2,3},{3,2},{4,5},{5,4},{6,7},{7,6},{8,9},{9,8},{10,11... | collective-permute-start | bytes 2064392 | tf_op jit(solution)/shard_map/ppermute | solution.py:153
  49.7 19.4 %collective-permute-start.2 = (bf16[3,112,1024]{2,1,0:T(8,128)(2,1)}, bf16[3,112,1024]{2,1,0:T(8,128)(2,1)S(1)}, u32[]{:S(2)}, u32[]{:S(2)}) collective-permute-start(bf16[3,112,1024]{2,1,0:T(8,128)(2,1)} %get-tuple-element.54), channel_id=1, source_target_pairs={{0,3},{1,2},{2,1},{3,0},{4,7},{5,6},{6,5},{7,4},{8,11},{9,10},{10,... | collective-permute-start | bytes 2064392 | tf_op jit(solution)/shard_map/ppermute | solution.py:153
  52.6 57.1 %copy-start = (bf16[3,112,1024]{2,1,0:T(8,128)(2,1)}, bf16[3,112,1024]{2,1,0:T(8,128)(2,1)S(1)}, u32[]{:S(2)}) copy-start(bf16[3,112,1024]{2,1,0:T(8,128)(2,1)S(1)} %collective-permute-done.1.refs_4_) | copy-start | bytes 2064388
  52.6 17.5 %collective-permute-start.4 = (bf16[3,112,1024]{2,1,0:T(8,128)(2,1)}, bf16[3,112,1024]{2,1,0:T(8,128)(2,1)S(1)}, u32[]{:S(2)}, u32[]{:S(2)}) collective-permute-start(bf16[3,112,1024]{2,1,0:T(8,128)(2,1)} %get-tuple-element.56), channel_id=1, source_target_pairs={{0,5},{1,4},{2,7},{3,6},{4,1},{5,0},{6,3},{7,2},{8,13},{9,12},{10,... | collective-permute-start | bytes 2064392 | tf_op jit(solution)/shard_map/ppermute | solution.py:153
  52.8 57.0 %copy-start.1 = (bf16[3,112,1024]{2,1,0:T(8,128)(2,1)}, bf16[3,112,1024]{2,1,0:T(8,128)(2,1)S(1)}, u32[]{:S(2)}) copy-start(bf16[3,112,1024]{2,1,0:T(8,128)(2,1)S(1)} %collective-permute-done.3.refs_6_) | copy-start | bytes 2064388
  52.8 32.0 %collective-permute-start.6 = (bf16[3,112,1024]{2,1,0:T(8,128)(2,1)}, bf16[3,112,1024]{2,1,0:T(8,128)(2,1)S(1)}, u32[]{:S(2)}, u32[]{:S(2)}) collective-permute-start(bf16[3,112,1024]{2,1,0:T(8,128)(2,1)} %get-tuple-element.58), channel_id=1, source_target_pairs={{0,7},{1,6},{2,5},{3,4},{4,3},{5,2},{6,1},{7,0},{8,15},{9,14},{10,... | collective-permute-start | bytes 2064392 | tf_op jit(solution)/shard_map/ppermute | solution.py:153
  62.7 47.0 %copy-start.2 = (bf16[3,112,1024]{2,1,0:T(8,128)(2,1)}, bf16[3,112,1024]{2,1,0:T(8,128)(2,1)S(1)}, u32[]{:S(2)}) copy-start(bf16[3,112,1024]{2,1,0:T(8,128)(2,1)S(1)} %collective-permute-done.5.refs_8_) | copy-start | bytes 2064388
  62.8 22.6 %collective-permute-start.10 = (bf16[2,112,512]{2,1,0:T(8,128)(2,1)}, bf16[2,112,512]{2,1,0:T(8,128)(2,1)S(1)}, u32[]{:S(2)}, u32[]{:S(2)}) collective-permute-start(bf16[2,112,512]{2,1,0:T(8,128)(2,1)} %get-tuple-element.64), channel_id=1, source_target_pairs={{0,1},{1,0},{2,3},{3,2},{4,5},{5,4},{6,7},{7,6},{8,9},{9,8},{10,11... | collective-permute-start | bytes 688136 | tf_op jit(solution)/shard_map/ppermute | solution.py:153
  63.0 46.8 %copy-start.3 = (bf16[3,112,1024]{2,1,0:T(8,128)(2,1)}, bf16[3,112,1024]{2,1,0:T(8,128)(2,1)S(1)}, u32[]{:S(2)}) copy-start(bf16[3,112,1024]{2,1,0:T(8,128)(2,1)S(1)} %collective-permute-done.refs_3_) | copy-start | bytes 2064388
  63.0 23.9 %collective-permute-start.24 = (bf16[2,112,512]{2,1,0:T(8,128)(2,1)}, bf16[2,112,512]{2,1,0:T(8,128)(2,1)S(1)}, u32[]{:S(2)}, u32[]{:S(2)}) collective-permute-start(bf16[2,112,512]{2,1,0:T(8,128)(2,1)} %get-tuple-element.80), channel_id=1, source_target_pairs={{0,1},{1,0},{2,3},{3,2},{4,5},{5,4},{6,7},{7,6},{8,9},{9,8},{10,11... | collective-permute-start | bytes 688136 | tf_op jit(solution)/shard_map/ppermute | solution.py:153
  69.1 40.7 %copy-start.4 = (bf16[3,112,1024]{2,1,0:T(8,128)(2,1)}, bf16[3,112,1024]{2,1,0:T(8,128)(2,1)S(1)}, u32[]{:S(2)}) copy-start(bf16[3,112,1024]{2,1,0:T(8,128)(2,1)S(1)} %collective-permute-done.2.refs_5_) | copy-start | bytes 2064388
  69.1 19.6 %collective-permute-start.25 = (bf16[2,112,512]{2,1,0:T(8,128)(2,1)}, bf16[2,112,512]{2,1,0:T(8,128)(2,1)S(1)}, u32[]{:S(2)}, u32[]{:S(2)}) collective-permute-start(bf16[2,112,512]{2,1,0:T(8,128)(2,1)} %get-tuple-element.81), channel_id=1, source_target_pairs={{0,2},{1,3},{2,0},{3,1},{4,6},{5,7},{6,4},{7,5},{8,10},{9,11},{10,... | collective-permute-start | bytes 688136 | tf_op jit(solution)/shard_map/ppermute | solution.py:153
  70.1 39.7 %copy-start.5 = (bf16[3,112,1024]{2,1,0:T(8,128)(2,1)}, bf16[3,112,1024]{2,1,0:T(8,128)(2,1)S(1)}, u32[]{:S(2)}) copy-start(bf16[3,112,1024]{2,1,0:T(8,128)(2,1)S(1)} %collective-permute-done.4.refs_7_) | copy-start | bytes 2064388
  70.1 23.6 %collective-permute-start.26 = (bf16[2,112,512]{2,1,0:T(8,128)(2,1)}, bf16[2,112,512]{2,1,0:T(8,128)(2,1)S(1)}, u32[]{:S(2)}, u32[]{:S(2)}) collective-permute-start(bf16[2,112,512]{2,1,0:T(8,128)(2,1)} %get-tuple-element.82), channel_id=1, source_target_pairs={{0,3},{1,2},{2,1},{3,0},{4,7},{5,6},{6,5},{7,4},{8,11},{9,10},{10,... | collective-permute-start | bytes 688136 | tf_op jit(solution)/shard_map/ppermute | solution.py:153
  84.8 9.0 %collective-permute-start.27 = (bf16[2,112,512]{2,1,0:T(8,128)(2,1)}, bf16[2,112,512]{2,1,0:T(8,128)(2,1)S(1)}, u32[]{:S(2)}, u32[]{:S(2)}) collective-permute-start(bf16[2,112,512]{2,1,0:T(8,128)(2,1)} %get-tuple-element.83), channel_id=1, source_target_pairs={{0,4},{1,5},{2,6},{3,7},{4,0},{5,1},{6,2},{7,3},{8,12},{9,13},{10,... | collective-permute-start | bytes 688136 | tf_op jit(solution)/shard_map/ppermute | solution.py:153
  85.4 32.2 %copy-start.24 = (bf16[2,112,512]{2,1,0:T(8,128)(2,1)}, bf16[2,112,512]{2,1,0:T(8,128)(2,1)S(1)}, u32[]{:S(2)}) copy-start(bf16[2,112,512]{2,1,0:T(8,128)(2,1)S(1)} %collective-permute-done.10.refs_11_) | copy-start | bytes 688132
  85.4 22.0 %collective-permute-start.28 = (bf16[2,112,512]{2,1,0:T(8,128)(2,1)}, bf16[2,112,512]{2,1,0:T(8,128)(2,1)S(1)}, u32[]{:S(2)}, u32[]{:S(2)}) collective-permute-start(bf16[2,112,512]{2,1,0:T(8,128)(2,1)} %get-tuple-element.84), channel_id=1, source_target_pairs={{0,5},{1,4},{2,7},{3,6},{4,1},{5,0},{6,3},{7,2},{8,13},{9,12},{10,... | collective-permute-start | bytes 688136 | tf_op jit(solution)/shard_map/ppermute | solution.py:153
  86.8 21.1 %collective-permute-start.29 = (bf16[2,112,512]{2,1,0:T(8,128)(2,1)}, bf16[2,112,512]{2,1,0:T(8,128)(2,1)S(1)}, u32[]{:S(2)}, u32[]{:S(2)}) collective-permute-start(bf16[2,112,512]{2,1,0:T(8,128)(2,1)} %get-tuple-element.85), channel_id=1, source_target_pairs={{0,6},{1,7},{2,4},{3,5},{4,2},{5,3},{6,0},{7,1},{8,14},{9,15},{10,... | collective-permute-start | bytes 688136 | tf_op jit(solution)/shard_map/ppermute | solution.py:153
  88.8 19.7 %collective-permute-start.30 = (bf16[2,112,512]{2,1,0:T(8,128)(2,1)}, bf16[2,112,512]{2,1,0:T(8,128)(2,1)S(1)}, u32[]{:S(2)}, u32[]{:S(2)}) collective-permute-start(bf16[2,112,512]{2,1,0:T(8,128)(2,1)} %get-tuple-element.86), channel_id=1, source_target_pairs={{0,7},{1,6},{2,5},{3,4},{4,3},{5,2},{6,1},{7,0},{8,15},{9,14},{10,... | collective-permute-start | bytes 688136 | tf_op jit(solution)/shard_map/ppermute | solution.py:153
  93.8 23.8 %collective-permute-start.11 = (bf16[2,112,512]{2,1,0:T(8,128)(2,1)}, bf16[2,112,512]{2,1,0:T(8,128)(2,1)S(1)}, u32[]{:S(2)}, u32[]{:S(2)}) collective-permute-start(bf16[2,112,512]{2,1,0:T(8,128)(2,1)} %get-tuple-element.65), channel_id=1, source_target_pairs={{0,2},{1,3},{2,0},{3,1},{4,6},{5,7},{6,4},{7,5},{8,10},{9,11},{10,... | collective-permute-start | bytes 688136 | tf_op jit(solution)/shard_map/ppermute | solution.py:153
  93.8 25.0 %collective-permute-start.12 = (bf16[2,112,512]{2,1,0:T(8,128)(2,1)}, bf16[2,112,512]{2,1,0:T(8,128)(2,1)S(1)}, u32[]{:S(2)}, u32[]{:S(2)}) collective-permute-start(bf16[2,112,512]{2,1,0:T(8,128)(2,1)} %get-tuple-element.66), channel_id=1, source_target_pairs={{0,3},{1,2},{2,1},{3,0},{4,7},{5,6},{6,5},{7,4},{8,11},{9,10},{10,... | collective-permute-start | bytes 688136 | tf_op jit(solution)/shard_map/ppermute | solution.py:153
  107.3 12.7 %collective-permute-start.13 = (bf16[2,112,512]{2,1,0:T(8,128)(2,1)}, bf16[2,112,512]{2,1,0:T(8,128)(2,1)S(1)}, u32[]{:S(2)}, u32[]{:S(2)}) collective-permute-start(bf16[2,112,512]{2,1,0:T(8,128)(2,1)} %get-tuple-element.67), channel_id=1, source_target_pairs={{0,4},{1,5},{2,6},{3,7},{4,0},{5,1},{6,2},{7,3},{8,12},{9,13},{10,... | collective-permute-start | bytes 688136 | tf_op jit(solution)/shard_map/ppermute | solution.py:153
  107.9 17.0 %collective-permute-start.14 = (bf16[2,112,512]{2,1,0:T(8,128)(2,1)}, bf16[2,112,512]{2,1,0:T(8,128)(2,1)S(1)}, u32[]{:S(2)}, u32[]{:S(2)}) collective-permute-start(bf16[2,112,512]{2,1,0:T(8,128)(2,1)} %get-tuple-element.68), channel_id=1, source_target_pairs={{0,5},{1,4},{2,7},{3,6},{4,1},{5,0},{6,3},{7,2},{8,13},{9,12},{10,... | collective-permute-start | bytes 688136 | tf_op jit(solution)/shard_map/ppermute | solution.py:153
  108.5 16.5 %collective-permute-start.15 = (bf16[2,112,512]{2,1,0:T(8,128)(2,1)}, bf16[2,112,512]{2,1,0:T(8,128)(2,1)S(1)}, u32[]{:S(2)}, u32[]{:S(2)}) collective-permute-start(bf16[2,112,512]{2,1,0:T(8,128)(2,1)} %get-tuple-element.69), channel_id=1, source_target_pairs={{0,6},{1,7},{2,4},{3,5},{4,2},{5,3},{6,0},{7,1},{8,14},{9,15},{10,... | collective-permute-start | bytes 688136 | tf_op jit(solution)/shard_map/ppermute | solution.py:153
  117.6 32.5 %collective-permute-start.31 = (bf16[3,112,512]{2,1,0:T(8,128)(2,1)}, bf16[3,112,512]{2,1,0:T(8,128)(2,1)S(1)}, u32[]{:S(2)}, u32[]{:S(2)}) collective-permute-start(bf16[3,112,512]{2,1,0:T(8,128)(2,1)} %get-tuple-element.88), channel_id=1, source_target_pairs={{0,1},{1,0},{2,3},{3,2},{4,5},{5,4},{6,7},{7,6},{8,9},{9,8},{10,11... | collective-permute-start | bytes 1032200 | tf_op jit(solution)/shard_map/ppermute | solution.py:153
  118.8 32.3 %collective-permute-start.32 = (bf16[3,112,512]{2,1,0:T(8,128)(2,1)}, bf16[3,112,512]{2,1,0:T(8,128)(2,1)S(1)}, u32[]{:S(2)}, u32[]{:S(2)}) collective-permute-start(bf16[3,112,512]{2,1,0:T(8,128)(2,1)} %get-tuple-element.89), channel_id=1, source_target_pairs={{0,2},{1,3},{2,0},{3,1},{4,6},{5,7},{6,4},{7,5},{8,10},{9,11},{10,... | collective-permute-start | bytes 1032200 | tf_op jit(solution)/shard_map/ppermute | solution.py:153
  120.0 33.1 %collective-permute-start.33 = (bf16[3,112,512]{2,1,0:T(8,128)(2,1)}, bf16[3,112,512]{2,1,0:T(8,128)(2,1)S(1)}, u32[]{:S(2)}, u32[]{:S(2)}) collective-permute-start(bf16[3,112,512]{2,1,0:T(8,128)(2,1)} %get-tuple-element.90), channel_id=1, source_target_pairs={{0,3},{1,2},{2,1},{3,0},{4,7},{5,6},{6,5},{7,4},{8,11},{9,10},{10,... | collective-permute-start | bytes 1032200 | tf_op jit(solution)/shard_map/ppermute | solution.py:153
  125.0 28.2 %collective-permute-start.34 = (bf16[3,112,512]{2,1,0:T(8,128)(2,1)}, bf16[3,112,512]{2,1,0:T(8,128)(2,1)S(1)}, u32[]{:S(2)}, u32[]{:S(2)}) collective-permute-start(bf16[3,112,512]{2,1,0:T(8,128)(2,1)} %get-tuple-element.91), channel_id=1, source_target_pairs={{0,4},{1,5},{2,6},{3,7},{4,0},{5,1},{6,2},{7,3},{8,12},{9,13},{10,... | collective-permute-start | bytes 1032200 | tf_op jit(solution)/shard_map/ppermute | solution.py:153
  125.0 15.9 %collective-permute-start.16 = (bf16[2,112,512]{2,1,0:T(8,128)(2,1)S(1)}, bf16[2,112,512]{2,1,0:T(8,128)(2,1)S(1)}, u32[]{:S(2)}, u32[]{:S(2)}) collective-permute-start(bf16[2,112,512]{2,1,0:T(8,128)(2,1)S(1)} %copy-done.42), channel_id=1, source_target_pairs={{0,7},{1,6},{2,5},{3,4},{4,3},{5,2},{6,1},{7,0},{8,15},{9,14},{10,... | collective-permute-start | bytes 688136 | tf_op jit(solution)/shard_map/ppermute | solution.py:153
  140.9 12.6 %collective-permute-start.35 = (bf16[3,112,512]{2,1,0:T(8,128)(2,1)}, bf16[3,112,512]{2,1,0:T(8,128)(2,1)S(1)}, u32[]{:S(2)}, u32[]{:S(2)}) collective-permute-start(bf16[3,112,512]{2,1,0:T(8,128)(2,1)} %get-tuple-element.92), channel_id=1, source_target_pairs={{0,5},{1,4},{2,7},{3,6},{4,1},{5,0},{6,3},{7,2},{8,13},{9,12},{10,... | collective-permute-start | bytes 1032200 | tf_op jit(solution)/shard_map/ppermute | solution.py:153
  150.1 27.2 %copy-start.17 = (bf16[3,112,512]{2,1,0:T(8,128)(2,1)}, bf16[3,112,512]{2,1,0:T(8,128)(2,1)S(1)}, u32[]{:S(2)}) copy-start(bf16[3,112,512]{2,1,0:T(8,128)(2,1)S(1)} %collective-permute-done.31.refs_1_) | copy-start | bytes 1032196
  150.2 10.3 %collective-permute-start.36 = (bf16[3,112,512]{2,1,0:T(8,128)(2,1)S(1)}, bf16[3,112,512]{2,1,0:T(8,128)(2,1)S(1)}, u32[]{:S(2)}, u32[]{:S(2)}) collective-permute-start(bf16[3,112,512]{2,1,0:T(8,128)(2,1)S(1)} %copy-done.41), channel_id=1, source_target_pairs={{0,6},{1,7},{2,4},{3,5},{4,2},{5,3},{6,0},{7,1},{8,14},{9,15},{10,... | collective-permute-start | bytes 1032200 | tf_op jit(solution)/shard_map/ppermute | solution.py:153
  151.2 17.9 %collective-permute-start.37 = (bf16[3,112,512]{2,1,0:T(8,128)(2,1)S(1)}, bf16[3,112,512]{2,1,0:T(8,128)(2,1)S(1)}, u32[]{:S(2)}, u32[]{:S(2)}) collective-permute-start(bf16[3,112,512]{2,1,0:T(8,128)(2,1)S(1)} %copy-done.40), channel_id=1, source_target_pairs={{0,7},{1,6},{2,5},{3,4},{4,3},{5,2},{6,1},{7,0},{8,15},{9,14},{10,... | collective-permute-start | bytes 1032200 | tf_op jit(solution)/shard_map/ppermute | solution.py:153
  153.1 15.9 %collective-permute-start.17 = (bf16[3,112,512]{2,1,0:T(8,128)(2,1)}, bf16[3,112,512]{2,1,0:T(8,128)(2,1)S(1)}, u32[]{:S(2)}, u32[]{:S(2)}) collective-permute-start(bf16[3,112,512]{2,1,0:T(8,128)(2,1)} %get-tuple-element.72), channel_id=1, source_target_pairs={{0,1},{1,0},{2,3},{3,2},{4,5},{5,4},{6,7},{7,6},{8,9},{9,8},{10,11... | collective-permute-start | bytes 1032200 | tf_op jit(solution)/shard_map/ppermute | solution.py:153
  153.2 21.5 %collective-permute-start.18 = (bf16[3,112,512]{2,1,0:T(8,128)(2,1)}, bf16[3,112,512]{2,1,0:T(8,128)(2,1)S(1)}, u32[]{:S(2)}, u32[]{:S(2)}) collective-permute-start(bf16[3,112,512]{2,1,0:T(8,128)(2,1)} %get-tuple-element.73), channel_id=1, source_target_pairs={{0,2},{1,3},{2,0},{3,1},{4,6},{5,7},{6,4},{7,5},{8,10},{9,11},{10,... | collective-permute-start | bytes 1032200 | tf_op jit(solution)/shard_map/ppermute | solution.py:153
  153.6 29.7 %collective-permute-start.19 = (bf16[3,112,512]{2,1,0:T(8,128)(2,1)}, bf16[3,112,512]{2,1,0:T(8,128)(2,1)S(1)}, u32[]{:S(2)}, u32[]{:S(2)}) collective-permute-start(bf16[3,112,512]{2,1,0:T(8,128)(2,1)} %get-tuple-element.74), channel_id=1, source_target_pairs={{0,3},{1,2},{2,1},{3,0},{4,7},{5,6},{6,5},{7,4},{8,11},{9,10},{10,... | collective-permute-start | bytes 1032200 | tf_op jit(solution)/shard_map/ppermute | solution.py:153
  160.5 22.8 %collective-permute-start.20 = (bf16[3,112,512]{2,1,0:T(8,128)(2,1)}, bf16[3,112,512]{2,1,0:T(8,128)(2,1)S(1)}, u32[]{:S(2)}, u32[]{:S(2)}) collective-permute-start(bf16[3,112,512]{2,1,0:T(8,128)(2,1)} %get-tuple-element.75), channel_id=1, source_target_pairs={{0,4},{1,5},{2,6},{3,7},{4,0},{5,1},{6,2},{7,3},{8,12},{9,13},{10,... | collective-permute-start | bytes 1032200 | tf_op jit(solution)/shard_map/ppermute | solution.py:153
  169.0 14.8 %collective-permute-start.21 = (bf16[3,112,512]{2,1,0:T(8,128)(2,1)}, bf16[3,112,512]{2,1,0:T(8,128)(2,1)S(1)}, u32[]{:S(2)}, u32[]{:S(2)}) collective-permute-start(bf16[3,112,512]{2,1,0:T(8,128)(2,1)} %get-tuple-element.76), channel_id=1, source_target_pairs={{0,5},{1,4},{2,7},{3,6},{4,1},{5,0},{6,3},{7,2},{8,13},{9,12},{10,... | collective-permute-start | bytes 1032200 | tf_op jit(solution)/shard_map/ppermute | solution.py:153
  169.1 28.8 %copy-start.10 = (bf16[3,112,512]{2,1,0:T(8,128)(2,1)}, bf16[3,112,512]{2,1,0:T(8,128)(2,1)S(1)}, u32[]{:S(2)}) copy-start(bf16[3,112,512]{2,1,0:T(8,128)(2,1)S(1)} %collective-permute-done.17.refs_1_) | copy-start | bytes 1032196
  169.1 20.9 %collective-permute-start.22 = (bf16[3,112,512]{2,1,0:T(8,128)(2,1)}, bf16[3,112,512]{2,1,0:T(8,128)(2,1)S(1)}, u32[]{:S(2)}, u32[]{:S(2)}) collective-permute-start(bf16[3,112,512]{2,1,0:T(8,128)(2,1)} %get-tuple-element.77), channel_id=1, source_target_pairs={{0,6},{1,7},{2,4},{3,5},{4,2},{5,3},{6,0},{7,1},{8,14},{9,15},{10,... | collective-permute-start | bytes 1032200 | tf_op jit(solution)/shard_map/ppermute | solution.py:153
  174.6 23.2 %collective-permute-start.23 = (bf16[3,112,512]{2,1,0:T(8,128)(2,1)}, bf16[3,112,512]{2,1,0:T(8,128)(2,1)S(1)}, u32[]{:S(2)}, u32[]{:S(2)}) collective-permute-start(bf16[3,112,512]{2,1,0:T(8,128)(2,1)} %get-tuple-element.78), channel_id=1, source_target_pairs={{0,7},{1,6},{2,5},{3,4},{4,3},{5,2},{6,1},{7,0},{8,15},{9,14},{10,... | collective-permute-start | bytes 1032200 | tf_op jit(solution)/shard_map/ppermute | solution.py:153
  (33 other events, 495.0 us)

commit v2 on v1

v2 whole, which is shorter than its diff:
```python
import functools

import jax
import jax.numpy as jnp
from jax import lax
from jax.experimental import pallas as pl
from jax.experimental.pallas import tpu as pltpu
from jax.sharding import PartitionSpec as P

beta_one = 0.9
beta_two = 0.95
bias_one = 0.9999734386011124
bias_two = 0.994079470779666
decay_rate = 0.1
adam_eps = 1e-08

BF = jnp.bfloat16
F32 = jnp.float32
CHUNK = 16
PARTS = 2
LIMIT = 61 * 1024 * 1024


def adam_update(weights, first_old, second_old, gradient):
    first_new = beta_one * first_old.astype(F32) + (1.0 - beta_one) * gradient
    second_new = beta_two * second_old.astype(F32) + (1.0 - beta_two) * gradient * gradient
    scaled = first_new / bias_one / (jnp.sqrt(second_new / bias_two) + adam_eps)
    step_new = -(scaled + decay_rate * weights)
    return step_new, first_new, second_new


def quick_update(weights, first_old, second_old, gradient):
    first_new = beta_one * first_old.astype(F32) + (1.0 - beta_one) * gradient
    second_new = beta_two * second_old.astype(F32) + (1.0 - beta_two) * gradient * gradient
    unbiased = second_new * (1.0 / bias_two)
    root = unbiased * lax.rsqrt(unbiased) + adam_eps
    scaled = first_new * (-1.0 / bias_one) * pl.reciprocal(root, approx=True)
    return scaled - decay_rate * weights, first_new, second_new


def spread_kernel(group, counts, grads, acts, *refs):
    outs = refs[1:]
    slots, tok, hidden = acts.shape
    columns = grads.shape[1]
    rows = grads.shape[0] // len(outs)
    row = lax.broadcasted_iota(jnp.int32, (tok, 1), 0)
    live = [jnp.where(row < counts[s], acts[s], jnp.zeros_like(acts[s])) for s in range(slots)]
    for k, out in enumerate(outs):
        start = pl.multiple_of((group[0] ^ k) * rows, CHUNK)
        out[:rows] = grads[pl.ds(start, rows)]
        for s in range(slots):
            for b in range(hidden // columns):
                to = rows + b * slots * tok + s * tok
                out[to : to + tok] = live[s][:, b * columns : (b + 1) * columns]


def pack_kernel(items, me, params, first, second, *refs):
    at = pl.program_id(0)
    for i, (j, _) in enumerate(items):

        @pl.when(at == i)
        def _(out=refs[-2:][j]):
            out[0] = params[...].astype(BF)
            out[1] = first[...]
            out[2] = second[...]


def grad_kernel(rows, part, hidden, me, *refs):
    at = pl.program_id(0)
    groups = lax.axis_size("edp")
    given, outs, table = refs[:groups], refs[-6:-1], refs[-1]
    columns = given[0].shape[1]
    slots, _, piece, width = outs[0].shape
    tok = columns // slots
    core = me[0] & 1

    @pl.when(at == 0)
    def _():
        zero = jnp.zeros((tok, columns), BF)
        for g in range(groups):
            for c in range(2):
                for b in range(width // columns):
                    block = (c * (hidden // 2) + part * width) // columns + b
                    for t in range(slots):
                        source = rows + (block * slots + t) * tok
                        for s in range(slots):
                            to = g * columns + t * tok
                            at = s * width + b * columns
                            table[c, to : to + tok, at : at + columns] = (
                                given[g][source : source + tok] if s == t else zero
                            )

    chip = jnp.where(at == 3, 0, at + 1)
    here = pl.ds(pl.multiple_of(((me[0] >> 1) ^ chip) * piece, CHUNK), piece)
    left = jnp.concatenate([given[g][here] for g in range(groups)], axis=1)
    for c in range(2):
        total = jnp.dot(left, table[core ^ c], preferred_element_type=F32).astype(BF)
        for i in range(4):

            @pl.when(at == i)
            def _(i=i, c=c, total=total):
                for s in range(slots):
                    block = total[:, s * width : (s + 1) * width]
                    if i < 3:
                        outs[i][s, c] = block
                    else:
                        outs[3 + c][s] = block


def find(n, names, places):
    for e in range(n):
        places[names[e]] = e


def update_kernel(n, me_ref, old, rep, new, *refs):
    mine, state, grads, outs = refs[:3], refs[3 : 2 + n], refs[2 + n : 2 + 2 * n], refs[-8:-4]
    sums, placed, owner, target = refs[-4:]
    me = me_ref[0]
    find(n, old, owner)
    find(n, new, target)
    to = [target[old[me ^ k]] ^ me for k in range(n)]
    serves = [owner[rep[me ^ k]] ^ me for k in range(n)]

    def update(r, _):
        rows = pl.ds(pl.multiple_of(r * CHUNK, CHUNK), CHUNK)
        for k in range(n):
            sums[k] = grads[k][0, rows].astype(F32)
        for k in range(n):
            sums[serves[k]] = sums[serves[k]] + grads[k][1, rows].astype(F32)
        for k in range(n):
            old_state = [ref[rows] for ref in mine] if k == 0 else [state[k - 1][i, rows] for i in range(3)]
            updated = quick_update(old_state[0].astype(F32), *old_state[1:], sums[k])
            for i, array in enumerate(updated):
                placed[to[k], i] = array.astype(BF)
        for chip in range(4):
            outs[chip][:, :, rows] = placed[2 * chip : 2 * chip + 2]
        return 0

    lax.fori_loop(0, mine[0].shape[0] // CHUNK, update, 0)


def unpack_kernel(part, me_ref, *refs):
    (step, first, second), (given, wide, came, went) = refs[-7:-4], refs[-4:]
    me = me_ref[0]
    count, _, piece, width = given.shape
    pieces = refs[:count]

    def place(i):
        chip, c = i // 2, i % 2
        row = pl.multiple_of(((me >> 1) ^ chip) * piece, CHUNK)
        column = pl.multiple_of((((me & 1) ^ c) * PARTS + part) * width, 128)
        return pl.ds(row, piece), pl.ds(column, width)

    arrive, leave = [], []
    for i in range(count):
        arrive.append(pltpu.make_async_copy(pieces[i].at[i % 2], given.at[i], came.at[i]))
        arrive[-1].start()
    for i in range(count):
        arrive[i].wait()
        leave.append(pltpu.make_async_copy(given.at[i, 1], first.at[place(i)], went.at[3 * i]))
        leave.append(pltpu.make_async_copy(given.at[i, 2], second.at[place(i)], went.at[3 * i + 1]))
        leave[-2].start()
        leave[-1].start()
        wide[i] = given[i, 0].astype(F32)
        leave.append(pltpu.make_async_copy(wide.at[i], step.at[place(i)], went.at[3 * i + 2]))
        leave[-1].start()
    for copy in leave:
        copy.wait()


def order_kernel(*refs):
    pass


def call(kernel, prefetch, grid, in_specs, out_specs, out_shape, scratch=(), aliases={}):
    return pl.pallas_call(
        kernel,
        grid_spec=pltpu.PrefetchScalarGridSpec(
            num_scalar_prefetch=prefetch,
            grid=grid,
            in_specs=in_specs,
            out_specs=out_specs,
            scratch_shapes=scratch,
        ),
        out_shape=out_shape,
        input_output_aliases=aliases,
        compiler_params=pltpu.CompilerParams(vmem_limit_bytes=LIMIT),
    )


def swap(array, k, axis):
    return lax.ppermute(array, axis, [(i, i ^ k) for i in range(lax.axis_size(axis))])


def fast_local(
    token_acts, out_grad, counts, params, first_moment, second_moment, old_expert, replica_of, new_expert
):
    groups = lax.axis_size("edp")
    n = lax.axis_size("ep")
    model_width, columns = out_grad.shape[2:]
    slots, tok, hidden = token_acts.shape[2:]
    rows = model_width // groups
    piece = rows // 4
    half = hidden // 2
    width = half // PARTS
    chunk = piece // 2 if piece % (2 * CHUNK) == 0 else CHUNK
    me = lax.axis_index("ep").astype(jnp.int32).reshape(1)
    group = lax.axis_index("edp").astype(jnp.int32).reshape(1)
    params, first, second = params[0], first_moment[0], second_moment[0]
    whole = lambda *shape: pl.BlockSpec(shape, lambda i, *_: (0,) * len(shape))
    shape = lambda *dims: jax.ShapeDtypeStruct(dims, BF)
    hbm = pl.BlockSpec(memory_space=pltpu.HBM)
    sibling = lambda array: swap(array, 1, "ep")

    def order(after, *arrays):
        return call(
            order_kernel,
            0,
            (),
            [hbm] * (len(arrays) + len(after)),
            [hbm] * len(arrays),
            [jax.ShapeDtypeStruct(array.shape, array.dtype) for array in arrays],
            aliases={j: j for j in range(len(arrays))},
        )(*arrays, *after)

    def members(kept, near, came, passed):
        result = [(kept, None), (near, None)]
        for here, there in zip(came, passed):
            result += [(here, 0), (there, 1)]
        return result

    def pack(items, chips, shapes, after):
        def block(i, me):
            chip, c = chips[-1]
            for j in range(len(chips) - 1):
                chip = jnp.where(i == j, chips[j][0], chip)
                c = jnp.where(i == j, chips[j][1], c)
            return ((me[0] >> 1) ^ chip, (me[0] & 1) ^ c)

        def slot_spec(j):
            begin = min(i for i, (to, _) in enumerate(items) if to == j)
            last = shapes[j][0] - 1
            return pl.BlockSpec(
                (None, 3, piece, half), lambda i, *_: (jnp.clip(i - begin, 0, last), 0, 0, 0)
            )

        return call(
            functools.partial(pack_kernel, items),
            1,
            (len(items),),
            [pl.BlockSpec((piece, half), block)] * 3 + [hbm] * len(after),
            [slot_spec(j) for j in range(2)],
            [shape(*dims) for dims in shapes],
        )(me, params, first, second, *after)

    two, one = (2, 3, piece, half), (1, 3, piece, half)
    sends = pack([(0, 0), (0, 1), (1, 0), (1, 1)], [(1, 0), (1, 1), (2, 0), (2, 1)], [two, two], [])
    came = [swap(array, 2 + 2 * j, "ep") for j, array in enumerate(sends)]

    tall = rows + slots * tok * (hidden // columns)
    spread = call(
        spread_kernel,
        2,
        (1,),
        [whole(model_width, columns), whole(slots, tok, hidden), hbm],
        [whole(tall, columns)] * groups,
        [shape(tall, columns)] * groups,
    )(group, counts[0, 0], out_grad[0, 0], token_acts[0, 0], sends[0])
    given = [spread[0]] + [swap(spread[k], k, "edp") for k in range(1, groups)]

    diagonal, near = pack([(0, 0), (0, 1), (1, 0)], [(3, 0), (3, 1), (0, 1)], [two, one], [spread[0]])
    last = swap(diagonal, 6, "ep")

    def part_grads(p, after):
        sent, kept = (slots, 2, piece, width), (slots, piece, width)
        return call(
            functools.partial(grad_kernel, rows, p, hidden),
            1,
            (4,),
            [whole(tall, columns)] * groups + [hbm] * len(after),
            [whole(*sent)] * 3 + [whole(*kept)] * 2,
            [shape(*sent)] * 3 + [shape(*kept)] * 2,
            [pltpu.VMEM((2, groups * columns, slots * width), BF)],
        )(me, *given, *after)

    state = [(sibling(near), 0)]
    for array in came:
        state += [(array, 0), (sibling(array), 1)]
    made = [part_grads(0, [state[j][0] for j in (0, 2, 4)])]
    for p in range(1, PARTS):
        made.append(part_grads(p, [made[-1][3]]))
    done = [made[-1][3]]
    last, *others = order(done, last, *[parts[4] for parts in made])
    state += [(last, 0), (sibling(last), 1)]
    grads = []
    for p in range(PARTS):
        arrived = [swap(array, 2 + 2 * j, "ep") for j, array in enumerate(made[p][:3])]
        arrived = order(done, *arrived)
        grads.append([(made[p][3], None), (sibling(others[p]), None)])
        for array in arrived:
            grads[p] += [(array, 0), (sibling(array), 1)]

    def grad_spec(slot):
        if slot is None:
            return pl.BlockSpec((slots, chunk, width), lambda i, *_: (0, i, 0))
        return pl.BlockSpec((slots, None, chunk, width), lambda i, *_: (0, slot, i, 0))

    result = []
    for p in range(PARTS):
        mine = pl.BlockSpec(
            (chunk, width), lambda i, me, *_: ((me[0] >> 1) * (piece // chunk) + i, (me[0] & 1) * PARTS + p)
        )
        held = lambda slot: pl.BlockSpec((None, 3, chunk, width), lambda i, *_: (slot, 0, i, p))
        home, *sent = call(
            functools.partial(update_kernel, n),
            4,
            (piece // chunk,),
            [mine] * 3 + [held(slot) for _, slot in state] + [grad_spec(slot) for _, slot in grads[p]],
            [pl.BlockSpec((2, 3, chunk, width), lambda i, *_: (0, 0, i, 0))] * 4,
            [shape(2, 3, piece, width)] * 4,
            [
                pltpu.VMEM((n, CHUNK, width), F32),
                pltpu.VMEM((n, 3, CHUNK, width), BF),
                pltpu.SMEM((n,), jnp.int32),
                pltpu.SMEM((n,), jnp.int32),
            ],
        )(
            me, old_expert, replica_of, new_expert, params, first, second,
            *[array for array, _ in state], *[array for array, _ in grads[p]],
        )

        if p + 1 < PARTS:
            after = [grads[p + 1][j][0] for j in (3, 5)]
            sent[2:] = order(after, *sent[2:])
        else:
            sent[1:] = order([pieces[1], pieces[3]], *sent[1:])
        arrived = [swap(array, 2 + 2 * j, "ep") for j, array in enumerate(sent)]
        if result:
            arrived = order(result, *arrived)
        pieces = [part for array in [home, *arrived] for part in (array, sibling(array))]
        result = call(
            functools.partial(unpack_kernel, p),
            1,
            (),
            [hbm] * (len(pieces) + len(result)),
            [hbm] * 3,
            [jax.ShapeDtypeStruct((rows, hidden), d) for d in (F32, BF, BF)],
            [
                pltpu.VMEM((len(pieces), 3, piece, width), BF),
                pltpu.VMEM((len(pieces), piece, width), F32),
                pltpu.SemaphoreType.DMA((len(pieces),)),
                pltpu.SemaphoreType.DMA((3 * len(pieces),)),
            ],
            {1 + len(pieces) + j: j for j in range(len(result))},
        )(me, *pieces, *result)
    step, first, second = result
    return step[None], first[None], second[None]


def plain_local(
    token_acts, out_grad, counts, params, first_moment, second_moment, old_expert, replica_of, new_expert
):
    groups = lax.axis_size("edp")
    owners = lax.axis_size("ep")
    model_width = out_grad.shape[2]
    slots, tok, hidden = token_acts.shape[2:]
    rows = model_width // groups
    piece = rows * hidden // owners
    exchange = functools.partial(lax.all_to_all, axis_name="ep", split_axis=0, concat_axis=0, tiled=True)
    row = jnp.arange(tok, dtype=jnp.int32)
    live = row[None, :] < counts[0, 0][:, None]
    acts = jnp.where(live[:, :, None], token_acts[0, 0], jnp.zeros_like(token_acts[0, 0]))
    all_acts = lax.all_gather(acts, "edp", axis=0)
    all_grads = lax.all_to_all(
        out_grad[0, 0].reshape(groups, rows, slots * tok), "edp", split_axis=0, concat_axis=0, tiled=True
    ).reshape(groups, rows, slots, tok)
    slot_grads = jnp.einsum("adst,astf->sdf", all_grads, all_acts, preferred_element_type=F32)
    pieces = lambda array: exchange(array.astype(BF).reshape(owners, piece))
    own, replica = pieces(slot_grads[0]), pieces(slot_grads[1])
    sum_matrix = (replica_of[None, :] == old_expert[:, None]).astype(BF)
    move_matrix = (old_expert[None, :] == new_expert[:, None]).astype(BF)
    total = own.astype(F32) + jnp.dot(sum_matrix, replica, preferred_element_type=F32)
    updated = adam_update(
        pieces(params[0]).astype(F32), pieces(first_moment[0]), pieces(second_moment[0]), total
    )
    result = []
    for array, kind in zip(updated, (F32, BF, BF)):
        placed = jnp.dot(move_matrix, array.astype(BF), preferred_element_type=F32)
        result.append(exchange(placed.astype(BF)).astype(kind).reshape(1, rows, hidden))
    return tuple(result)


def local(token_acts, out_grad, *others):
    groups, n = lax.axis_size("edp"), lax.axis_size("ep")
    rows, columns = out_grad.shape[2] // groups, out_grad.shape[3]
    slots, tok, hidden = token_acts.shape[2:]
    fast = n == 8 and groups & (groups - 1) == 0 and rows % (4 * CHUNK) == 0
    fast = fast and slots == 2 and columns == 128 and tok == 64 and hidden % (256 * PARTS) == 0
    return (fast_local if fast else plain_local)(token_acts, out_grad, *others)


def solution(mesh):
    return jax.shard_map(
        local,
        mesh=mesh,
        in_specs=(
            P("edp", "ep", None, None, None),
            P("edp", "ep", None, None),
            P("edp", "ep", None),
            P("ep", "edp", None),
            P("ep", "edp", None),
            P("ep", "edp", None),
            P(),
            P(),
            P(),
        ),
        out_specs=(P("ep", "edp", None), P("ep", "edp", None), P("ep", "edp", None)),
        check_vma=False,
    )
```

time: 205 us -> 237 us (1.16)
  waiting for transfers between devices: 91.8 us -> 147 us
  starting transfers between devices: 63.6 us -> 34.7 us
  local copies, waits for them, and re-layouts: 0.86 us -> 11.8 us
  Pallas kernels: 46.4 us -> 40.5 us
    ppermute x38, waiting for transfers between devices: 91.8 us -> 147 us  [swap(): lax.ppermute(array, axis, [(i, i ^ k) for i in range(lax.axis_size(axis))])]
    ppermute x38, starting transfers between devices: 63.6 us -> 34.7 us  [swap(): lax.ppermute(array, axis, [(i, i ^ k) for i in range(lax.axis_size(axis))])]
    unnamed x86 -> x64, local copies, waits for them, and re-layouts: 0.86 us -> 11.8 us
    pallas_call x8 -> x15, Pallas kernels: 46.4 us -> 40.5 us  [the longest x2 11.7 us: fast_local(): call(functools.partial(update_kernel, n), 4, (piece // chunk,), [mine] *...]
  transfers between devices with their start and end apart: 38 -> 38, of which waited for: 18 -> 17; matrix products, arithmetic and copies ran while one was open for 0% -> 0% of each run, Pallas kernels for 18% -> 14%
where the time goes in v2:
time: 237 us; the launch traced here: 235 us
  waiting for transfers between devices  147 us (62%)
  Pallas kernels  40.5 us (17%)
  starting transfers between devices  34.7 us (15%)
  local copies, waits for them, and re-layouts  11.8 us (5%)
    ppermute x38, waiting for transfers between devices, swap(): lax.ppermute(array, axis, [(i, i ^ k) for i in range(lax.axis_size(axis))])  147 us
    ppermute x38, starting transfers between devices, swap(): lax.ppermute(array, axis, [(i, i ^ k) for i in range(lax.axis_size(axis))])  34.7 us
    unnamed x64, local copies, waits for them, and re-layouts  11.8 us
    pallas_call x2, Pallas kernels, fast_local(): call(functools.partial(update_kernel, n), 4, (piece // chunk,), [mine] *...  11.7 us
    pallas_call x2, Pallas kernels, part_grads(): call(functools.partial(grad_kernel, rows, p, hidden), 1, (4,), [whole(tal...  11 us
    pallas_call x2, Pallas kernels, pack(): call(functools.partial(pack_kernel, items), 1, (len(items),), [pl.BlockSp...  8.35 us
    pallas_call x2, Pallas kernels, fast_local(): call(functools.partial(unpack_kernel, p), 1, (), [hbm] * (len(pieces) + l...  6.16 us
  transfers between devices with their start and end apart: 38, of which 17 were waited for; matrix products, arithmetic and copies ran while one was open for 0% of the time, Pallas kernels for 14%

profile of v2, /device:TPU:17, one launch (start us, length us, event | category | flops | bytes accessed | tf_op | source)
XLA Modules:
  0.0 235.0 jit_solution(12726017205227757025)
XLA Ops:
  0.6 4.5 %shard_map.112 = (bf16[2,3,224,512]{3,2,1,0:T(8,128)(2,1)}, bf16[2,3,224,512]{3,2,1,0:T(8,128)(2,1)}) custom-call(s32[1]{0:T(128)} %bitcast.me.me_ref, f32[896,1024]{1,0:T(8,128)} %bitcast.11, bf16[896,1024]{1,0:T(8,128)(2,1)} %bitcast.15, bf16[896,1024]{1,0:T(8,128)(2,1)} %bitcast.19), custom_call_target="tpu_custom_call" | custom-call | tf_op jit(solution)/shard_map/pallas_call | solution.py:247
  5.1 1.2 collective-permute-start.3
  6.4 1.2 collective-permute-start.1
  7.6 3.4 %shard_map.113 = (bf16[1920,128]{1,0:T(8,128)(2,1)}, bf16[1920,128]{1,0:T(8,128)(2,1)}, bf16[1920,128]{1,0:T(8,128)(2,1)}, bf16[1920,128]{1,0:T(8,128)(2,1)}) custom-call(s32[1]{0:T(128)} %bitcast.4.group, s32[2]{0:T(128)} %bitcast.28, bf16[3584,128]{1,0:T(8,128)(2,1)} %bitcast.26, bf16[2,64,1024]{2,1,0:T(8,128)(2,1)} %bitcast.27, ...), custom_call_target="tpu_custom_call" | custom-call | tf_op jit(solution)/shard_map/pallas_call | solution.py:261
  11.0 25.6 %collective-permute-done.3.refs_6_ = bf16[2,3,224,512]{3,2,1,0:T(8,128)(2,1)} collective-permute-done((bf16[2,3,224,512]{3,2,1,0:T(8,128)(2,1)}, bf16[2,3,224,512]{3,2,1,0:T(8,128)(2,1)}, u32[]{:S(2)}, u32[]{:S(2)}) %collective-permute-start.3) | collective-permute-done | bytes 1376288 | tf_op jit(solution)/shard_map/ppermute | solution.py:192
  36.5 1.5 collective-permute-start.4
  38.1 1.2 collective-permute-start.2
  39.3 3.8 %shard_map.114 = (bf16[2,3,224,512]{3,2,1,0:T(8,128)(2,1)}, bf16[1,3,224,512]{3,2,1,0:T(8,128)(2,1)}) custom-call(s32[1]{0:T(128)} %bitcast.me.me_ref, f32[896,1024]{1,0:T(8,128)} %bitcast.12, bf16[896,1024]{1,0:T(8,128)(2,1)} %bitcast.16, bf16[896,1024]{1,0:T(8,128)(2,1)} %bitcast.20, bf16[1920,128]{1,0:T(8,128)(2,1)} %get-tuple-element.50.refs_0_), custom_call_target="tpu_custom_call" | custom-call | tf_op jit(solution)/shard_map/pallas_call | solution.py:247
  43.1 1.2 collective-permute-start.5
  44.3 1.3 collective-permute-start.6
  45.6 19.6 %collective-permute-done.6.refs_1_ = bf16[1920,128]{1,0:T(8,128)(2,1)S(1)} collective-permute-done((bf16[1920,128]{1,0:T(8,128)(2,1)}, bf16[1920,128]{1,0:T(8,128)(2,1)S(1)}, u32[]{:S(2)}, u32[]{:S(2)}) %collective-permute-start.6) | collective-permute-done | bytes 491552 | tf_op jit(solution)/shard_map/ppermute | solution.py:192
  66.0 1.4 collective-permute-start
  67.4 1.2 collective-permute-start.8
  68.6 21.0 %collective-permute-done.8.refs_3_ = bf16[1920,128]{1,0:T(8,128)(2,1)S(1)} collective-permute-done((bf16[1920,128]{1,0:T(8,128)(2,1)}, bf16[1920,128]{1,0:T(8,128)(2,1)S(1)}, u32[]{:S(2)}, u32[]{:S(2)}) %collective-permute-start.8) | collective-permute-done | bytes 491552 | tf_op jit(solution)/shard_map/ppermute | solution.py:192
  90.7 1.1 copy-done
  91.8 1.1 copy-done.1
  92.8 5.5 %shard_map.115 = (bf16[2,2,224,256]{3,2,1,0:T(8,128)(2,1)}, bf16[2,2,224,256]{3,2,1,0:T(8,128)(2,1)}, bf16[2,2,224,256]{3,2,1,0:T(8,128)(2,1)}, bf16[2,224,256]{2,1,0:T(8,128)(2,1)}, bf16[2,224,256]{2,1,0:T(8,128)(2,1)}) custom-call(s32[1]{0:T(128)} %bitcast.me.me_ref, bf16[1920,128]{1,0:T(8,128)(2,1)} %get-tuple-element.50.refs_0_, ...), custom_call_target="tpu_custom_call" | custom-call | tf_op jit(solution)/shard_map/pallas_call | solution.py:276
  98.3 5.5 %shard_map.116 = (bf16[2,2,224,256]{3,2,1,0:T(8,128)(2,1)}, bf16[2,2,224,256]{3,2,1,0:T(8,128)(2,1)}, bf16[2,2,224,256]{3,2,1,0:T(8,128)(2,1)}, bf16[2,224,256]{2,1,0:T(8,128)(2,1)}, bf16[2,224,256]{2,1,0:T(8,128)(2,1)}) custom-call(s32[1]{0:T(128)} %bitcast.me.me_ref, bf16[1920,128]{1,0:T(8,128)(2,1)} %get-tuple-element.50.refs_0_, ...), custom_call_target="tpu_custom_call" | custom-call | tf_op jit(solution)/shard_map/pallas_call | solution.py:276
  103.8 2.2 collective-permute-start.9
  106.3 1.4 collective-permute-start.21
  107.7 1.0 collective-permute-start.22
  108.7 9.6 %collective-permute-done.20.refs_0_ = bf16[2,2,224,256]{3,2,1,0:T(8,128)(2,1)S(1)} collective-permute-done((bf16[2,2,224,256]{3,2,1,0:T(8,128)(2,1)}, bf16[2,2,224,256]{3,2,1,0:T(8,128)(2,1)S(1)}, u32[]{:S(2)}, u32[]{:S(2)}) %collective-permute-start.20) | collective-permute-done | bytes 458784 | tf_op jit(solution)/shard_map/ppermute | solution.py:192
  118.3 10.9 %collective-permute-done.22.refs_2_ = bf16[2,2,224,256]{3,2,1,0:T(8,128)(2,1)S(1)} collective-permute-done((bf16[2,2,224,256]{3,2,1,0:T(8,128)(2,1)}, bf16[2,2,224,256]{3,2,1,0:T(8,128)(2,1)S(1)}, u32[]{:S(2)}, u32[]{:S(2)}) %collective-permute-start.22) | collective-permute-done | bytes 458784 | tf_op jit(solution)/shard_map/ppermute | solution.py:192
  131.5 1.6 collective-permute-done.19.refs_11_
  133.5 2.1 collective-permute-start.12
  137.2 1.1 copy-done.3
  138.3 5.9 %shard_map.121 = (bf16[2,3,224,256]{3,2,1,0:T(8,128)(2,1)}, bf16[2,3,224,256]{3,2,1,0:T(8,128)(2,1)}, bf16[2,3,224,256]{3,2,1,0:T(8,128)(2,1)}, bf16[2,3,224,256]{3,2,1,0:T(8,128)(2,1)}) custom-call(s32[1]{0:T(128)} %bitcast.me.me_ref, s32[8]{0:T(128)} %old.3, s32[8]{0:T(128)} %rep.3, s32[8]{0:T(128)} %new.3, f32[896,1024]{1,0:T(8,128)} %bitcast.13, ...), custom_call_target="tpu_custom_call" | custom-call | tf_op jit(solution)/shard_map/pallas_call | solution.py:314
  145.0 1.1 collective-permute-done.12.refs_1_
  146.1 9.8 %collective-permute-done.13.refs_2_ = bf16[2,2,224,256]{3,2,1,0:T(8,128)(2,1)S(1)} collective-permute-done((bf16[2,2,224,256]{3,2,1,0:T(8,128)(2,1)}, bf16[2,2,224,256]{3,2,1,0:T(8,128)(2,1)S(1)}, u32[]{:S(2)}, u32[]{:S(2)}) %collective-permute-start.13) | collective-permute-done | bytes 458784 | tf_op jit(solution)/shard_map/ppermute | solution.py:192
  156.7 2.0 collective-permute-start.14
  159.2 1.5 collective-permute-start.31
  161.8 1.4 collective-permute-start.33
  163.9 5.9 %collective-permute-done.27.refs_2_ = bf16[2,3,224,256]{3,2,1,0:T(8,128)(2,1)} collective-permute-done((bf16[2,3,224,256]{3,2,1,0:T(8,128)(2,1)}, bf16[2,3,224,256]{3,2,1,0:T(8,128)(2,1)}, u32[]{:S(2)}, u32[]{:S(2)}) %collective-permute-start.27) | collective-permute-done | bytes 688160 | tf_op jit(solution)/shard_map/ppermute | solution.py:192
  169.7 2.0 collective-permute-start.28
  171.8 2.5 %collective-permute-done.16.refs_17_ = bf16[2,2,224,256]{3,2,1,0:T(8,128)(2,1)} collective-permute-done((bf16[2,2,224,256]{3,2,1,0:T(8,128)(2,1)S(1)}, bf16[2,2,224,256]{3,2,1,0:T(8,128)(2,1)}, u32[]{:S(2)}, u32[]{:S(2)}) %collective-permute-start.16) | collective-permute-done | bytes 458784 | tf_op jit(solution)/shard_map/ppermute | solution.py:192
  174.3 5.8 %shard_map.119 = (bf16[2,3,224,256]{3,2,1,0:T(8,128)(2,1)}, bf16[2,3,224,256]{3,2,1,0:T(8,128)(2,1)}, bf16[2,3,224,256]{3,2,1,0:T(8,128)(2,1)}, bf16[2,3,224,256]{3,2,1,0:T(8,128)(2,1)}) custom-call(s32[1]{0:T(128)} %bitcast.me.me_ref, s32[8]{0:T(128)} %old.3, s32[8]{0:T(128)} %rep.3, s32[8]{0:T(128)} %new.3, f32[896,1024]{1,0:T(8,128)} %bitcast.14, ...), custom_call_target="tpu_custom_call" | custom-call | tf_op jit(solution)/shard_map/pallas_call | solution.py:314
  180.6 10.6 %collective-permute-done.31.refs_4_ = bf16[2,3,224,256]{3,2,1,0:T(8,128)(2,1)} collective-permute-done((bf16[2,3,224,256]{3,2,1,0:T(8,128)(2,1)}, bf16[2,3,224,256]{3,2,1,0:T(8,128)(2,1)}, u32[]{:S(2)}, u32[]{:S(2)}) %collective-permute-start.31) | collective-permute-done | bytes 688160 | tf_op jit(solution)/shard_map/ppermute | solution.py:192
  193.2 1.5 collective-permute-start.29
  194.7 0.9 collective-permute-start.30
  195.6 1.1 collective-permute-start.17
  196.7 3.1 %shard_map.124 = (f32[896,1024]{1,0:T(8,128)}, bf16[896,1024]{1,0:T(8,128)(2,1)}, bf16[896,1024]{1,0:T(8,128)(2,1)}) custom-call(s32[1]{0:T(128)} %bitcast.me.me_ref, bf16[2,3,224,256]{3,2,1,0:T(8,128)(2,1)} %get-tuple-element.80.refs_0_, bf16[2,3,224,256]{3,2,1,0:T(8,128)(2,1)} %copy-done.4, bf16[2,3,224,256]{3,2,1,0:T(8,128)(2,1)} %collective-permute-done.27.refs_2_, ...), custom_call_target="tpu_custom_call" | custom-call | tf_op jit(solution)/shard_map/pallas_call | solution.py:341
  199.8 24.9 %collective-permute-done.29.refs_1_ = bf16[2,3,224,256]{3,2,1,0:T(8,128)(2,1)S(1)} collective-permute-done((bf16[2,3,224,256]{3,2,1,0:T(8,128)(2,1)}, bf16[2,3,224,256]{3,2,1,0:T(8,128)(2,1)S(1)}, u32[]{:S(2)}, u32[]{:S(2)}) %collective-permute-start.29) | collective-permute-done | bytes 688160 | tf_op jit(solution)/shard_map/ppermute | solution.py:192
  225.8 1.4 collective-permute-start.35
  227.7 1.5 collective-permute-done.35.refs_3_
  229.1 1.0 collective-permute-done.36.refs_5_
  230.1 1.0 collective-permute-done.37.refs_7_
  231.1 0.9 copy-done.25
  232.0 3.1 %shard_map.126 = (f32[896,1024]{1,0:T(8,128)}, bf16[896,1024]{1,0:T(8,128)(2,1)}, bf16[896,1024]{1,0:T(8,128)(2,1)}) custom-call(s32[1]{0:T(128)} %bitcast.me.me_ref, bf16[2,3,224,256]{3,2,1,0:T(8,128)(2,1)} %get-tuple-element.69.refs_0_, ...), custom_call_target="tpu_custom_call", output_to_operand_aliasing={{0}: (9, {}), {1}: (10, {}), {2}: (11, {})} | custom-call | tf_op jit(solution)/shard_map/pallas_call | solution.py:341
  (107 shorter events, 14.4 us)
Async XLA Ops:
  5.1 31.4 %collective-permute-start.3 = (bf16[2,3,224,512]{3,2,1,0:T(8,128)(2,1)}, bf16[2,3,224,512]{3,2,1,0:T(8,128)(2,1)}, u32[]{:S(2)}, u32[]{:S(2)}) collective-permute-start(bf16[2,3,224,512]{3,2,1,0:T(8,128)(2,1)} %get-tuple-element.52), channel_id=1, source_target_pairs={{0,4},{1,5},{2,6},{3,7},{4,0},{5,1},{6,2},{7,3},{8,12},{9,13},{10,... | collective-permute-start | bytes 4128776 | tf_op jit(solution)/shard_map/ppermute | solution.py:192
  6.4 31.7 %collective-permute-start.1 = (bf16[2,3,224,512]{3,2,1,0:T(8,128)(2,1)}, bf16[2,3,224,512]{3,2,1,0:T(8,128)(2,1)}, u32[]{:S(2)}, u32[]{:S(2)}) collective-permute-start(bf16[2,3,224,512]{3,2,1,0:T(8,128)(2,1)} %get-tuple-element.49.refs_0_), channel_id=1, source_target_pairs={{0,2},{1,3},{2,0},{3,1},{4,6},{5,7},{6,4},{7,5},{8,10},{9,11},{10,... | collective-permute-start | bytes 4128776 | tf_op jit(solution)/shard_map/ppermute | solution.py:192
  36.5 53.1 %collective-permute-start.4 = (bf16[2,3,224,512]{3,2,1,0:T(8,128)(2,1)}, bf16[2,3,224,512]{3,2,1,0:T(8,128)(2,1)S(1)}, u32[]{:S(2)}, u32[]{:S(2)}) collective-permute-start(bf16[2,3,224,512]{3,2,1,0:T(8,128)(2,1)} %collective-permute-done.3.refs_6_), channel_id=1, source_target_pairs={{0,1},{1,0},{2,3},{3,2},{4,5},{5,4},{6,7},{7,6},{8,9},{9,8},{10,11... | collective-permute-start | bytes 4128776 | tf_op jit(solution)/shard_map/ppermute | solution.py:192
  38.1 52.6 %collective-permute-start.2 = (bf16[2,3,224,512]{3,2,1,0:T(8,128)(2,1)}, bf16[2,3,224,512]{3,2,1,0:T(8,128)(2,1)S(1)}, u32[]{:S(2)}, u32[]{:S(2)}) collective-permute-start(bf16[2,3,224,512]{3,2,1,0:T(8,128)(2,1)} %collective-permute-done.1.refs_4_), channel_id=1, source_target_pairs={{0,1},{1,0},{2,3},{3,2},{4,5},{5,4},{6,7},{7,6},{8,9},{9,8},{10,11... | collective-permute-start | bytes 4128776 | tf_op jit(solution)/shard_map/ppermute | solution.py:192
  43.1 60.7 %collective-permute-start.5 = (bf16[2,3,224,512]{3,2,1,0:T(8,128)(2,1)}, bf16[2,3,224,512]{3,2,1,0:T(8,128)(2,1)}, u32[]{:S(2)}, u32[]{:S(2)}) collective-permute-start(bf16[2,3,224,512]{3,2,1,0:T(8,128)(2,1)} %get-tuple-element.53), channel_id=1, source_target_pairs={{0,6},{1,7},{2,4},{3,5},{4,2},{5,3},{6,0},{7,1},{8,14},{9,15},{10,... | collective-permute-start | bytes 4128776 | tf_op jit(solution)/shard_map/ppermute | solution.py:192
  44.3 20.9 %collective-permute-start.6 = (bf16[1920,128]{1,0:T(8,128)(2,1)}, bf16[1920,128]{1,0:T(8,128)(2,1)S(1)}, u32[]{:S(2)}, u32[]{:S(2)}) collective-permute-start(bf16[1920,128]{1,0:T(8,128)(2,1)} %get-tuple-element.54), channel_id=1, source_target_pairs={{0,8},{8,0},{16,24},{24,16},{1,9},{9,1},{17,25},{25,17},{2,10},{10... | collective-permute-start | bytes 1474568 | tf_op jit(solution)/shard_map/ppermute | solution.py:192
  45.6 21.8 %collective-permute-start.7 = (bf16[1920,128]{1,0:T(8,128)(2,1)}, bf16[1920,128]{1,0:T(8,128)(2,1)S(1)}, u32[]{:S(2)}, u32[]{:S(2)}) collective-permute-start(bf16[1920,128]{1,0:T(8,128)(2,1)} %get-tuple-element.55), channel_id=1, source_target_pairs={{0,16},{8,24},{16,0},{24,8},{1,17},{9,25},{17,1},{25,9},{2,18},{10... | collective-permute-start | bytes 1474568 | tf_op jit(solution)/shard_map/ppermute | solution.py:192
  66.0 23.7 %collective-permute-start = (bf16[1,3,224,512]{3,2,1,0:T(8,128)(2,1)}, bf16[1,3,224,512]{3,2,1,0:T(8,128)(2,1)S(1)}, u32[]{:S(2)}, u32[]{:S(2)}) collective-permute-start(bf16[1,3,224,512]{3,2,1,0:T(8,128)(2,1)} %get-tuple-element.51), channel_id=1, source_target_pairs={{0,1},{1,0},{2,3},{3,2},{4,5},{5,4},{6,7},{7,6},{8,9},{9,8},{10,11... | collective-permute-start | bytes 2064392 | tf_op jit(solution)/shard_map/ppermute | solution.py:192
  67.4 22.2 %copy-start.10 = (bf16[1920,128]{1,0:T(8,128)(2,1)}, bf16[1920,128]{1,0:T(8,128)(2,1)S(1)}, u32[]{:S(2)}) copy-start(bf16[1920,128]{1,0:T(8,128)(2,1)S(1)} %collective-permute-done.7.refs_2_) | copy-start | bytes 1474564
  67.4 22.2 %collective-permute-start.8 = (bf16[1920,128]{1,0:T(8,128)(2,1)}, bf16[1920,128]{1,0:T(8,128)(2,1)S(1)}, u32[]{:S(2)}, u32[]{:S(2)}) collective-permute-start(bf16[1920,128]{1,0:T(8,128)(2,1)} %get-tuple-element.56), channel_id=1, source_target_pairs={{0,24},{8,16},{16,8},{24,0},{1,25},{9,17},{17,9},{25,1},{2,26},{10... | collective-permute-start | bytes 1474568 | tf_op jit(solution)/shard_map/ppermute | solution.py:192
  103.8 27.2 %copy-start.31 = (bf16[2,224,256]{2,1,0:T(8,128)(2,1)S(1)}, bf16[2,224,256]{2,1,0:T(8,128)(2,1)}, u32[]{:S(2)}) copy-start(bf16[2,224,256]{2,1,0:T(8,128)(2,1)} %get-tuple-element.73) | copy-start | bytes 688132
  103.8 33.4 %collective-permute-start.9 = (bf16[2,3,224,512]{3,2,1,0:T(8,128)(2,1)}, bf16[2,3,224,512]{3,2,1,0:T(8,128)(2,1)S(1)}, u32[]{:S(2)}, u32[]{:S(2)}) collective-permute-start(bf16[2,3,224,512]{3,2,1,0:T(8,128)(2,1)} %get-tuple-element.61.refs_8_), channel_id=1, source_target_pairs={{0,1},{1,0},{2,3},{3,2},{4,5},{5,4},{6,7},{7,6},{8,9},{9,8},{10,11... | collective-permute-start | bytes 4128776 | tf_op jit(solution)/shard_map/ppermute | solution.py:192
  106.0 12.3 %collective-permute-start.20 = (bf16[2,2,224,256]{3,2,1,0:T(8,128)(2,1)}, bf16[2,2,224,256]{3,2,1,0:T(8,128)(2,1)S(1)}, u32[]{:S(2)}, u32[]{:S(2)}) collective-permute-start(bf16[2,2,224,256]{3,2,1,0:T(8,128)(2,1)} %get-tuple-element.74), channel_id=1, source_target_pairs={{0,2},{1,3},{2,0},{3,1},{4,6},{5,7},{6,4},{7,5},{8,10},{9,11},{10,... | collective-permute-start | bytes 1376264 | tf_op jit(solution)/shard_map/ppermute | solution.py:192
  106.3 12.0 %collective-permute-start.21 = (bf16[2,2,224,256]{3,2,1,0:T(8,128)(2,1)}, bf16[2,2,224,256]{3,2,1,0:T(8,128)(2,1)S(1)}, u32[]{:S(2)}, u32[]{:S(2)}) collective-permute-start(bf16[2,2,224,256]{3,2,1,0:T(8,128)(2,1)} %get-tuple-element.75), channel_id=1, source_target_pairs={{0,4},{1,5},{2,6},{3,7},{4,0},{5,1},{6,2},{7,3},{8,12},{9,13},{10,... | collective-permute-start | bytes 1376264 | tf_op jit(solution)/shard_map/ppermute | solution.py:192
  107.7 21.6 %collective-permute-start.22 = (bf16[2,2,224,256]{3,2,1,0:T(8,128)(2,1)}, bf16[2,2,224,256]{3,2,1,0:T(8,128)(2,1)S(1)}, u32[]{:S(2)}, u32[]{:S(2)}) collective-permute-start(bf16[2,2,224,256]{3,2,1,0:T(8,128)(2,1)} %get-tuple-element.76), channel_id=1, source_target_pairs={{0,6},{1,7},{2,4},{3,5},{4,2},{5,3},{6,0},{7,1},{8,14},{9,15},{10,... | collective-permute-start | bytes 1376264 | tf_op jit(solution)/shard_map/ppermute | solution.py:192
  118.3 10.9 %copy-start.16 = (bf16[2,2,224,256]{3,2,1,0:T(8,128)(2,1)}, bf16[2,2,224,256]{3,2,1,0:T(8,128)(2,1)S(1)}, u32[]{:S(2)}) copy-start(bf16[2,2,224,256]{3,2,1,0:T(8,128)(2,1)S(1)} %collective-permute-done.20.refs_0_) | copy-start | bytes 1376260
  118.3 10.9 %copy-start.17 = (bf16[2,2,224,256]{3,2,1,0:T(8,128)(2,1)}, bf16[2,2,224,256]{3,2,1,0:T(8,128)(2,1)S(1)}, u32[]{:S(2)}) copy-start(bf16[2,2,224,256]{3,2,1,0:T(8,128)(2,1)S(1)} %collective-permute-done.21.refs_1_) | copy-start | bytes 1376260
  130.1 3.4 %collective-permute-start.23 = (bf16[2,2,224,256]{3,2,1,0:T(8,128)(2,1)}, bf16[2,2,224,256]{3,2,1,0:T(8,128)(2,1)S(1)}, u32[]{:S(2)}, u32[]{:S(2)}) collective-permute-start(bf16[2,2,224,256]{3,2,1,0:T(8,128)(2,1)} %get-tuple-element.77.refs_12_), channel_id=1, source_target_pairs={{0,1},{1,0},{2,3},{3,2},{4,5},{5,4},{6,7},{7,6},{8,9},{9,8},{10,11... | collective-permute-start | bytes 1376264 | tf_op jit(solution)/shard_map/ppermute | solution.py:192
  131.0 4.7 %collective-permute-start.24 = (bf16[2,2,224,256]{3,2,1,0:T(8,128)(2,1)}, bf16[2,2,224,256]{3,2,1,0:T(8,128)(2,1)S(1)}, u32[]{:S(2)}, u32[]{:S(2)}) collective-permute-start(bf16[2,2,224,256]{3,2,1,0:T(8,128)(2,1)} %get-tuple-element.78.refs_14_), channel_id=1, source_target_pairs={{0,1},{1,0},{2,3},{3,2},{4,5},{5,4},{6,7},{7,6},{8,9},{9,8},{10,11... | collective-permute-start | bytes 1376264 | tf_op jit(solution)/shard_map/ppermute | solution.py:192
  131.0 2.1 collective-permute-start.19
  131.5 4.4 %collective-permute-start.25 = (bf16[2,2,224,256]{3,2,1,0:T(8,128)(2,1)}, bf16[2,2,224,256]{3,2,1,0:T(8,128)(2,1)S(1)}, u32[]{:S(2)}, u32[]{:S(2)}) collective-permute-start(bf16[2,2,224,256]{3,2,1,0:T(8,128)(2,1)} %get-tuple-element.79.refs_16_), channel_id=1, source_target_pairs={{0,1},{1,0},{2,3},{3,2},{4,5},{5,4},{6,7},{7,6},{8,9},{9,8},{10,11... | collective-permute-start | bytes 1376264 | tf_op jit(solution)/shard_map/ppermute | solution.py:192
  133.1 4.1 %copy-start.30 = (bf16[2,224,256]{2,1,0:T(8,128)(2,1)}, bf16[2,224,256]{2,1,0:T(8,128)(2,1)S(1)}, u32[]{:S(2)}) copy-start(bf16[2,224,256]{2,1,0:T(8,128)(2,1)S(1)} %collective-permute-done.19.refs_11_) | copy-start | bytes 688132
  133.1 11.9 %collective-permute-start.11 = (bf16[2,2,224,256]{3,2,1,0:T(8,128)(2,1)}, bf16[2,2,224,256]{3,2,1,0:T(8,128)(2,1)S(1)}, u32[]{:S(2)}, u32[]{:S(2)}) collective-permute-start(bf16[2,2,224,256]{3,2,1,0:T(8,128)(2,1)} %get-tuple-element.63), channel_id=1, source_target_pairs={{0,2},{1,3},{2,0},{3,1},{4,6},{5,7},{6,4},{7,5},{8,10},{9,11},{10,... | collective-permute-start | bytes 1376264 | tf_op jit(solution)/shard_map/ppermute | solution.py:192
  133.5 12.6 %collective-permute-start.12 = (bf16[2,2,224,256]{3,2,1,0:T(8,128)(2,1)}, bf16[2,2,224,256]{3,2,1,0:T(8,128)(2,1)S(1)}, u32[]{:S(2)}, u32[]{:S(2)}) collective-permute-start(bf16[2,2,224,256]{3,2,1,0:T(8,128)(2,1)} %get-tuple-element.64), channel_id=1, source_target_pairs={{0,4},{1,5},{2,6},{3,7},{4,0},{5,1},{6,2},{7,3},{8,12},{9,13},{10,... | collective-permute-start | bytes 1376264 | tf_op jit(solution)/shard_map/ppermute | solution.py:192
  135.6 20.3 %collective-permute-start.13 = (bf16[2,2,224,256]{3,2,1,0:T(8,128)(2,1)}, bf16[2,2,224,256]{3,2,1,0:T(8,128)(2,1)S(1)}, u32[]{:S(2)}, u32[]{:S(2)}) collective-permute-start(bf16[2,2,224,256]{3,2,1,0:T(8,128)(2,1)} %get-tuple-element.65), channel_id=1, source_target_pairs={{0,6},{1,7},{2,4},{3,5},{4,2},{5,3},{6,0},{7,1},{8,14},{9,15},{10,... | collective-permute-start | bytes 1376264 | tf_op jit(solution)/shard_map/ppermute | solution.py:192
  144.2 25.6 %collective-permute-start.27 = (bf16[2,3,224,256]{3,2,1,0:T(8,128)(2,1)}, bf16[2,3,224,256]{3,2,1,0:T(8,128)(2,1)}, u32[]{:S(2)}, u32[]{:S(2)}) collective-permute-start(bf16[2,3,224,256]{3,2,1,0:T(8,128)(2,1)} %get-tuple-element.81), channel_id=1, source_target_pairs={{0,2},{1,3},{2,0},{3,1},{4,6},{5,7},{6,4},{7,5},{8,10},{9,11},{10,... | collective-permute-start | bytes 2064392 | tf_op jit(solution)/shard_map/ppermute | solution.py:192
  145.0 10.9 %copy-start.12 = (bf16[2,2,224,256]{3,2,1,0:T(8,128)(2,1)}, bf16[2,2,224,256]{3,2,1,0:T(8,128)(2,1)S(1)}, u32[]{:S(2)}) copy-start(bf16[2,2,224,256]{3,2,1,0:T(8,128)(2,1)S(1)} %collective-permute-done.11.refs_0_) | copy-start | bytes 1376260
  146.1 9.8 %copy-start.13 = (bf16[2,2,224,256]{3,2,1,0:T(8,128)(2,1)}, bf16[2,2,224,256]{3,2,1,0:T(8,128)(2,1)S(1)}, u32[]{:S(2)}) copy-start(bf16[2,2,224,256]{3,2,1,0:T(8,128)(2,1)S(1)} %collective-permute-done.12.refs_1_) | copy-start | bytes 1376260
  156.7 6.5 %copy-start.21 = (bf16[2,3,224,256]{3,2,1,0:T(8,128)(2,1)S(1)}, bf16[2,3,224,256]{3,2,1,0:T(8,128)(2,1)}, u32[]{:S(2)}) copy-start(bf16[2,3,224,256]{3,2,1,0:T(8,128)(2,1)} %get-tuple-element.80.refs_0_) | copy-start | bytes 2064388
  156.7 15.1 %copy-start.15 = (bf16[2,2,224,256]{3,2,1,0:T(8,128)(2,1)S(1)}, bf16[2,2,224,256]{3,2,1,0:T(8,128)(2,1)}, u32[]{:S(2)}) copy-start(bf16[2,2,224,256]{3,2,1,0:T(8,128)(2,1)} %get-tuple-element.68.refs_16_) | copy-start | bytes 1376260
  156.7 4.0 %collective-permute-start.14 = (bf16[2,2,224,256]{3,2,1,0:T(8,128)(2,1)}, bf16[2,2,224,256]{3,2,1,0:T(8,128)(2,1)S(1)}, u32[]{:S(2)}, u32[]{:S(2)}) collective-permute-start(bf16[2,2,224,256]{3,2,1,0:T(8,128)(2,1)} %get-tuple-element.66.refs_12_), channel_id=1, source_target_pairs={{0,1},{1,0},{2,3},{3,2},{4,5},{5,4},{6,7},{7,6},{8,9},{9,8},{10,11... | collective-permute-start | bytes 1376264 | tf_op jit(solution)/shard_map/ppermute | solution.py:192
  158.7 2.3 collective-permute-start.15
  158.8 13.0 %collective-permute-start.10 = (bf16[2,224,256]{2,1,0:T(8,128)(2,1)}, bf16[2,224,256]{2,1,0:T(8,128)(2,1)S(1)}, u32[]{:S(2)}, u32[]{:S(2)}) collective-permute-start(bf16[2,224,256]{2,1,0:T(8,128)(2,1)} %get-tuple-element.62), channel_id=1, source_target_pairs={{0,1},{1,0},{2,3},{3,2},{4,5},{5,4},{6,7},{7,6},{8,9},{9,8},{10,11... | collective-permute-start | bytes 688136 | tf_op jit(solution)/shard_map/ppermute | solution.py:192
  159.2 32.1 %collective-permute-start.31 = (bf16[2,3,224,256]{3,2,1,0:T(8,128)(2,1)}, bf16[2,3,224,256]{3,2,1,0:T(8,128)(2,1)}, u32[]{:S(2)}, u32[]{:S(2)}) collective-permute-start(bf16[2,3,224,256]{3,2,1,0:T(8,128)(2,1)} %get-tuple-element.84), channel_id=1, source_target_pairs={{0,4},{1,5},{2,6},{3,7},{4,0},{5,1},{6,2},{7,3},{8,12},{9,13},{10,... | collective-permute-start | bytes 2064392 | tf_op jit(solution)/shard_map/ppermute | solution.py:192
  161.8 30.4 %collective-permute-start.33 = (bf16[2,3,224,256]{3,2,1,0:T(8,128)(2,1)}, bf16[2,3,224,256]{3,2,1,0:T(8,128)(2,1)}, u32[]{:S(2)}, u32[]{:S(2)}) collective-permute-start(bf16[2,3,224,256]{3,2,1,0:T(8,128)(2,1)} %shard_map.123), channel_id=1, source_target_pairs={{0,6},{1,7},{2,4},{3,5},{4,2},{5,3},{6,0},{7,1},{8,14},{9,15},{10,... | collective-permute-start | bytes 2064392 | tf_op jit(solution)/shard_map/ppermute | solution.py:192
  163.2 28.9 %collective-permute-start.26 = (bf16[2,3,224,256]{3,2,1,0:T(8,128)(2,1)S(1)}, bf16[2,3,224,256]{3,2,1,0:T(8,128)(2,1)S(1)}, u32[]{:S(2)}, u32[]{:S(2)}) collective-permute-start(bf16[2,3,224,256]{3,2,1,0:T(8,128)(2,1)S(1)} %copy-done.21), channel_id=1, source_target_pairs={{0,1},{1,0},{2,3},{3,2},{4,5},{5,4},{6,7},{7,6},{8,9},{9,8},{10,11... | collective-permute-start | bytes 2064392 | tf_op jit(solution)/shard_map/ppermute | solution.py:192
  169.7 22.4 %collective-permute-start.28 = (bf16[2,3,224,256]{3,2,1,0:T(8,128)(2,1)}, bf16[2,3,224,256]{3,2,1,0:T(8,128)(2,1)S(1)}, u32[]{:S(2)}, u32[]{:S(2)}) collective-permute-start(bf16[2,3,224,256]{3,2,1,0:T(8,128)(2,1)} %collective-permute-done.27.refs_2_), channel_id=1, source_target_pairs={{0,1},{1,0},{2,3},{3,2},{4,5},{5,4},{6,7},{7,6},{8,9},{9,8},{10,11... | collective-permute-start | bytes 2064392 | tf_op jit(solution)/shard_map/ppermute | solution.py:192
  171.8 2.6 %collective-permute-start.16 = (bf16[2,2,224,256]{3,2,1,0:T(8,128)(2,1)S(1)}, bf16[2,2,224,256]{3,2,1,0:T(8,128)(2,1)}, u32[]{:S(2)}, u32[]{:S(2)}) collective-permute-start(bf16[2,2,224,256]{3,2,1,0:T(8,128)(2,1)S(1)} %copy-done.15), channel_id=1, source_target_pairs={{0,1},{1,0},{2,3},{3,2},{4,5},{5,4},{6,7},{7,6},{8,9},{9,8},{10,11... | collective-permute-start | bytes 1376264 | tf_op jit(solution)/shard_map/ppermute | solution.py:192
  180.1 19.6 %collective-permute-start.18 = (bf16[2,3,224,256]{3,2,1,0:T(8,128)(2,1)}, bf16[2,3,224,256]{3,2,1,0:T(8,128)(2,1)S(1)}, u32[]{:S(2)}, u32[]{:S(2)}) collective-permute-start(bf16[2,3,224,256]{3,2,1,0:T(8,128)(2,1)} %get-tuple-element.70), channel_id=1, source_target_pairs={{0,2},{1,3},{2,0},{3,1},{4,6},{5,7},{6,4},{7,5},{8,10},{9,11},{10,... | collective-permute-start | bytes 2064392 | tf_op jit(solution)/shard_map/ppermute | solution.py:192
  191.3 4.4 %collective-permute-start.32 = (bf16[2,3,224,256]{3,2,1,0:T(8,128)(2,1)}, bf16[2,3,224,256]{3,2,1,0:T(8,128)(2,1)}, u32[]{:S(2)}, u32[]{:S(2)}) collective-permute-start(bf16[2,3,224,256]{3,2,1,0:T(8,128)(2,1)} %collective-permute-done.31.refs_4_), channel_id=1, source_target_pairs={{0,1},{1,0},{2,3},{3,2},{4,5},{5,4},{6,7},{7,6},{8,9},{9,8},{10,11... | collective-permute-start | bytes 2064392 | tf_op jit(solution)/shard_map/ppermute | solution.py:192
  192.1 4.6 %collective-permute-start.34 = (bf16[2,3,224,256]{3,2,1,0:T(8,128)(2,1)}, bf16[2,3,224,256]{3,2,1,0:T(8,128)(2,1)}, u32[]{:S(2)}, u32[]{:S(2)}) collective-permute-start(bf16[2,3,224,256]{3,2,1,0:T(8,128)(2,1)} %collective-permute-done.33.refs_6_), channel_id=1, source_target_pairs={{0,1},{1,0},{2,3},{3,2},{4,5},{5,4},{6,7},{7,6},{8,9},{9,8},{10,11... | collective-permute-start | bytes 2064392 | tf_op jit(solution)/shard_map/ppermute | solution.py:192
  193.2 31.5 %collective-permute-start.29 = (bf16[2,3,224,256]{3,2,1,0:T(8,128)(2,1)}, bf16[2,3,224,256]{3,2,1,0:T(8,128)(2,1)S(1)}, u32[]{:S(2)}, u32[]{:S(2)}) collective-permute-start(bf16[2,3,224,256]{3,2,1,0:T(8,128)(2,1)} %get-tuple-element.82), channel_id=1, source_target_pairs={{0,4},{1,5},{2,6},{3,7},{4,0},{5,1},{6,2},{7,3},{8,12},{9,13},{10,... | collective-permute-start | bytes 2064392 | tf_op jit(solution)/shard_map/ppermute | solution.py:192
  194.7 30.0 %collective-permute-start.30 = (bf16[2,3,224,256]{3,2,1,0:T(8,128)(2,1)}, bf16[2,3,224,256]{3,2,1,0:T(8,128)(2,1)S(1)}, u32[]{:S(2)}, u32[]{:S(2)}) collective-permute-start(bf16[2,3,224,256]{3,2,1,0:T(8,128)(2,1)} %get-tuple-element.83), channel_id=1, source_target_pairs={{0,6},{1,7},{2,4},{3,5},{4,2},{5,3},{6,0},{7,1},{8,14},{9,15},{10,... | collective-permute-start | bytes 2064392 | tf_op jit(solution)/shard_map/ppermute | solution.py:192
  195.6 32.0 %collective-permute-start.17 = (bf16[2,3,224,256]{3,2,1,0:T(8,128)(2,1)S(1)}, bf16[2,3,224,256]{3,2,1,0:T(8,128)(2,1)}, u32[]{:S(2)}, u32[]{:S(2)}) collective-permute-start(bf16[2,3,224,256]{3,2,1,0:T(8,128)(2,1)S(1)} %copy-done.22), channel_id=1, source_target_pairs={{0,1},{1,0},{2,3},{3,2},{4,5},{5,4},{6,7},{7,6},{8,9},{9,8},{10,11... | collective-permute-start | bytes 2064392 | tf_op jit(solution)/shard_map/ppermute | solution.py:192
  199.8 24.9 %copy-start.6 = (bf16[2,3,224,256]{3,2,1,0:T(8,128)(2,1)}, bf16[2,3,224,256]{3,2,1,0:T(8,128)(2,1)S(1)}, u32[]{:S(2)}) copy-start(bf16[2,3,224,256]{3,2,1,0:T(8,128)(2,1)S(1)} %collective-permute-done.18.refs_0_) | copy-start | bytes 2064388
  225.8 3.3 %collective-permute-start.35 = (bf16[2,3,224,256]{3,2,1,0:T(8,128)(2,1)}, bf16[2,3,224,256]{3,2,1,0:T(8,128)(2,1)S(1)}, u32[]{:S(2)}, u32[]{:S(2)}) collective-permute-start(bf16[2,3,224,256]{3,2,1,0:T(8,128)(2,1)} %get-tuple-element.89.refs_2_), channel_id=1, source_target_pairs={{0,1},{1,0},{2,3},{3,2},{4,5},{5,4},{6,7},{7,6},{8,9},{9,8},{10,11... | collective-permute-start | bytes 2064392 | tf_op jit(solution)/shard_map/ppermute | solution.py:192
  227.2 3.0 %collective-permute-start.36 = (bf16[2,3,224,256]{3,2,1,0:T(8,128)(2,1)}, bf16[2,3,224,256]{3,2,1,0:T(8,128)(2,1)S(1)}, u32[]{:S(2)}, u32[]{:S(2)}) collective-permute-start(bf16[2,3,224,256]{3,2,1,0:T(8,128)(2,1)} %get-tuple-element.90.refs_4_), channel_id=1, source_target_pairs={{0,1},{1,0},{2,3},{3,2},{4,5},{5,4},{6,7},{7,6},{8,9},{9,8},{10,11... | collective-permute-start | bytes 2064392 | tf_op jit(solution)/shard_map/ppermute | solution.py:192
  227.2 3.9 %collective-permute-start.37 = (bf16[2,3,224,256]{3,2,1,0:T(8,128)(2,1)}, bf16[2,3,224,256]{3,2,1,0:T(8,128)(2,1)S(1)}, u32[]{:S(2)}, u32[]{:S(2)}) collective-permute-start(bf16[2,3,224,256]{3,2,1,0:T(8,128)(2,1)} %get-tuple-element.91.refs_6_), channel_id=1, source_target_pairs={{0,1},{1,0},{2,3},{3,2},{4,5},{5,4},{6,7},{7,6},{8,9},{9,8},{10,11... | collective-permute-start | bytes 2064392 | tf_op jit(solution)/shard_map/ppermute | solution.py:192
  (22 other events, 25.6 us)

commit v3 on v2

v3 whole, which is shorter than its diff:
```python
import functools

import jax
import jax.numpy as jnp
from jax import lax
from jax.experimental import pallas as pl
from jax.experimental.pallas import tpu as pltpu
from jax.sharding import PartitionSpec as P

beta_one = 0.9
beta_two = 0.95
bias_one = 0.9999734386011124
bias_two = 0.994079470779666
decay_rate = 0.1
adam_eps = 1e-08

BF = jnp.bfloat16
F32 = jnp.float32
CHUNK = 16
LIMIT = 56 * 1024 * 1024
FINE = 256
SPLIT = (2, 2)
ORDER = (0, 6, 2, 4, 3, 5, 7, 1)


def adam_update(weights, first_old, second_old, gradient):
    first_new = beta_one * first_old.astype(F32) + (1.0 - beta_one) * gradient
    second_new = beta_two * second_old.astype(F32) + (1.0 - beta_two) * gradient * gradient
    scaled = first_new / bias_one / (jnp.sqrt(second_new / bias_two) + adam_eps)
    step_new = -(scaled + decay_rate * weights)
    return step_new, first_new, second_new


def quick_update(weights, first_old, second_old, gradient):
    first_new = beta_one * first_old.astype(F32) + (1.0 - beta_one) * gradient
    second_new = beta_two * second_old.astype(F32) + (1.0 - beta_two) * gradient * gradient
    unbiased = second_new * (1.0 / bias_two)
    root = unbiased * lax.rsqrt(unbiased) + adam_eps
    scaled = first_new * (-1.0 / bias_one) * pl.reciprocal(root, approx=True)
    return scaled - decay_rate * weights, first_new, second_new


def spread_kernel(group, counts, grads, acts, *refs):
    outs = refs[1:]
    slots, tok, hidden = acts.shape
    columns = grads.shape[1]
    rows = grads.shape[0] // len(outs)
    row = lax.broadcasted_iota(jnp.int32, (tok, 1), 0)
    live = [jnp.where(row < counts[s], acts[s], jnp.zeros_like(acts[s])) for s in range(slots)]
    for k, out in enumerate(outs):
        start = pl.multiple_of((group[0] ^ k) * rows, CHUNK)
        out[:rows] = grads[pl.ds(start, rows)]
        for s in range(slots):
            for b in range(hidden // columns):
                to = rows + b * slots * tok + s * tok
                out[to : to + tok] = live[s][:, b * columns : (b + 1) * columns]


def pack_kernel(items, me, params, first, second, *refs):
    at = pl.program_id(0)
    for i, (j, _) in enumerate(items):

        @pl.when(at == i)
        def _(out=refs[-2:][j]):
            out[0] = params[...].astype(BF)
            out[1] = first[...]
            out[2] = second[...]


def bundle_kernel(picks, *refs):
    out, (buffer, came, went) = refs[-4], refs[-3:]
    arrive, leave = [], []
    for i, pick in enumerate(picks):
        ref = refs[i] if pick is None else refs[i].at[pick]
        arrive.append(pltpu.make_async_copy(ref, buffer.at[i], came.at[i]))
        leave.append(pltpu.make_async_copy(buffer.at[i], out.at[i], went.at[i]))
        arrive[i].start()
    for i in range(4):
        arrive[i].wait()
        leave[i].start()
    for i in range(4):
        leave[i].wait()


def grad_kernel(n, rows, me, *refs):
    at = pl.program_id(0)
    groups = lax.axis_size("edp")
    given, outs, table = refs[:groups], refs[-1 - n : -1], refs[-1]
    columns = given[0].shape[1]
    slots, piece, hidden = outs[0].shape
    tok = columns // slots

    @pl.when(at == 0)
    def _():
        table[...] = jnp.zeros_like(table)
        for g in range(groups):
            for b in range(hidden // columns):
                for s in range(slots):
                    source = rows + (b * slots + s) * tok
                    to, column = g * columns + s * tok, s * hidden + b * columns
                    table[to : to + tok, column : column + columns] = given[g][source : source + tok]

    here = pl.ds(pl.multiple_of((me[0] ^ at) * piece, CHUNK), piece)
    left = jnp.concatenate([given[g][here] for g in range(groups)], axis=1)
    total = jnp.dot(left, table[...], preferred_element_type=F32).astype(BF)
    for k in range(n):

        @pl.when(at == k)
        def _(k=k):
            for s in range(slots):
                outs[k][s] = total[:, s * hidden : (s + 1) * hidden]


def find(n, names, places):
    for e in range(n):
        places[names[e]] = e


def update_kernel(n, me_ref, old, rep, new, *refs):
    mine, outs = refs[:3], refs[-4 - n : -4]
    state, grads = refs[3 : 2 + n], dict(zip(ORDER, refs[2 + n : 2 + 2 * n]))
    sums, placed, owner, target = refs[-4:]
    me = me_ref[0]
    find(n, old, owner)
    find(n, new, target)
    to = [target[old[me ^ k]] ^ me for k in range(n)]
    serves = [owner[rep[me ^ k]] ^ me for k in range(n)]

    def update(r, _):
        rows = pl.ds(pl.multiple_of(r * CHUNK, CHUNK), CHUNK)
        for k in range(n):
            sums[k] = grads[k][0, rows].astype(F32)
        for k in range(n):
            sums[serves[k]] = sums[serves[k]] + grads[k][1, rows].astype(F32)
        for k in range(n):
            old_state = [ref[rows] for ref in mine] if k == 0 else [state[k - 1][i, rows] for i in range(3)]
            updated = quick_update(old_state[0].astype(F32), *old_state[1:], sums[k])
            for i, array in enumerate(updated):
                placed[to[k], i] = array.astype(BF)
        for k in range(n):
            outs[k][:, rows] = placed[k]
        return 0

    lax.fori_loop(0, mine[0].shape[0] // CHUNK, update, 0)


def unpack_kernel(begin, me_ref, *refs):
    (step, first, second), (given, wide, came, went) = refs[-7:-4], refs[-4:]
    me = me_ref[0]
    count, _, piece, width = given.shape
    pieces = refs[:count]

    def place(i):
        k = ORDER[i]
        row = pl.multiple_of((me ^ k) * piece, CHUNK)
        return pl.ds(row, piece), pl.ds(begin, width)

    arrive, leave = [], []
    for i in range(count):
        arrive.append(pltpu.make_async_copy(pieces[i], given.at[i], came.at[i]))
        arrive[-1].start()
    for i in range(count):
        arrive[i].wait()
        leave.append(pltpu.make_async_copy(given.at[i, 1], first.at[place(i)], went.at[3 * i]))
        leave.append(pltpu.make_async_copy(given.at[i, 2], second.at[place(i)], went.at[3 * i + 1]))
        leave[-2].start()
        leave[-1].start()
        wide[i] = given[i, 0].astype(F32)
        leave.append(pltpu.make_async_copy(wide.at[i], step.at[place(i)], went.at[3 * i + 2]))
        leave[-1].start()
    for copy in leave:
        copy.wait()


def bundle_kernel(*refs):
    out, (buffer, came, went) = refs[-4], refs[-3:]
    arrive, leave = [], []
    count = buffer.shape[0]
    for i in range(count):
        arrive.append(pltpu.make_async_copy(refs[i].at[min(i, 1)], buffer.at[i], came.at[i]))
        leave.append(pltpu.make_async_copy(buffer.at[i], out.at[i], went.at[i]))
        arrive[i].start()
    for i in range(count):
        arrive[i].wait()
        leave[i].start()
    for i in range(count):
        leave[i].wait()


def order_kernel(*refs):
    pass


def call(kernel, prefetch, grid, in_specs, out_specs, out_shape, scratch=(), aliases={}):
    return pl.pallas_call(
        kernel,
        grid_spec=pltpu.PrefetchScalarGridSpec(
            num_scalar_prefetch=prefetch,
            grid=grid,
            in_specs=in_specs,
            out_specs=out_specs,
            scratch_shapes=scratch,
        ),
        out_shape=out_shape,
        input_output_aliases=aliases,
        compiler_params=pltpu.CompilerParams(vmem_limit_bytes=LIMIT),
    )


def swap(array, k, axis):
    return lax.ppermute(array, axis, [(i, i ^ k) for i in range(lax.axis_size(axis))])


def fast_local(
    token_acts, out_grad, counts, params, first_moment, second_moment, old_expert, replica_of, new_expert
):
    groups = lax.axis_size("edp")
    n = lax.axis_size("ep")
    model_width, columns = out_grad.shape[2:]
    slots, tok, hidden = token_acts.shape[2:]
    rows = model_width // groups
    piece = rows // n
    unit = hidden // sum(SPLIT)
    block = min(FINE, unit)
    begins = [sum(SPLIT[:p]) * unit for p in range(len(SPLIT))]
    widths = [count * unit for count in SPLIT]
    me = lax.axis_index("ep").astype(jnp.int32).reshape(1)
    group = lax.axis_index("edp").astype(jnp.int32).reshape(1)
    params, first, second = params[0], first_moment[0], second_moment[0]
    whole = lambda *shape: pl.BlockSpec(shape, lambda i, *_: (0,) * len(shape))
    shape = lambda *dims: jax.ShapeDtypeStruct(dims, BF)
    hbm = pl.BlockSpec(memory_space=pltpu.HBM)
    others = ORDER[1:]

    def order(after, *arrays):
        return call(
            order_kernel,
            0,
            (),
            [hbm] * (len(arrays) + len(after)),
            [hbm] * len(arrays),
            [jax.ShapeDtypeStruct(array.shape, array.dtype) for array in arrays],
            aliases={j: j for j in range(len(arrays))},
        )(*arrays, *after)

    def pack(ks, counts, after):
        def source(i, me):
            k = ks[-1]
            for j in range(len(ks) - 1):
                k = jnp.where(i == j, ks[j], k)
            return (me[0] ^ k, 0)

        def slot(j):
            begin = sum(counts[:j])
            return pl.BlockSpec(
                (None, 3, piece, hidden), lambda i, *_: (jnp.clip(i - begin, 0, counts[j] - 1), 0, 0, 0)
            )

        items = [(j, s) for j in range(2) for s in range(counts[j])]
        return call(
            functools.partial(pack_kernel, items),
            1,
            (len(ks),),
            [pl.BlockSpec((piece, hidden), source)] * 3 + [hbm] * len(after),
            [slot(j) for j in range(2)],
            [shape(count, 3, piece, hidden) for count in counts],
        )(me, params, first, second, *after)

    sends = pack([4, 5, 2, 3], [2, 2], [])
    came = [swap(sends[1], 2, "ep"), swap(sends[0], 4, "ep")]

    tall = rows + slots * tok * (hidden // columns)
    spread = call(
        spread_kernel,
        2,
        (1,),
        [whole(model_width, columns), whole(slots, tok, hidden), hbm],
        [whole(tall, columns)] * groups,
        [shape(tall, columns)] * groups,
    )(group, counts[0, 0], out_grad[0, 0], token_acts[0, 0], sends[0])
    given = [spread[0]] + [swap(spread[k], k, "edp") for k in range(1, groups)]
    diagonal, near = pack([6, 7, 1], [2, 1], [spread[0]])
    came.append(swap(diagonal, 6, "ep"))

    made = call(
        functools.partial(grad_kernel, n, rows),
        1,
        (n,),
        [whole(tall, columns)] * groups,
        [whole(slots, piece, hidden)] * n,
        [shape(slots, piece, hidden)] * n,
        [pltpu.VMEM((groups * columns, slots * hidden), BF)],
    )(me, *given)
    grads = {0: made[0], **{k: swap(made[k], k, "ep") for k in others}}
    came = order([made[0]], *came)
    passed = swap(
        call(
            bundle_kernel,
            0,
            (),
            [hbm] * (4),
            hbm,
            shape(4, 3, piece, hidden),
            [
                pltpu.VMEM((4, 3, piece, hidden), BF),
                pltpu.SemaphoreType.DMA((4,)),
                pltpu.SemaphoreType.DMA((4,)),
            ],
        )(near, *came),
        1,
        "ep",
    )
    state = [(passed, 0)] + [part for j in range(3) for part in ((came[j], 0), (passed, 1 + j))]

    homes = []
    for p, (begin, width) in enumerate(zip(begins, widths)):
        first_block = begin // block
        mine = pl.BlockSpec((piece, block), lambda i, me, *_, at=first_block: (me[0], at + i))
        held = lambda slot, at=first_block: pl.BlockSpec((None, 3, piece, block), lambda i, *_: (slot, 0, 0, at + i))
        part = pl.BlockSpec((slots, piece, block), lambda i, *_, at=first_block: (0, 0, at + i))
        after = homes[-1][:1] if homes else []
        homes.append(
            call(
                functools.partial(update_kernel, n),
                4,
                (width // block,),
                [mine] * 3 + [held(slot) for _, slot in state] + [part] * n + [hbm] * len(after),
                [pl.BlockSpec((3, piece, block), lambda i, *_: (0, 0, i))] * n,
                [shape(3, piece, width)] * n,
                [
                    pltpu.VMEM((n, CHUNK, block), F32),
                    pltpu.VMEM((n, 3, CHUNK, block), BF),
                    pltpu.SMEM((n,), jnp.int32),
                    pltpu.SMEM((n,), jnp.int32),
                ],
            )(
                me, old_expert, replica_of, new_expert, params, first, second,
                *[array for array, _ in state], *[grads[k] for k in ORDER], *after,
            )
        )

    result = []
    for p, (begin, width) in enumerate(zip(begins, widths)):
        pieces = {0: homes[p][0], **{k: swap(homes[p][k], k, "ep") for k in others}}
        result = call(
            functools.partial(unpack_kernel, begin),
            1,
            (),
            [hbm] * (n + len(result)),
            [hbm] * 3,
            [jax.ShapeDtypeStruct((rows, hidden), d) for d in (F32, BF, BF)],
            [
                pltpu.VMEM((n, 3, piece, width), BF),
                pltpu.VMEM((n, piece, width), F32),
                pltpu.SemaphoreType.DMA((n,)),
                pltpu.SemaphoreType.DMA((3 * n,)),
            ],
            {1 + n + j: j for j in range(len(result))},
        )(me, *[pieces[k] for k in ORDER], *result)
    step, first, second = result
    return step[None], first[None], second[None]


def plain_local(
    token_acts, out_grad, counts, params, first_moment, second_moment, old_expert, replica_of, new_expert
):
    groups = lax.axis_size("edp")
    owners = lax.axis_size("ep")
    model_width = out_grad.shape[2]
    slots, tok, hidden = token_acts.shape[2:]
    rows = model_width // groups
    piece = rows * hidden // owners
    exchange = functools.partial(lax.all_to_all, axis_name="ep", split_axis=0, concat_axis=0, tiled=True)
    row = jnp.arange(tok, dtype=jnp.int32)
    live = row[None, :] < counts[0, 0][:, None]
    acts = jnp.where(live[:, :, None], token_acts[0, 0], jnp.zeros_like(token_acts[0, 0]))
    all_acts = lax.all_gather(acts, "edp", axis=0)
    all_grads = lax.all_to_all(
        out_grad[0, 0].reshape(groups, rows, slots * tok), "edp", split_axis=0, concat_axis=0, tiled=True
    ).reshape(groups, rows, slots, tok)
    slot_grads = jnp.einsum("adst,astf->sdf", all_grads, all_acts, preferred_element_type=F32)
    pieces = lambda array: exchange(array.astype(BF).reshape(owners, piece))
    own, replica = pieces(slot_grads[0]), pieces(slot_grads[1])
    sum_matrix = (replica_of[None, :] == old_expert[:, None]).astype(BF)
    move_matrix = (old_expert[None, :] == new_expert[:, None]).astype(BF)
    total = own.astype(F32) + jnp.dot(sum_matrix, replica, preferred_element_type=F32)
    updated = adam_update(
        pieces(params[0]).astype(F32), pieces(first_moment[0]), pieces(second_moment[0]), total
    )
    result = []
    for array, kind in zip(updated, (F32, BF, BF)):
        placed = jnp.dot(move_matrix, array.astype(BF), preferred_element_type=F32)
        result.append(exchange(placed.astype(BF)).astype(kind).reshape(1, rows, hidden))
    return tuple(result)


def local(token_acts, out_grad, *others):
    groups, n = lax.axis_size("edp"), lax.axis_size("ep")
    rows, columns = out_grad.shape[2] // groups, out_grad.shape[3]
    slots, tok, hidden = token_acts.shape[2:]
    fast = n == 8 and groups & (groups - 1) == 0 and rows % (8 * CHUNK) == 0
    fast = fast and slots == 2 and columns == 128 and tok == 64 and hidden % (FINE * sum(SPLIT)) == 0
    return (fast_local if fast else plain_local)(token_acts, out_grad, *others)


def solution(mesh):
    return jax.shard_map(
        local,
        mesh=mesh,
        in_specs=(
            P("edp", "ep", None, None, None),
            P("edp", "ep", None, None),
            P("edp", "ep", None),
            P("ep", "edp", None),
            P("ep", "edp", None),
            P("ep", "edp", None),
            P(),
            P(),
            P(),
        ),
        out_specs=(P("ep", "edp", None), P("ep", "edp", None), P("ep", "edp", None)),
        check_vma=False,
    )
```

time: 237 us -> 194 us (0.82)
  waiting for transfers between devices: 147 us -> 109 us
  local copies, waits for them, and re-layouts: 11.8 us -> 6.06 us
    ppermute x38 -> x28, waiting for transfers between devices: 147 us -> 109 us  [swap(): lax.ppermute(array, axis, [(i, i ^ k) for i in range(lax.axis_size(axis))])]
    unnamed x64 -> x80, local copies, waits for them, and re-layouts: 11.8 us -> 6.06 us
    ppermute x38 -> x28, starting transfers between devices: 34.7 us -> 36.3 us  [swap(): lax.ppermute(array, axis, [(i, i ^ k) for i in range(lax.axis_size(axis))])]
  transfers between devices with their start and end apart: 38 -> 28, of which waited for: 17 -> 14; matrix products, arithmetic and copies ran while one was open for 0% -> 0% of each run, Pallas kernels for 14% -> 13%
where the time goes in v3:
time: 194 us; the launch traced here: 193 us
  waiting for transfers between devices  109 us (56%)
  Pallas kernels  40.7 us (21%)
  starting transfers between devices  36.3 us (19%)
  local copies, waits for them, and re-layouts  6.06 us (3%)
    ppermute x28, waiting for transfers between devices, swap(): lax.ppermute(array, axis, [(i, i ^ k) for i in range(lax.axis_size(axis))])  109 us
    ppermute x28, starting transfers between devices, swap(): lax.ppermute(array, axis, [(i, i ^ k) for i in range(lax.axis_size(axis))])  36.3 us
    pallas_call x2, Pallas kernels, fast_local(): call(functools.partial(update_kernel, n), 4, (width // block,), [mine] *...  11.7 us
    pallas_call x2, Pallas kernels, pack(): call(functools.partial(pack_kernel, items), 1, (len(ks),), [pl.BlockSpec(...  8.51 us
    pallas_call x1, Pallas kernels, fast_local(): call(functools.partial(grad_kernel, n, rows), 1, (n,), [whole(tall, colum...  8.22 us
    pallas_call x2, Pallas kernels, fast_local(): call(functools.partial(unpack_kernel, begin), 1, (), [hbm] * (n + len(res...  6.16 us
    unnamed x80, local copies, waits for them, and re-layouts  6.06 us
  transfers between devices with their start and end apart: 28, of which 14 were waited for; matrix products, arithmetic and copies ran while one was open for 0% of the time, Pallas kernels for 13%

profile of v3, /device:TPU:17, one launch (start us, length us, event | category | flops | bytes accessed | tf_op | source)
XLA Modules:
  0.0 193.0 jit_solution(17467537127278989414)
XLA Ops:
  0.6 4.5 %shard_map.112 = (bf16[2,3,112,1024]{3,2,1,0:T(8,128)(2,1)}, bf16[2,3,112,1024]{3,2,1,0:T(8,128)(2,1)}) custom-call(s32[1]{0:T(128)} %bitcast.me.me_ref, f32[896,1024]{1,0:T(8,128)} %bitcast.11, bf16[896,1024]{1,0:T(8,128)(2,1)} %bitcast.15, bf16[896,1024]{1,0:T(8,128)(2,1)} %bitcast.19), custom_call_target="tpu_custom_call" | custom-call | tf_op jit(solution)/shard_map/pallas_call | solution.py:260
  5.1 1.2 collective-permute-start
  6.3 1.2 collective-permute-start.1
  7.6 3.3 %shard_map.113 = (bf16[1920,128]{1,0:T(8,128)(2,1)}, bf16[1920,128]{1,0:T(8,128)(2,1)}, bf16[1920,128]{1,0:T(8,128)(2,1)}, bf16[1920,128]{1,0:T(8,128)(2,1)}) custom-call(s32[1]{0:T(128)} %bitcast.4.group, s32[2]{0:T(128)} %bitcast.28, bf16[3584,128]{1,0:T(8,128)(2,1)} %bitcast.26, bf16[2,64,1024]{2,1,0:T(8,128)(2,1)} %bitcast.27, ...), custom_call_target="tpu_custom_call" | custom-call | tf_op jit(solution)/shard_map/pallas_call | solution.py:273
  10.9 4.0 %shard_map.114 = (bf16[2,3,112,1024]{3,2,1,0:T(8,128)(2,1)}, bf16[1,3,112,1024]{3,2,1,0:T(8,128)(2,1)}) custom-call(s32[1]{0:T(128)} %bitcast.me.me_ref, f32[896,1024]{1,0:T(8,128)} %bitcast.12, bf16[896,1024]{1,0:T(8,128)(2,1)} %bitcast.16, bf16[896,1024]{1,0:T(8,128)(2,1)} %bitcast.20, bf16[1920,128]{1,0:T(8,128)(2,1)} %get-tuple-element.45.refs_0_), custom_call_target="tpu_custom_call" | custom-call | tf_op jit(solution)/shard_map/pallas_call | solution.py:260
  15.1 1.3 collective-permute-start.3
  16.5 19.0 %collective-permute-done.3.refs_1_ = bf16[1920,128]{1,0:T(8,128)(2,1)S(1)} collective-permute-done((bf16[1920,128]{1,0:T(8,128)(2,1)S(1)}, bf16[1920,128]{1,0:T(8,128)(2,1)S(1)}, u32[]{:S(2)}, u32[]{:S(2)}) %collective-permute-start.3) | collective-permute-done | bytes 491552 | tf_op jit(solution)/shard_map/ppermute | solution.py:211
  35.5 1.3 collective-permute-done.4.refs_2_
  36.8 23.2 %collective-permute-done.5.refs_3_ = bf16[1920,128]{1,0:T(8,128)(2,1)S(1)} collective-permute-done((bf16[1920,128]{1,0:T(8,128)(2,1)S(1)}, bf16[1920,128]{1,0:T(8,128)(2,1)S(1)}, u32[]{:S(2)}, u32[]{:S(2)}) %collective-permute-start.5) | collective-permute-done | bytes 491552 | tf_op jit(solution)/shard_map/ppermute | solution.py:211
  60.0 0.8 copy-done.13
  60.8 8.2 %shard_map.115 = (bf16[2,112,1024]{2,1,0:T(8,128)(2,1)}, bf16[2,112,1024]{2,1,0:T(8,128)(2,1)}, bf16[2,112,1024]{2,1,0:T(8,128)(2,1)}, bf16[2,112,1024]{2,1,0:T(...) custom-call(s32[1]{0:T(128)} %bitcast.me.me_ref, ...), custom_call_target="tpu_custom_call" | custom-call | tf_op jit(solution)/shard_map/pallas_call | solution.py:285
  69.1 1.0 copy-done.1
  70.6 0.5 copy-done.3
  71.1 2.8 %shard_map.117 = bf16[4,3,112,1024]{3,2,1,0:T(8,128)(2,1)} custom-call(bf16[1,3,112,1024]{3,2,1,0:T(8,128)(2,1)} %get-tuple-element.46.refs_0_, bf16[2,3,112,1024]{3,2,1,0:T(8,128)(2,1)} %get-tuple-element.53.refs_1_.refs_4_, bf16[2,3,112,1024]{3,2,1,0:T(8,128)(2,1)} %get-tuple-element.54.refs_2_.refs_6_, ...), custom_call_target="tpu_custom_call" | custom-call | tf_op jit(solution)/shard_map/pallas_call | solution.py:297
  73.9 1.6 collective-permute-start.6
  75.5 2.2 %collective-permute-start.7 = (bf16[2,112,1024]{2,1,0:T(8,128)(2,1)S(1)}, bf16[2,112,1024]{2,1,0:T(8,128)(2,1)S(1)}, u32[]{:S(2)}, u32[]{:S(2)}) collective-permute-start(bf16[2,112,1024]{2,1,0:T(8,128)(2,1)S(1)} %copy-done.37), channel_id=1, source_target_pairs={{0,6},{1,7},{2,4},{3,5},{4,2},{5,3},{6,0},{7,1},{8,14},{9,15},{10,... | collective-permute-start | bytes 1376264 | tf_op jit(solution)/shard_map/ppermute | solution.py:211
  78.2 2.0 %collective-permute-start.10 = (bf16[2,112,1024]{2,1,0:T(8,128)(2,1)S(1)}, bf16[2,112,1024]{2,1,0:T(8,128)(2,1)S(1)}, u32[]{:S(2)}, u32[]{:S(2)}) collective-permute-start(bf16[2,112,1024]{2,1,0:T(8,128)(2,1)S(1)} %copy-done.34), channel_id=1, source_target_pairs={{0,3},{1,2},{2,1},{3,0},{4,7},{5,6},{6,5},{7,4},{8,11},{9,10},{10,... | collective-permute-start | bytes 1376264 | tf_op jit(solution)/shard_map/ppermute | solution.py:211
  80.2 8.3 %collective-permute-done.7.refs_11_ = bf16[2,112,1024]{2,1,0:T(8,128)(2,1)S(1)} collective-permute-done((bf16[2,112,1024]{2,1,0:T(8,128)(2,1)S(1)}, bf16[2,112,1024]{2,1,0:T(8,128)(2,1)S(1)}, u32[]{:S(2)}, u32[]{:S(2)}) %collective-permute-start.7) | collective-permute-done | bytes 458784 | tf_op jit(solution)/shard_map/ppermute | solution.py:211
  88.6 2.4 %collective-permute-start.11 = (bf16[2,112,1024]{2,1,0:T(8,128)(2,1)S(1)}, bf16[2,112,1024]{2,1,0:T(8,128)(2,1)S(1)}, u32[]{:S(2)}, u32[]{:S(2)}) collective-permute-start(bf16[2,112,1024]{2,1,0:T(8,128)(2,1)S(1)} %copy-done.33), channel_id=1, source_target_pairs={{0,5},{1,4},{2,7},{3,6},{4,1},{5,0},{6,3},{7,2},{8,13},{9,12},{10,... | collective-permute-start | bytes 1376264 | tf_op jit(solution)/shard_map/ppermute | solution.py:211
  91.0 7.4 %collective-permute-done.8.refs_12_ = bf16[2,112,1024]{2,1,0:T(8,128)(2,1)S(1)} collective-permute-done((bf16[2,112,1024]{2,1,0:T(8,128)(2,1)S(1)}, bf16[2,112,1024]{2,1,0:T(8,128)(2,1)S(1)}, u32[]{:S(2)}, u32[]{:S(2)}) %collective-permute-start.8) | collective-permute-done | bytes 458784 | tf_op jit(solution)/shard_map/ppermute | solution.py:211
  98.5 2.4 %collective-permute-start.12 = (bf16[2,112,1024]{2,1,0:T(8,128)(2,1)S(1)}, bf16[2,112,1024]{2,1,0:T(8,128)(2,1)S(1)}, u32[]{:S(2)}, u32[]{:S(2)}) collective-permute-start(bf16[2,112,1024]{2,1,0:T(8,128)(2,1)S(1)} %copy-done.32), channel_id=1, source_target_pairs={{0,7},{1,6},{2,5},{3,4},{4,3},{5,2},{6,1},{7,0},{8,15},{9,14},{10,... | collective-permute-start | bytes 1376264 | tf_op jit(solution)/shard_map/ppermute | solution.py:211
  100.9 8.3 %collective-permute-done.10.refs_14_ = bf16[2,112,1024]{2,1,0:T(8,128)(2,1)S(1)} collective-permute-done((bf16[2,112,1024]{2,1,0:T(8,128)(2,1)S(1)}, bf16[2,112,1024]{2,1,0:T(8,128)(2,1)S(1)}, u32[]{:S(2)}, u32[]{:S(2)}) %collective-permute-start.10) | collective-permute-done | bytes 458784 | tf_op jit(solution)/shard_map/ppermute | solution.py:211
  109.2 9.0 %collective-permute-done.12.refs_16_ = bf16[2,112,1024]{2,1,0:T(8,128)(2,1)S(1)} collective-permute-done((bf16[2,112,1024]{2,1,0:T(8,128)(2,1)S(1)}, bf16[2,112,1024]{2,1,0:T(8,128)(2,1)S(1)}, u32[]{:S(2)}, u32[]{:S(2)}) %collective-permute-start.12) | collective-permute-done | bytes 458784 | tf_op jit(solution)/shard_map/ppermute | solution.py:211
  118.3 0.7 copy-done.9
  119.2 1.5 copy-done
  120.7 5.8 %shard_map.118 = (bf16[3,112,512]{2,1,0:T(8,128)(2,1)}, bf16[3,112,512]{2,1,0:T(8,128)(2,1)}, bf16[3,112,512]{2,1,0:T(8,128)(2,1)}, bf16[3,112,512]{2,1,0:T(8,12...) custom-call(s32[1]{0:T(128)} %bitcast.me.me_ref, ...), custom_call_target="tpu_custom_call" | custom-call | tf_op jit(solution)/shard_map/pallas_call | solution.py:323
  126.5 2.2 %collective-permute-start.21 = (bf16[3,112,512]{2,1,0:T(8,128)(2,1)}, bf16[3,112,512]{2,1,0:T(8,128)(2,1)S(1)}, u32[]{:S(2)}, u32[]{:S(2)}) collective-permute-start(bf16[3,112,512]{2,1,0:T(8,128)(2,1)} %get-tuple-element.72), channel_id=1, source_target_pairs={{0,6},{1,7},{2,4},{3,5},{4,2},{5,3},{6,0},{7,1},{8,14},{9,15},{10,... | collective-permute-start | bytes 1032200 | tf_op jit(solution)/shard_map/ppermute | solution.py:211
  129.2 2.2 %collective-permute-start.24 = (bf16[3,112,512]{2,1,0:T(8,128)(2,1)}, bf16[3,112,512]{2,1,0:T(8,128)(2,1)S(1)}, u32[]{:S(2)}, u32[]{:S(2)}) collective-permute-start(bf16[3,112,512]{2,1,0:T(8,128)(2,1)} %get-tuple-element.75), channel_id=1, source_target_pairs={{0,3},{1,2},{2,1},{3,0},{4,7},{5,6},{6,5},{7,4},{8,11},{9,10},{10,... | collective-permute-start | bytes 1032200 | tf_op jit(solution)/shard_map/ppermute | solution.py:211
  131.4 0.5 collective-permute-start.25
  131.9 5.9 %shard_map.119 = (bf16[3,112,512]{2,1,0:T(8,128)(2,1)}, bf16[3,112,512]{2,1,0:T(8,128)(2,1)}, bf16[3,112,512]{2,1,0:T(8,128)(2,1)}, bf16[3,112,512]{2,1,0:T(8,12...) custom-call(s32[1]{0:T(128)} %bitcast.me.me_ref, ...), custom_call_target="tpu_custom_call" | custom-call | tf_op jit(solution)/shard_map/pallas_call | solution.py:323
  137.9 3.0 %collective-permute-start.26 = (bf16[3,112,512]{2,1,0:T(8,128)(2,1)S(1)}, bf16[3,112,512]{2,1,0:T(8,128)(2,1)S(1)}, u32[]{:S(2)}, u32[]{:S(2)}) collective-permute-start(bf16[3,112,512]{2,1,0:T(8,128)(2,1)S(1)} %copy-done.39), channel_id=1, source_target_pairs={{0,7},{1,6},{2,5},{3,4},{4,3},{5,2},{6,1},{7,0},{8,15},{9,14},{10,... | collective-permute-start | bytes 1032200 | tf_op jit(solution)/shard_map/ppermute | solution.py:211
  140.9 3.6 %collective-permute-done.22.refs_2_ = bf16[3,112,512]{2,1,0:T(8,128)(2,1)S(1)} collective-permute-done((bf16[3,112,512]{2,1,0:T(8,128)(2,1)}, bf16[3,112,512]{2,1,0:T(8,128)(2,1)S(1)}, u32[]{:S(2)}, u32[]{:S(2)}) %collective-permute-start.22) | collective-permute-done | bytes 344096 | tf_op jit(solution)/shard_map/ppermute | solution.py:211
  144.5 1.8 collective-permute-start.27
  146.3 1.2 collective-permute-start.14
  147.5 5.8 %collective-permute-done.24.refs_4_ = bf16[3,112,512]{2,1,0:T(8,128)(2,1)S(1)} collective-permute-done((bf16[3,112,512]{2,1,0:T(8,128)(2,1)}, bf16[3,112,512]{2,1,0:T(8,128)(2,1)S(1)}, u32[]{:S(2)}, u32[]{:S(2)}) %collective-permute-start.24) | collective-permute-done | bytes 344096 | tf_op jit(solution)/shard_map/ppermute | solution.py:211
  153.3 1.1 collective-permute-start.15
  154.7 5.6 %collective-permute-done.26.refs_6_ = bf16[3,112,512]{2,1,0:T(8,128)(2,1)S(1)} collective-permute-done((bf16[3,112,512]{2,1,0:T(8,128)(2,1)S(1)}, bf16[3,112,512]{2,1,0:T(8,128)(2,1)S(1)}, u32[]{:S(2)}, u32[]{:S(2)}) %collective-permute-start.26) | collective-permute-done | bytes 344096 | tf_op jit(solution)/shard_map/ppermute | solution.py:211
  160.3 0.5 collective-permute-start.17
  160.8 2.3 %collective-permute-start.18 = (bf16[3,112,512]{2,1,0:T(8,128)(2,1)}, bf16[3,112,512]{2,1,0:T(8,128)(2,1)S(1)}, u32[]{:S(2)}, u32[]{:S(2)}) collective-permute-start(bf16[3,112,512]{2,1,0:T(8,128)(2,1)} %get-tuple-element.69), channel_id=1, source_target_pairs={{0,5},{1,4},{2,7},{3,6},{4,1},{5,0},{6,3},{7,2},{8,13},{9,12},{10,... | collective-permute-start | bytes 1032200 | tf_op jit(solution)/shard_map/ppermute | solution.py:211
  163.1 3.6 %collective-permute-done.14.refs_1_ = bf16[3,112,512]{2,1,0:T(8,128)(2,1)S(1)} collective-permute-done((bf16[3,112,512]{2,1,0:T(8,128)(2,1)}, bf16[3,112,512]{2,1,0:T(8,128)(2,1)S(1)}, u32[]{:S(2)}, u32[]{:S(2)}) %collective-permute-start.14) | collective-permute-done | bytes 344096 | tf_op jit(solution)/shard_map/ppermute | solution.py:211
  166.7 3.7 %collective-permute-start.19 = (bf16[3,112,512]{2,1,0:T(8,128)(2,1)}, bf16[3,112,512]{2,1,0:T(8,128)(2,1)S(1)}, u32[]{:S(2)}, u32[]{:S(2)}) collective-permute-start(bf16[3,112,512]{2,1,0:T(8,128)(2,1)} %get-tuple-element.70), channel_id=1, source_target_pairs={{0,7},{1,6},{2,5},{3,4},{4,3},{5,2},{6,1},{7,0},{8,15},{9,14},{10,... | collective-permute-start | bytes 1032200 | tf_op jit(solution)/shard_map/ppermute | solution.py:211
  170.4 3.6 %collective-permute-done.15.refs_2_ = bf16[3,112,512]{2,1,0:T(8,128)(2,1)S(1)} collective-permute-done((bf16[3,112,512]{2,1,0:T(8,128)(2,1)}, bf16[3,112,512]{2,1,0:T(8,128)(2,1)S(1)}, u32[]{:S(2)}, u32[]{:S(2)}) %collective-permute-start.15) | collective-permute-done | bytes 344096 | tf_op jit(solution)/shard_map/ppermute | solution.py:211
  174.0 1.8 collective-permute-start.20
  175.9 3.1 %shard_map.120 = (f32[896,1024]{1,0:T(8,128)}, bf16[896,1024]{1,0:T(8,128)(2,1)}, bf16[896,1024]{1,0:T(8,128)(2,1)}) custom-call(s32[1]{0:T(128)} %bitcast.me.me_ref, bf16[3,112,512]{2,1,0:T(8,128)(2,1)} %get-tuple-element.63.refs_18_.refs_0_, bf16[3,112,512]{2,1,0:T(8,128)(2,1)} %copy-done.21, bf16[3,112,512]{2,1,0:T(8,128)(2,1)} %copy-done.22, ...), custom_call_target="tpu_custom_call" | custom-call | tf_op jit(solution)/shard_map/pallas_call | solution.py:345
  179.0 3.8 %collective-permute-done.17.refs_4_ = bf16[3,112,512]{2,1,0:T(8,128)(2,1)S(1)} collective-permute-done((bf16[3,112,512]{2,1,0:T(8,128)(2,1)}, bf16[3,112,512]{2,1,0:T(8,128)(2,1)S(1)}, u32[]{:S(2)}, u32[]{:S(2)}) %collective-permute-start.17) | collective-permute-done | bytes 344096 | tf_op jit(solution)/shard_map/ppermute | solution.py:211
  182.8 6.3 %collective-permute-done.19.refs_6_ = bf16[3,112,512]{2,1,0:T(8,128)(2,1)S(1)} collective-permute-done((bf16[3,112,512]{2,1,0:T(8,128)(2,1)}, bf16[3,112,512]{2,1,0:T(8,128)(2,1)S(1)}, u32[]{:S(2)}, u32[]{:S(2)}) %collective-permute-start.19) | collective-permute-done | bytes 344096 | tf_op jit(solution)/shard_map/ppermute | solution.py:211
  189.2 0.7 copy-done.19
  190.0 3.1 %shard_map.121 = (f32[896,1024]{1,0:T(8,128)}, bf16[896,1024]{1,0:T(8,128)(2,1)}, bf16[896,1024]{1,0:T(8,128)(2,1)}) custom-call(s32[1]{0:T(128)} %bitcast.me.me_ref, bf16[3,112,512]{2,1,0:T(8,128)(2,1)} %get-tuple-element.64.refs_0_, bf16[3,112,512]{2,1,0:T(8,128)(2,1)} %copy-done.14, ...), custom_call_target="tpu_custom_call", output_to_operand_aliasing={{0}: (9, {}), {1}: (10, {}), {2}: (11, {})} | custom-call | tf_op jit(solution)/shard_map/pallas_call | solution.py:345
  (98 shorter events, 2.4 us)
Async XLA Ops:
  5.1 63.9 %collective-permute-start = (bf16[2,3,112,1024]{3,2,1,0:T(8,128)(2,1)}, bf16[2,3,112,1024]{3,2,1,0:T(8,128)(2,1)S(1)}, u32[]{:S(2)}, u32[]{:S(2)}) collective-permute-start(bf16[2,3,112,1024]{3,2,1,0:T(8,128)(2,1)} %get-tuple-element.47), channel_id=1, source_target_pairs={{0,2},{1,3},{2,0},{3,1},{4,6},{5,7},{6,4},{7,5},{8,10},{9,11},{10,... | collective-permute-start | bytes 4128776 | tf_op jit(solution)/shard_map/ppermute | solution.py:211
  6.3 62.7 %collective-permute-start.1 = (bf16[2,3,112,1024]{3,2,1,0:T(8,128)(2,1)}, bf16[2,3,112,1024]{3,2,1,0:T(8,128)(2,1)S(1)}, u32[]{:S(2)}, u32[]{:S(2)}) collective-permute-start(bf16[2,3,112,1024]{3,2,1,0:T(8,128)(2,1)} %get-tuple-element.44.refs_0_), channel_id=1, source_target_pairs={{0,4},{1,5},{2,6},{3,7},{4,0},{5,1},{6,2},{7,3},{8,12},{9,13},{10,... | collective-permute-start | bytes 4128776 | tf_op jit(solution)/shard_map/ppermute | solution.py:211
  10.9 24.6 %copy-start.28 = (bf16[1920,128]{1,0:T(8,128)(2,1)S(1)}, bf16[1920,128]{1,0:T(8,128)(2,1)}, u32[]{:S(2)}) copy-start(bf16[1920,128]{1,0:T(8,128)(2,1)} %get-tuple-element.51) | copy-start | bytes 1474564
  14.9 54.2 %collective-permute-start.2 = (bf16[2,3,112,1024]{3,2,1,0:T(8,128)(2,1)}, bf16[2,3,112,1024]{3,2,1,0:T(8,128)(2,1)S(1)}, u32[]{:S(2)}, u32[]{:S(2)}) collective-permute-start(bf16[2,3,112,1024]{3,2,1,0:T(8,128)(2,1)} %get-tuple-element.48), channel_id=1, source_target_pairs={{0,6},{1,7},{2,4},{3,5},{4,2},{5,3},{6,0},{7,1},{8,14},{9,15},{10,... | collective-permute-start | bytes 4128776 | tf_op jit(solution)/shard_map/ppermute | solution.py:211
  15.1 20.4 %collective-permute-start.3 = (bf16[1920,128]{1,0:T(8,128)(2,1)S(1)}, bf16[1920,128]{1,0:T(8,128)(2,1)S(1)}, u32[]{:S(2)}, u32[]{:S(2)}) collective-permute-start(bf16[1920,128]{1,0:T(8,128)(2,1)S(1)} %copy-done.30), channel_id=1, source_target_pairs={{0,8},{8,0},{16,24},{24,16},{1,9},{9,1},{17,25},{25,17},{2,10},{10... | collective-permute-start | bytes 1474568 | tf_op jit(solution)/shard_map/ppermute | solution.py:211
  16.4 20.4 %collective-permute-start.4 = (bf16[1920,128]{1,0:T(8,128)(2,1)S(1)}, bf16[1920,128]{1,0:T(8,128)(2,1)S(1)}, u32[]{:S(2)}, u32[]{:S(2)}) collective-permute-start(bf16[1920,128]{1,0:T(8,128)(2,1)S(1)} %copy-done.29), channel_id=1, source_target_pairs={{0,16},{8,24},{16,0},{24,8},{1,17},{9,25},{17,1},{25,9},{2,18},{10... | collective-permute-start | bytes 1474568 | tf_op jit(solution)/shard_map/ppermute | solution.py:211
  35.5 24.5 %copy-start.11 = (bf16[1920,128]{1,0:T(8,128)(2,1)}, bf16[1920,128]{1,0:T(8,128)(2,1)S(1)}, u32[]{:S(2)}) copy-start(bf16[1920,128]{1,0:T(8,128)(2,1)S(1)} %collective-permute-done.3.refs_1_) | copy-start | bytes 1474564
  35.5 24.5 %collective-permute-start.5 = (bf16[1920,128]{1,0:T(8,128)(2,1)S(1)}, bf16[1920,128]{1,0:T(8,128)(2,1)S(1)}, u32[]{:S(2)}, u32[]{:S(2)}) collective-permute-start(bf16[1920,128]{1,0:T(8,128)(2,1)S(1)} %copy-done.28), channel_id=1, source_target_pairs={{0,24},{8,16},{16,8},{24,0},{1,25},{9,17},{17,9},{25,1},{2,26},{10... | collective-permute-start | bytes 1474568 | tf_op jit(solution)/shard_map/ppermute | solution.py:211
  36.8 23.2 %copy-start.12 = (bf16[1920,128]{1,0:T(8,128)(2,1)}, bf16[1920,128]{1,0:T(8,128)(2,1)S(1)}, u32[]{:S(2)}) copy-start(bf16[1920,128]{1,0:T(8,128)(2,1)S(1)} %collective-permute-done.4.refs_2_) | copy-start | bytes 1474564
  71.0 17.5 %copy-start.33 = (bf16[2,112,1024]{2,1,0:T(8,128)(2,1)S(1)}, bf16[2,112,1024]{2,1,0:T(8,128)(2,1)}, u32[]{:S(2)}) copy-start(bf16[2,112,1024]{2,1,0:T(8,128)(2,1)} %get-tuple-element.60) | copy-start | bytes 1376260
  71.0 27.4 %copy-start.32 = (bf16[2,112,1024]{2,1,0:T(8,128)(2,1)S(1)}, bf16[2,112,1024]{2,1,0:T(8,128)(2,1)}, u32[]{:S(2)}) copy-start(bf16[2,112,1024]{2,1,0:T(8,128)(2,1)} %get-tuple-element.61) | copy-start | bytes 1376260
  71.0 29.8 %copy-start.31 = (bf16[2,112,1024]{2,1,0:T(8,128)(2,1)S(1)}, bf16[2,112,1024]{2,1,0:T(8,128)(2,1)}, u32[]{:S(2)}) copy-start(bf16[2,112,1024]{2,1,0:T(8,128)(2,1)} %get-tuple-element.62) | copy-start | bytes 1376260
  73.9 44.3 %collective-permute-start.6 = (bf16[4,3,112,1024]{3,2,1,0:T(8,128)(2,1)}, bf16[4,3,112,1024]{3,2,1,0:T(8,128)(2,1)S(1)}, u32[]{:S(2)}, u32[]{:S(2)}) collective-permute-start(bf16[4,3,112,1024]{3,2,1,0:T(8,128)(2,1)} %shard_map.117), channel_id=1, source_target_pairs={{0,1},{1,0},{2,3},{3,2},{4,5},{5,4},{6,7},{7,6},{8,9},{9,8},{10,11... | collective-permute-start | bytes 8257544 | tf_op jit(solution)/shard_map/ppermute | solution.py:211
  75.5 13.0 %collective-permute-start.7 = (bf16[2,112,1024]{2,1,0:T(8,128)(2,1)S(1)}, bf16[2,112,1024]{2,1,0:T(8,128)(2,1)S(1)}, u32[]{:S(2)}, u32[]{:S(2)}) collective-permute-start(bf16[2,112,1024]{2,1,0:T(8,128)(2,1)S(1)} %copy-done.37), channel_id=1, source_target_pairs={{0,6},{1,7},{2,4},{3,5},{4,2},{5,3},{6,0},{7,1},{8,14},{9,15},{10,... | collective-permute-start | bytes 1376264 | tf_op jit(solution)/shard_map/ppermute | solution.py:211
  77.7 20.7 %collective-permute-start.8 = (bf16[2,112,1024]{2,1,0:T(8,128)(2,1)S(1)}, bf16[2,112,1024]{2,1,0:T(8,128)(2,1)S(1)}, u32[]{:S(2)}, u32[]{:S(2)}) collective-permute-start(bf16[2,112,1024]{2,1,0:T(8,128)(2,1)S(1)} %copy-done.36), channel_id=1, source_target_pairs={{0,2},{1,3},{2,0},{3,1},{4,6},{5,7},{6,4},{7,5},{8,10},{9,11},{10,... | collective-permute-start | bytes 1376264 | tf_op jit(solution)/shard_map/ppermute | solution.py:211
  78.0 22.8 %collective-permute-start.9 = (bf16[2,112,1024]{2,1,0:T(8,128)(2,1)S(1)}, bf16[2,112,1024]{2,1,0:T(8,128)(2,1)S(1)}, u32[]{:S(2)}, u32[]{:S(2)}) collective-permute-start(bf16[2,112,1024]{2,1,0:T(8,128)(2,1)S(1)} %copy-done.35), channel_id=1, source_target_pairs={{0,4},{1,5},{2,6},{3,7},{4,0},{5,1},{6,2},{7,3},{8,12},{9,13},{10,... | collective-permute-start | bytes 1376264 | tf_op jit(solution)/shard_map/ppermute | solution.py:211
  78.2 31.0 %collective-permute-start.10 = (bf16[2,112,1024]{2,1,0:T(8,128)(2,1)S(1)}, bf16[2,112,1024]{2,1,0:T(8,128)(2,1)S(1)}, u32[]{:S(2)}, u32[]{:S(2)}) collective-permute-start(bf16[2,112,1024]{2,1,0:T(8,128)(2,1)S(1)} %copy-done.34), channel_id=1, source_target_pairs={{0,3},{1,2},{2,1},{3,0},{4,7},{5,6},{6,5},{7,4},{8,11},{9,10},{10,... | collective-permute-start | bytes 1376264 | tf_op jit(solution)/shard_map/ppermute | solution.py:211
  88.6 29.7 %copy-start.4 = (bf16[2,112,1024]{2,1,0:T(8,128)(2,1)}, bf16[2,112,1024]{2,1,0:T(8,128)(2,1)S(1)}, u32[]{:S(2)}) copy-start(bf16[2,112,1024]{2,1,0:T(8,128)(2,1)S(1)} %collective-permute-done.7.refs_11_) | copy-start | bytes 1376260
  88.6 20.6 %collective-permute-start.11 = (bf16[2,112,1024]{2,1,0:T(8,128)(2,1)S(1)}, bf16[2,112,1024]{2,1,0:T(8,128)(2,1)S(1)}, u32[]{:S(2)}, u32[]{:S(2)}) collective-permute-start(bf16[2,112,1024]{2,1,0:T(8,128)(2,1)S(1)} %copy-done.33), channel_id=1, source_target_pairs={{0,5},{1,4},{2,7},{3,6},{4,1},{5,0},{6,3},{7,2},{8,13},{9,12},{10,... | collective-permute-start | bytes 1376264 | tf_op jit(solution)/shard_map/ppermute | solution.py:211
  98.5 19.8 %copy-start.5 = (bf16[2,112,1024]{2,1,0:T(8,128)(2,1)}, bf16[2,112,1024]{2,1,0:T(8,128)(2,1)S(1)}, u32[]{:S(2)}) copy-start(bf16[2,112,1024]{2,1,0:T(8,128)(2,1)S(1)} %collective-permute-done.8.refs_12_) | copy-start | bytes 1376260
  98.5 19.8 %collective-permute-start.12 = (bf16[2,112,1024]{2,1,0:T(8,128)(2,1)S(1)}, bf16[2,112,1024]{2,1,0:T(8,128)(2,1)S(1)}, u32[]{:S(2)}, u32[]{:S(2)}) collective-permute-start(bf16[2,112,1024]{2,1,0:T(8,128)(2,1)S(1)} %copy-done.32), channel_id=1, source_target_pairs={{0,7},{1,6},{2,5},{3,4},{4,3},{5,2},{6,1},{7,0},{8,15},{9,14},{10,... | collective-permute-start | bytes 1376264 | tf_op jit(solution)/shard_map/ppermute | solution.py:211
  100.8 17.4 %copy-start.6 = (bf16[2,112,1024]{2,1,0:T(8,128)(2,1)}, bf16[2,112,1024]{2,1,0:T(8,128)(2,1)S(1)}, u32[]{:S(2)}) copy-start(bf16[2,112,1024]{2,1,0:T(8,128)(2,1)S(1)} %collective-permute-done.9.refs_13_) | copy-start | bytes 1376260
  100.8 17.4 %collective-permute-start.13 = (bf16[2,112,1024]{2,1,0:T(8,128)(2,1)S(1)}, bf16[2,112,1024]{2,1,0:T(8,128)(2,1)S(1)}, u32[]{:S(2)}, u32[]{:S(2)}) collective-permute-start(bf16[2,112,1024]{2,1,0:T(8,128)(2,1)S(1)} %copy-done.31), channel_id=1, source_target_pairs={{0,1},{1,0},{2,3},{3,2},{4,5},{5,4},{6,7},{7,6},{8,9},{9,8},{10,11... | collective-permute-start | bytes 1376264 | tf_op jit(solution)/shard_map/ppermute | solution.py:211
  126.5 11.4 %collective-permute-start.21 = (bf16[3,112,512]{2,1,0:T(8,128)(2,1)}, bf16[3,112,512]{2,1,0:T(8,128)(2,1)S(1)}, u32[]{:S(2)}, u32[]{:S(2)}) collective-permute-start(bf16[3,112,512]{2,1,0:T(8,128)(2,1)} %get-tuple-element.72), channel_id=1, source_target_pairs={{0,6},{1,7},{2,4},{3,5},{4,2},{5,3},{6,0},{7,1},{8,14},{9,15},{10,... | collective-permute-start | bytes 1032200 | tf_op jit(solution)/shard_map/ppermute | solution.py:211
  128.7 15.8 %collective-permute-start.22 = (bf16[3,112,512]{2,1,0:T(8,128)(2,1)}, bf16[3,112,512]{2,1,0:T(8,128)(2,1)S(1)}, u32[]{:S(2)}, u32[]{:S(2)}) collective-permute-start(bf16[3,112,512]{2,1,0:T(8,128)(2,1)} %get-tuple-element.73), channel_id=1, source_target_pairs={{0,2},{1,3},{2,0},{3,1},{4,6},{5,7},{6,4},{7,5},{8,10},{9,11},{10,... | collective-permute-start | bytes 1032200 | tf_op jit(solution)/shard_map/ppermute | solution.py:211
  129.0 17.3 %collective-permute-start.23 = (bf16[3,112,512]{2,1,0:T(8,128)(2,1)}, bf16[3,112,512]{2,1,0:T(8,128)(2,1)S(1)}, u32[]{:S(2)}, u32[]{:S(2)}) collective-permute-start(bf16[3,112,512]{2,1,0:T(8,128)(2,1)} %get-tuple-element.74), channel_id=1, source_target_pairs={{0,4},{1,5},{2,6},{3,7},{4,0},{5,1},{6,2},{7,3},{8,12},{9,13},{10,... | collective-permute-start | bytes 1032200 | tf_op jit(solution)/shard_map/ppermute | solution.py:211
  129.2 24.1 %collective-permute-start.24 = (bf16[3,112,512]{2,1,0:T(8,128)(2,1)}, bf16[3,112,512]{2,1,0:T(8,128)(2,1)S(1)}, u32[]{:S(2)}, u32[]{:S(2)}) collective-permute-start(bf16[3,112,512]{2,1,0:T(8,128)(2,1)} %get-tuple-element.75), channel_id=1, source_target_pairs={{0,3},{1,2},{2,1},{3,0},{4,7},{5,6},{6,5},{7,4},{8,11},{9,10},{10,... | collective-permute-start | bytes 1032200 | tf_op jit(solution)/shard_map/ppermute | solution.py:211
  131.4 23.0 %collective-permute-start.25 = (bf16[3,112,512]{2,1,0:T(8,128)(2,1)}, bf16[3,112,512]{2,1,0:T(8,128)(2,1)S(1)}, u32[]{:S(2)}, u32[]{:S(2)}) collective-permute-start(bf16[3,112,512]{2,1,0:T(8,128)(2,1)} %get-tuple-element.76), channel_id=1, source_target_pairs={{0,5},{1,4},{2,7},{3,6},{4,1},{5,0},{6,3},{7,2},{8,13},{9,12},{10,... | collective-permute-start | bytes 1032200 | tf_op jit(solution)/shard_map/ppermute | solution.py:211
  131.9 12.6 %copy-start.38 = (bf16[3,112,512]{2,1,0:T(8,128)(2,1)S(1)}, bf16[3,112,512]{2,1,0:T(8,128)(2,1)}, u32[]{:S(2)}) copy-start(bf16[3,112,512]{2,1,0:T(8,128)(2,1)} %get-tuple-element.78) | copy-start | bytes 1032196
  137.9 38.0 %copy-start.21 = (bf16[3,112,512]{2,1,0:T(8,128)(2,1)}, bf16[3,112,512]{2,1,0:T(8,128)(2,1)S(1)}, u32[]{:S(2)}) copy-start(bf16[3,112,512]{2,1,0:T(8,128)(2,1)S(1)} %collective-permute-done.21.refs_1_) | copy-start | bytes 1032196
  137.9 22.4 %collective-permute-start.26 = (bf16[3,112,512]{2,1,0:T(8,128)(2,1)S(1)}, bf16[3,112,512]{2,1,0:T(8,128)(2,1)S(1)}, u32[]{:S(2)}, u32[]{:S(2)}) collective-permute-start(bf16[3,112,512]{2,1,0:T(8,128)(2,1)S(1)} %copy-done.39), channel_id=1, source_target_pairs={{0,7},{1,6},{2,5},{3,4},{4,3},{5,2},{6,1},{7,0},{8,15},{9,14},{10,... | collective-permute-start | bytes 1032200 | tf_op jit(solution)/shard_map/ppermute | solution.py:211
  144.5 31.3 %copy-start.22 = (bf16[3,112,512]{2,1,0:T(8,128)(2,1)}, bf16[3,112,512]{2,1,0:T(8,128)(2,1)S(1)}, u32[]{:S(2)}) copy-start(bf16[3,112,512]{2,1,0:T(8,128)(2,1)S(1)} %collective-permute-done.22.refs_2_) | copy-start | bytes 1032196
  144.5 16.3 %collective-permute-start.27 = (bf16[3,112,512]{2,1,0:T(8,128)(2,1)S(1)}, bf16[3,112,512]{2,1,0:T(8,128)(2,1)S(1)}, u32[]{:S(2)}, u32[]{:S(2)}) collective-permute-start(bf16[3,112,512]{2,1,0:T(8,128)(2,1)S(1)} %copy-done.38), channel_id=1, source_target_pairs={{0,1},{1,0},{2,3},{3,2},{4,5},{5,4},{6,7},{7,6},{8,9},{9,8},{10,11... | collective-permute-start | bytes 1032200 | tf_op jit(solution)/shard_map/ppermute | solution.py:211
  146.3 29.5 %copy-start.23 = (bf16[3,112,512]{2,1,0:T(8,128)(2,1)}, bf16[3,112,512]{2,1,0:T(8,128)(2,1)S(1)}, u32[]{:S(2)}) copy-start(bf16[3,112,512]{2,1,0:T(8,128)(2,1)S(1)} %collective-permute-done.23.refs_3_) | copy-start | bytes 1032196
  146.3 20.4 %collective-permute-start.14 = (bf16[3,112,512]{2,1,0:T(8,128)(2,1)}, bf16[3,112,512]{2,1,0:T(8,128)(2,1)S(1)}, u32[]{:S(2)}, u32[]{:S(2)}) collective-permute-start(bf16[3,112,512]{2,1,0:T(8,128)(2,1)} %get-tuple-element.65), channel_id=1, source_target_pairs={{0,6},{1,7},{2,4},{3,5},{4,2},{5,3},{6,0},{7,1},{8,14},{9,15},{10,... | collective-permute-start | bytes 1032200 | tf_op jit(solution)/shard_map/ppermute | solution.py:211
  153.3 22.6 %copy-start.24 = (bf16[3,112,512]{2,1,0:T(8,128)(2,1)}, bf16[3,112,512]{2,1,0:T(8,128)(2,1)S(1)}, u32[]{:S(2)}) copy-start(bf16[3,112,512]{2,1,0:T(8,128)(2,1)S(1)} %collective-permute-done.24.refs_4_) | copy-start | bytes 1032196
  153.3 20.8 %collective-permute-start.15 = (bf16[3,112,512]{2,1,0:T(8,128)(2,1)}, bf16[3,112,512]{2,1,0:T(8,128)(2,1)S(1)}, u32[]{:S(2)}, u32[]{:S(2)}) collective-permute-start(bf16[3,112,512]{2,1,0:T(8,128)(2,1)} %get-tuple-element.66), channel_id=1, source_target_pairs={{0,2},{1,3},{2,0},{3,1},{4,6},{5,7},{6,4},{7,5},{8,10},{9,11},{10,... | collective-permute-start | bytes 1032200 | tf_op jit(solution)/shard_map/ppermute | solution.py:211
  154.4 21.4 %copy-start.25 = (bf16[3,112,512]{2,1,0:T(8,128)(2,1)}, bf16[3,112,512]{2,1,0:T(8,128)(2,1)S(1)}, u32[]{:S(2)}) copy-start(bf16[3,112,512]{2,1,0:T(8,128)(2,1)S(1)} %collective-permute-done.25.refs_5_) | copy-start | bytes 1032196
  154.4 24.5 %collective-permute-start.16 = (bf16[3,112,512]{2,1,0:T(8,128)(2,1)}, bf16[3,112,512]{2,1,0:T(8,128)(2,1)S(1)}, u32[]{:S(2)}, u32[]{:S(2)}) collective-permute-start(bf16[3,112,512]{2,1,0:T(8,128)(2,1)} %get-tuple-element.67), channel_id=1, source_target_pairs={{0,4},{1,5},{2,6},{3,7},{4,0},{5,1},{6,2},{7,3},{8,12},{9,13},{10,... | collective-permute-start | bytes 1032200 | tf_op jit(solution)/shard_map/ppermute | solution.py:211
  160.3 15.5 %copy-start.26 = (bf16[3,112,512]{2,1,0:T(8,128)(2,1)}, bf16[3,112,512]{2,1,0:T(8,128)(2,1)S(1)}, u32[]{:S(2)}) copy-start(bf16[3,112,512]{2,1,0:T(8,128)(2,1)S(1)} %collective-permute-done.26.refs_6_) | copy-start | bytes 1032196
  160.3 22.5 %collective-permute-start.17 = (bf16[3,112,512]{2,1,0:T(8,128)(2,1)}, bf16[3,112,512]{2,1,0:T(8,128)(2,1)S(1)}, u32[]{:S(2)}, u32[]{:S(2)}) collective-permute-start(bf16[3,112,512]{2,1,0:T(8,128)(2,1)} %get-tuple-element.68), channel_id=1, source_target_pairs={{0,3},{1,2},{2,1},{3,0},{4,7},{5,6},{6,5},{7,4},{8,11},{9,10},{10,... | collective-permute-start | bytes 1032200 | tf_op jit(solution)/shard_map/ppermute | solution.py:211
  160.8 15.1 %copy-start.27 = (bf16[3,112,512]{2,1,0:T(8,128)(2,1)}, bf16[3,112,512]{2,1,0:T(8,128)(2,1)S(1)}, u32[]{:S(2)}) copy-start(bf16[3,112,512]{2,1,0:T(8,128)(2,1)S(1)} %collective-permute-done.27.refs_7_) | copy-start | bytes 1032196
  160.8 22.0 %collective-permute-start.18 = (bf16[3,112,512]{2,1,0:T(8,128)(2,1)}, bf16[3,112,512]{2,1,0:T(8,128)(2,1)S(1)}, u32[]{:S(2)}, u32[]{:S(2)}) collective-permute-start(bf16[3,112,512]{2,1,0:T(8,128)(2,1)} %get-tuple-element.69), channel_id=1, source_target_pairs={{0,5},{1,4},{2,7},{3,6},{4,1},{5,0},{6,3},{7,2},{8,13},{9,12},{10,... | collective-permute-start | bytes 1032200 | tf_op jit(solution)/shard_map/ppermute | solution.py:211
  166.7 22.5 %copy-start.14 = (bf16[3,112,512]{2,1,0:T(8,128)(2,1)}, bf16[3,112,512]{2,1,0:T(8,128)(2,1)S(1)}, u32[]{:S(2)}) copy-start(bf16[3,112,512]{2,1,0:T(8,128)(2,1)S(1)} %collective-permute-done.14.refs_1_) | copy-start | bytes 1032196
  166.7 22.5 %collective-permute-start.19 = (bf16[3,112,512]{2,1,0:T(8,128)(2,1)}, bf16[3,112,512]{2,1,0:T(8,128)(2,1)S(1)}, u32[]{:S(2)}, u32[]{:S(2)}) collective-permute-start(bf16[3,112,512]{2,1,0:T(8,128)(2,1)} %get-tuple-element.70), channel_id=1, source_target_pairs={{0,7},{1,6},{2,5},{3,4},{4,3},{5,2},{6,1},{7,0},{8,15},{9,14},{10,... | collective-permute-start | bytes 1032200 | tf_op jit(solution)/shard_map/ppermute | solution.py:211
  174.0 15.1 %copy-start.15 = (bf16[3,112,512]{2,1,0:T(8,128)(2,1)}, bf16[3,112,512]{2,1,0:T(8,128)(2,1)S(1)}, u32[]{:S(2)}) copy-start(bf16[3,112,512]{2,1,0:T(8,128)(2,1)S(1)} %collective-permute-done.15.refs_2_) | copy-start | bytes 1032196
  174.0 15.1 %collective-permute-start.20 = (bf16[3,112,512]{2,1,0:T(8,128)(2,1)}, bf16[3,112,512]{2,1,0:T(8,128)(2,1)S(1)}, u32[]{:S(2)}, u32[]{:S(2)}) collective-permute-start(bf16[3,112,512]{2,1,0:T(8,128)(2,1)} %get-tuple-element.71), channel_id=1, source_target_pairs={{0,1},{1,0},{2,3},{3,2},{4,5},{5,4},{6,7},{7,6},{8,9},{9,8},{10,11... | collective-permute-start | bytes 1032200 | tf_op jit(solution)/shard_map/ppermute | solution.py:211
  179.0 10.2 %copy-start.16 = (bf16[3,112,512]{2,1,0:T(8,128)(2,1)}, bf16[3,112,512]{2,1,0:T(8,128)(2,1)S(1)}, u32[]{:S(2)}) copy-start(bf16[3,112,512]{2,1,0:T(8,128)(2,1)S(1)} %collective-permute-done.16.refs_3_) | copy-start | bytes 1032196
  (20 other events, 82.2 us)

commit v4 on v3

--- a/solution.py
+++ b/solution.py
@@ -82,12 +82,13 @@
         leave[i].wait()
 
 
-def grad_kernel(n, rows, me, *refs):
+def grad_kernel(n, count, rows, me, *refs):
     at = pl.program_id(0)
     groups = lax.axis_size("edp")
-    given, outs, table = refs[:groups], refs[-1 - n : -1], refs[-1]
+    given, outs, table = refs[:groups], refs[-1 - n * count : -1], refs[-1]
     columns = given[0].shape[1]
-    slots, piece, hidden = outs[0].shape
+    slots, piece, width = outs[0].shape
+    hidden = width * count
     tok = columns // slots
 
     @pl.when(at == 0)
@@ -108,7 +109,9 @@
         @pl.when(at == k)
         def _(k=k):
             for s in range(slots):
-                outs[k][s] = total[:, s * hidden : (s + 1) * hidden]
+                for p in range(count):
+                    start = s * hidden + p * width
+                    outs[p * n + k][s] = total[:, start : start + width]
 
 
 def find(n, names, places):
@@ -282,23 +285,26 @@
     diagonal, near = pack([6, 7, 1], [2, 1], [spread[0]])
     came.append(swap(diagonal, 6, "ep"))
 
+    count = len(SPLIT)
     made = call(
-        functools.partial(grad_kernel, n, rows),
+        functools.partial(grad_kernel, n, count, rows),
         1,
         (n,),
         [whole(tall, columns)] * groups,
-        [whole(slots, piece, hidden)] * n,
-        [shape(slots, piece, hidden)] * n,
+        [whole(slots, piece, hidden // count)] * (n * count),
+        [shape(slots, piece, hidden // count)] * (n * count),
         [pltpu.VMEM((groups * columns, slots * hidden), BF)],
     )(me, *given)
-    grads = {0: made[0], **{k: swap(made[k], k, "ep") for k in others}}
+    all_grads = [
+        {0: made[p * n], **{k: swap(made[p * n + k], k, "ep") for k in others}} for p in range(count)
+    ]
     came = order([made[0]], *came)
     passed = swap(
         call(
             bundle_kernel,
             0,
             (),
-            [hbm] * (4),
+            [hbm] * 4,
             hbm,
             shape(4, 3, piece, hidden),
             [
@@ -315,9 +321,10 @@
     homes = []
     for p, (begin, width) in enumerate(zip(begins, widths)):
         first_block = begin // block
+        grads = all_grads[p]
         mine = pl.BlockSpec((piece, block), lambda i, me, *_, at=first_block: (me[0], at + i))
         held = lambda slot, at=first_block: pl.BlockSpec((None, 3, piece, block), lambda i, *_: (slot, 0, 0, at + i))
-        part = pl.BlockSpec((slots, piece, block), lambda i, *_, at=first_block: (0, 0, at + i))
+        part = pl.BlockSpec((slots, piece, block), lambda i, *_: (0, 0, i))
         after = homes[-1][:1] if homes else []
         homes.append(
             call(
@@ -399,7 +406,7 @@
     rows, columns = out_grad.shape[2] // groups, out_grad.shape[3]
     slots, tok, hidden = token_acts.shape[2:]
     fast = n == 8 and groups & (groups - 1) == 0 and rows % (8 * CHUNK) == 0
-    fast = fast and slots == 2 and columns == 128 and tok == 64 and hidden % (FINE * sum(SPLIT)) == 0
+    fast = fast and len(set(SPLIT)) == 1 and slots == 2 and columns == 128 and tok == 64 and hidden % (FINE * sum(SPLIT)) == 0
     return (fast_local if fast else plain_local)(token_acts, out_grad, *others)
 
 

time: 194 us -> 182 us (0.938)
  waiting for transfers between devices: 109 us -> 94.2 us
  starting transfers between devices: 36.3 us -> 40.2 us
    ppermute x28 -> x35, waiting for transfers between devices: 109 us -> 94.2 us  [swap(): lax.ppermute(array, axis, [(i, i ^ k) for i in range(lax.axis_size(axis))])]
    ppermute x28 -> x35, starting transfers between devices: 36.3 us -> 40.2 us  [swap(): lax.ppermute(array, axis, [(i, i ^ k) for i in range(lax.axis_size(axis))])]
    unnamed x80 -> x108, local copies, waits for them, and re-layouts: 6.06 us -> 5.07 us
  transfers between devices with their start and end apart: 28 -> 35, of which waited for: 14 -> 17; matrix products, arithmetic and copies ran while one was open for 0% -> 0% of each run, Pallas kernels for 13% -> 17%
where the time goes in v4:
time: 182 us; the launch traced here: 181 us
  waiting for transfers between devices  94.2 us (52%)
  Pallas kernels  40.9 us (22%)
  starting transfers between devices  40.2 us (22%)
  local copies, waits for them, and re-layouts  5.07 us (3%)
    ppermute x35, waiting for transfers between devices, swap(): lax.ppermute(array, axis, [(i, i ^ k) for i in range(lax.axis_size(axis))])  94.2 us
    ppermute x35, starting transfers between devices, swap(): lax.ppermute(array, axis, [(i, i ^ k) for i in range(lax.axis_size(axis))])  40.2 us
    pallas_call x2, Pallas kernels, fast_local(): call(functools.partial(update_kernel, n), 4, (width // block,), [mine] *...  11.7 us
    pallas_call x2, Pallas kernels, pack(): call(functools.partial(pack_kernel, items), 1, (len(ks),), [pl.BlockSpec(...  8.47 us
    pallas_call x1, Pallas kernels, fast_local(): call(functools.partial(grad_kernel, n, count, rows), 1, (n,), [whole(tall...  8.36 us
    pallas_call x2, Pallas kernels, fast_local(): call(functools.partial(unpack_kernel, begin), 1, (), [hbm] * (n + len(res...  6.16 us
    unnamed x108, local copies, waits for them, and re-layouts  5.07 us
  transfers between devices with their start and end apart: 35, of which 17 were waited for; matrix products, arithmetic and copies ran while one was open for 0% of the time, Pallas kernels for 17%

profile of v4, /device:TPU:17, one launch (start us, length us, event | category | flops | bytes accessed | tf_op | source)
XLA Modules:
  0.0 181.4 jit_solution(11121722288134162576)
XLA Ops:
  0.6 4.5 %shard_map.112 = (bf16[2,3,112,1024]{3,2,1,0:T(8,128)(2,1)}, bf16[2,3,112,1024]{3,2,1,0:T(8,128)(2,1)}) custom-call(s32[1]{0:T(128)} %bitcast.me.me_ref, f32[896,1024]{1,0:T(8,128)} %bitcast.11, bf16[896,1024]{1,0:T(8,128)(2,1)} %bitcast.15, bf16[896,1024]{1,0:T(8,128)(2,1)} %bitcast.19), custom_call_target="tpu_custom_call" | custom-call | tf_op jit(solution)/shard_map/pallas_call | solution.py:263
  5.1 1.2 collective-permute-start
  6.3 1.2 collective-permute-start.1
  7.6 3.3 %shard_map.113 = (bf16[1920,128]{1,0:T(8,128)(2,1)}, bf16[1920,128]{1,0:T(8,128)(2,1)}, bf16[1920,128]{1,0:T(8,128)(2,1)}, bf16[1920,128]{1,0:T(8,128)(2,1)}) custom-call(s32[1]{0:T(128)} %bitcast.4.group, s32[2]{0:T(128)} %bitcast.28, bf16[3584,128]{1,0:T(8,128)(2,1)} %bitcast.26, bf16[2,64,1024]{2,1,0:T(8,128)(2,1)} %bitcast.27, ...), custom_call_target="tpu_custom_call" | custom-call | tf_op jit(solution)/shard_map/pallas_call | solution.py:276
  10.9 4.0 %shard_map.114 = (bf16[2,3,112,1024]{3,2,1,0:T(8,128)(2,1)}, bf16[1,3,112,1024]{3,2,1,0:T(8,128)(2,1)}) custom-call(s32[1]{0:T(128)} %bitcast.me.me_ref, f32[896,1024]{1,0:T(8,128)} %bitcast.12, bf16[896,1024]{1,0:T(8,128)(2,1)} %bitcast.16, bf16[896,1024]{1,0:T(8,128)(2,1)} %bitcast.20, bf16[1920,128]{1,0:T(8,128)(2,1)} %get-tuple-element.53.refs_0_), custom_call_target="tpu_custom_call" | custom-call | tf_op jit(solution)/shard_map/pallas_call | solution.py:263
  15.1 1.3 collective-permute-start.3
  16.4 19.0 %collective-permute-done.3.refs_1_ = bf16[1920,128]{1,0:T(8,128)(2,1)S(1)} collective-permute-done((bf16[1920,128]{1,0:T(8,128)(2,1)S(1)}, bf16[1920,128]{1,0:T(8,128)(2,1)S(1)}, u32[]{:S(2)}, u32[]{:S(2)}) %collective-permute-start.3) | collective-permute-done | bytes 491552 | tf_op jit(solution)/shard_map/ppermute | solution.py:214
  35.5 1.3 collective-permute-done.4.refs_2_
  36.7 23.2 %collective-permute-done.5.refs_3_ = bf16[1920,128]{1,0:T(8,128)(2,1)S(1)} collective-permute-done((bf16[1920,128]{1,0:T(8,128)(2,1)S(1)}, bf16[1920,128]{1,0:T(8,128)(2,1)S(1)}, u32[]{:S(2)}, u32[]{:S(2)}) %collective-permute-start.5) | collective-permute-done | bytes 491552 | tf_op jit(solution)/shard_map/ppermute | solution.py:214
  60.8 8.4 %shard_map.115 = (bf16[2,112,512]{2,1,0:T(8,128)(2,1)}, bf16[2,112,512]{2,1,0:T(8,128)(2,1)}, bf16[2,112,512]{2,1,0:T(8,128)(2,1)}, bf16[2,112,512]{2,1,0:T(8,12...) custom-call(s32[1]{0:T(128)} %bitcast.me.me_ref, ...), custom_call_target="tpu_custom_call" | custom-call | tf_op jit(solution)/shard_map/pallas_call | solution.py:289
  71.2 2.8 %shard_map.117 = bf16[4,3,112,1024]{3,2,1,0:T(8,128)(2,1)} custom-call(bf16[1,3,112,1024]{3,2,1,0:T(8,128)(2,1)} %get-tuple-element.54.refs_0_, bf16[2,3,112,1024]{3,2,1,0:T(8,128)(2,1)} %get-tuple-element.61.refs_1_.refs_4_, bf16[2,3,112,1024]{3,2,1,0:T(8,128)(2,1)} %get-tuple-element.62.refs_2_.refs_6_, ...), custom_call_target="tpu_custom_call" | custom-call | tf_op jit(solution)/shard_map/pallas_call | solution.py:303
  74.1 1.7 collective-permute-start.6
  75.7 2.2 %collective-permute-start.7 = (bf16[2,112,512]{2,1,0:T(8,128)(2,1)S(1)}, bf16[2,112,512]{2,1,0:T(8,128)(2,1)S(1)}, u32[]{:S(2)}, u32[]{:S(2)}) collective-permute-start(bf16[2,112,512]{2,1,0:T(8,128)(2,1)S(1)} %copy-done.53), channel_id=1, source_target_pairs={{0,6},{1,7},{2,4},{3,5},{4,2},{5,3},{6,0},{7,1},{8,14},{9,15},{10,... | collective-permute-start | bytes 688136 | tf_op jit(solution)/shard_map/ppermute | solution.py:214
  78.1 1.2 collective-permute-start.15
  79.3 1.2 collective-permute-start.16
  80.6 3.3 %collective-permute-done.7.refs_11_ = bf16[2,112,512]{2,1,0:T(8,128)(2,1)S(1)} collective-permute-done((bf16[2,112,512]{2,1,0:T(8,128)(2,1)S(1)}, bf16[2,112,512]{2,1,0:T(8,128)(2,1)S(1)}, u32[]{:S(2)}, u32[]{:S(2)}) %collective-permute-start.7) | collective-permute-done | bytes 229408 | tf_op jit(solution)/shard_map/ppermute | solution.py:214
  83.8 2.5 %collective-permute-start.17 = (bf16[2,112,512]{2,1,0:T(8,128)(2,1)S(1)}, bf16[2,112,512]{2,1,0:T(8,128)(2,1)S(1)}, u32[]{:S(2)}, u32[]{:S(2)}) collective-permute-start(bf16[2,112,512]{2,1,0:T(8,128)(2,1)S(1)} %copy-done.49), channel_id=1, source_target_pairs={{0,3},{1,2},{2,1},{3,0},{4,7},{5,6},{6,5},{7,4},{8,11},{9,10},{10,... | collective-permute-start | bytes 688136 | tf_op jit(solution)/shard_map/ppermute | solution.py:214
  86.3 2.4 %collective-permute-done.14.refs_11_ = bf16[2,112,512]{2,1,0:T(8,128)(2,1)S(1)} collective-permute-done((bf16[2,112,512]{2,1,0:T(8,128)(2,1)S(1)}, bf16[2,112,512]{2,1,0:T(8,128)(2,1)S(1)}, u32[]{:S(2)}, u32[]{:S(2)}) %collective-permute-start.14) | collective-permute-done | bytes 229408 | tf_op jit(solution)/shard_map/ppermute | solution.py:214
  88.8 2.4 %collective-permute-start.18 = (bf16[2,112,512]{2,1,0:T(8,128)(2,1)S(1)}, bf16[2,112,512]{2,1,0:T(8,128)(2,1)S(1)}, u32[]{:S(2)}, u32[]{:S(2)}) collective-permute-start(bf16[2,112,512]{2,1,0:T(8,128)(2,1)S(1)} %copy-done.48), channel_id=1, source_target_pairs={{0,5},{1,4},{2,7},{3,6},{4,1},{5,0},{6,3},{7,2},{8,13},{9,12},{10,... | collective-permute-start | bytes 688136 | tf_op jit(solution)/shard_map/ppermute | solution.py:214
  91.2 2.5 %collective-permute-done.15.refs_12_ = bf16[2,112,512]{2,1,0:T(8,128)(2,1)S(1)} collective-permute-done((bf16[2,112,512]{2,1,0:T(8,128)(2,1)S(1)}, bf16[2,112,512]{2,1,0:T(8,128)(2,1)S(1)}, u32[]{:S(2)}, u32[]{:S(2)}) %collective-permute-start.15) | collective-permute-done | bytes 229408 | tf_op jit(solution)/shard_map/ppermute | solution.py:214
  93.7 2.3 %collective-permute-start.19 = (bf16[2,112,512]{2,1,0:T(8,128)(2,1)S(1)}, bf16[2,112,512]{2,1,0:T(8,128)(2,1)S(1)}, u32[]{:S(2)}, u32[]{:S(2)}) collective-permute-start(bf16[2,112,512]{2,1,0:T(8,128)(2,1)S(1)} %copy-done.47), channel_id=1, source_target_pairs={{0,7},{1,6},{2,5},{3,4},{4,3},{5,2},{6,1},{7,0},{8,15},{9,14},{10,... | collective-permute-start | bytes 688136 | tf_op jit(solution)/shard_map/ppermute | solution.py:214
  96.2 3.4 %collective-permute-done.17.refs_14_ = bf16[2,112,512]{2,1,0:T(8,128)(2,1)S(1)} collective-permute-done((bf16[2,112,512]{2,1,0:T(8,128)(2,1)S(1)}, bf16[2,112,512]{2,1,0:T(8,128)(2,1)S(1)}, u32[]{:S(2)}, u32[]{:S(2)}) %collective-permute-start.17) | collective-permute-done | bytes 229408 | tf_op jit(solution)/shard_map/ppermute | solution.py:214
  99.6 1.2 collective-permute-start.8
  101.1 3.1 %collective-permute-done.19.refs_16_ = bf16[2,112,512]{2,1,0:T(8,128)(2,1)S(1)} collective-permute-done((bf16[2,112,512]{2,1,0:T(8,128)(2,1)S(1)}, bf16[2,112,512]{2,1,0:T(8,128)(2,1)S(1)}, u32[]{:S(2)}, u32[]{:S(2)}) %collective-permute-start.19) | collective-permute-done | bytes 229408 | tf_op jit(solution)/shard_map/ppermute | solution.py:214
  105.1 1.8 %collective-permute-start.11 = (bf16[2,112,512]{2,1,0:T(8,128)(2,1)S(1)}, bf16[2,112,512]{2,1,0:T(8,128)(2,1)S(1)}, u32[]{:S(2)}, u32[]{:S(2)}) collective-permute-start(bf16[2,112,512]{2,1,0:T(8,128)(2,1)S(1)} %copy-done.42), channel_id=1, source_target_pairs={{0,5},{1,4},{2,7},{3,6},{4,1},{5,0},{6,3},{7,2},{8,13},{9,12},{10,... | collective-permute-start | bytes 688136 | tf_op jit(solution)/shard_map/ppermute | solution.py:214
  107.1 1.4 copy-done
  108.5 5.8 %shard_map.118 = (bf16[3,112,512]{2,1,0:T(8,128)(2,1)}, bf16[3,112,512]{2,1,0:T(8,128)(2,1)}, bf16[3,112,512]{2,1,0:T(8,128)(2,1)}, bf16[3,112,512]{2,1,0:T(8,12...) custom-call(s32[1]{0:T(128)} %bitcast.me.me_ref, ...), custom_call_target="tpu_custom_call" | custom-call | tf_op jit(solution)/shard_map/pallas_call | solution.py:330
  115.7 1.3 collective-permute-start.30
  117.0 1.2 collective-permute-start.31
  119.0 1.5 collective-permute-done.13.refs_17_
  120.5 1.2 collective-permute-start.32
  121.8 6.0 %shard_map.119 = (bf16[3,112,512]{2,1,0:T(8,128)(2,1)}, bf16[3,112,512]{2,1,0:T(8,128)(2,1)}, bf16[3,112,512]{2,1,0:T(8,128)(2,1)}, bf16[3,112,512]{2,1,0:T(8,12...) custom-call(s32[1]{0:T(128)} %bitcast.me.me_ref, ...), custom_call_target="tpu_custom_call" | custom-call | tf_op jit(solution)/shard_map/pallas_call | solution.py:330
  127.8 1.6 collective-permute-start.33
  129.3 3.7 %collective-permute-done.29.refs_2_ = bf16[3,112,512]{2,1,0:T(8,128)(2,1)S(1)} collective-permute-done((bf16[3,112,512]{2,1,0:T(8,128)(2,1)}, bf16[3,112,512]{2,1,0:T(8,128)(2,1)S(1)}, u32[]{:S(2)}, u32[]{:S(2)}) %collective-permute-start.29) | collective-permute-done | bytes 344096 | tf_op jit(solution)/shard_map/ppermute | solution.py:214
  133.1 1.3 collective-permute-start.34
  134.4 1.1 collective-permute-start.21
  135.6 5.8 %collective-permute-done.31.refs_4_ = bf16[3,112,512]{2,1,0:T(8,128)(2,1)S(1)} collective-permute-done((bf16[3,112,512]{2,1,0:T(8,128)(2,1)}, bf16[3,112,512]{2,1,0:T(8,128)(2,1)S(1)}, u32[]{:S(2)}, u32[]{:S(2)}) %collective-permute-start.31) | collective-permute-done | bytes 344096 | tf_op jit(solution)/shard_map/ppermute | solution.py:214
  141.4 1.2 collective-permute-start.22
  142.8 5.7 %collective-permute-done.33.refs_6_ = bf16[3,112,512]{2,1,0:T(8,128)(2,1)S(1)} collective-permute-done((bf16[3,112,512]{2,1,0:T(8,128)(2,1)S(1)}, bf16[3,112,512]{2,1,0:T(8,128)(2,1)S(1)}, u32[]{:S(2)}, u32[]{:S(2)}) %collective-permute-start.33) | collective-permute-done | bytes 344096 | tf_op jit(solution)/shard_map/ppermute | solution.py:214
  149.4 1.9 %collective-permute-start.25 = (bf16[3,112,512]{2,1,0:T(8,128)(2,1)}, bf16[3,112,512]{2,1,0:T(8,128)(2,1)S(1)}, u32[]{:S(2)}, u32[]{:S(2)}) collective-permute-start(bf16[3,112,512]{2,1,0:T(8,128)(2,1)} %get-tuple-element.85), channel_id=1, source_target_pairs={{0,5},{1,4},{2,7},{3,6},{4,1},{5,0},{6,3},{7,2},{8,13},{9,12},{10,... | collective-permute-start | bytes 1032200 | tf_op jit(solution)/shard_map/ppermute | solution.py:214
  151.2 4.0 %collective-permute-done.21.refs_1_ = bf16[3,112,512]{2,1,0:T(8,128)(2,1)S(1)} collective-permute-done((bf16[3,112,512]{2,1,0:T(8,128)(2,1)}, bf16[3,112,512]{2,1,0:T(8,128)(2,1)S(1)}, u32[]{:S(2)}, u32[]{:S(2)}) %collective-permute-start.21) | collective-permute-done | bytes 344096 | tf_op jit(solution)/shard_map/ppermute | solution.py:214
  155.2 3.4 %collective-permute-start.26 = (bf16[3,112,512]{2,1,0:T(8,128)(2,1)}, bf16[3,112,512]{2,1,0:T(8,128)(2,1)S(1)}, u32[]{:S(2)}, u32[]{:S(2)}) collective-permute-start(bf16[3,112,512]{2,1,0:T(8,128)(2,1)} %get-tuple-element.86), channel_id=1, source_target_pairs={{0,7},{1,6},{2,5},{3,4},{4,3},{5,2},{6,1},{7,0},{8,15},{9,14},{10,... | collective-permute-start | bytes 1032200 | tf_op jit(solution)/shard_map/ppermute | solution.py:214
  158.6 4.1 %collective-permute-done.22.refs_2_ = bf16[3,112,512]{2,1,0:T(8,128)(2,1)S(1)} collective-permute-done((bf16[3,112,512]{2,1,0:T(8,128)(2,1)}, bf16[3,112,512]{2,1,0:T(8,128)(2,1)S(1)}, u32[]{:S(2)}, u32[]{:S(2)}) %collective-permute-start.22) | collective-permute-done | bytes 344096 | tf_op jit(solution)/shard_map/ppermute | solution.py:214
  162.6 1.3 collective-permute-start.27
  164.0 3.1 %shard_map.120 = (f32[896,1024]{1,0:T(8,128)}, bf16[896,1024]{1,0:T(8,128)(2,1)}, bf16[896,1024]{1,0:T(8,128)(2,1)}) custom-call(s32[1]{0:T(128)} %bitcast.me.me_ref, bf16[3,112,512]{2,1,0:T(8,128)(2,1)} %get-tuple-element.79.refs_18_.refs_0_, bf16[3,112,512]{2,1,0:T(8,128)(2,1)} %copy-done.14, bf16[3,112,512]{2,1,0:T(8,128)(2,1)} %copy-done.15, ...), custom_call_target="tpu_custom_call" | custom-call | tf_op jit(solution)/shard_map/pallas_call | solution.py:352
  167.1 3.8 %collective-permute-done.24.refs_4_ = bf16[3,112,512]{2,1,0:T(8,128)(2,1)S(1)} collective-permute-done((bf16[3,112,512]{2,1,0:T(8,128)(2,1)}, bf16[3,112,512]{2,1,0:T(8,128)(2,1)S(1)}, u32[]{:S(2)}, u32[]{:S(2)}) %collective-permute-start.24) | collective-permute-done | bytes 344096 | tf_op jit(solution)/shard_map/ppermute | solution.py:214
  170.9 6.6 %collective-permute-done.26.refs_6_ = bf16[3,112,512]{2,1,0:T(8,128)(2,1)S(1)} collective-permute-done((bf16[3,112,512]{2,1,0:T(8,128)(2,1)}, bf16[3,112,512]{2,1,0:T(8,128)(2,1)S(1)}, u32[]{:S(2)}, u32[]{:S(2)}) %collective-permute-start.26) | collective-permute-done | bytes 344096 | tf_op jit(solution)/shard_map/ppermute | solution.py:214
  178.3 3.1 %shard_map.121 = (f32[896,1024]{1,0:T(8,128)}, bf16[896,1024]{1,0:T(8,128)(2,1)}, bf16[896,1024]{1,0:T(8,128)(2,1)}) custom-call(s32[1]{0:T(128)} %bitcast.me.me_ref, bf16[3,112,512]{2,1,0:T(8,128)(2,1)} %get-tuple-element.80.refs_0_, bf16[3,112,512]{2,1,0:T(8,128)(2,1)} %copy-done.7, ...), custom_call_target="tpu_custom_call", output_to_operand_aliasing={{0}: (9, {}), {1}: (10, {}), {2}: (11, {})} | custom-call | tf_op jit(solution)/shard_map/pallas_call | solution.py:352
  (140 shorter events, 8.9 us)
Async XLA Ops:
  5.1 64.0 %collective-permute-start = (bf16[2,3,112,1024]{3,2,1,0:T(8,128)(2,1)}, bf16[2,3,112,1024]{3,2,1,0:T(8,128)(2,1)S(1)}, u32[]{:S(2)}, u32[]{:S(2)}) collective-permute-start(bf16[2,3,112,1024]{3,2,1,0:T(8,128)(2,1)} %get-tuple-element.55), channel_id=1, source_target_pairs={{0,2},{1,3},{2,0},{3,1},{4,6},{5,7},{6,4},{7,5},{8,10},{9,11},{10,... | collective-permute-start | bytes 4128776 | tf_op jit(solution)/shard_map/ppermute | solution.py:214
  6.3 62.8 %collective-permute-start.1 = (bf16[2,3,112,1024]{3,2,1,0:T(8,128)(2,1)}, bf16[2,3,112,1024]{3,2,1,0:T(8,128)(2,1)S(1)}, u32[]{:S(2)}, u32[]{:S(2)}) collective-permute-start(bf16[2,3,112,1024]{3,2,1,0:T(8,128)(2,1)} %get-tuple-element.52.refs_0_), channel_id=1, source_target_pairs={{0,4},{1,5},{2,6},{3,7},{4,0},{5,1},{6,2},{7,3},{8,12},{9,13},{10,... | collective-permute-start | bytes 4128776 | tf_op jit(solution)/shard_map/ppermute | solution.py:214
  10.9 24.6 %copy-start.35 = (bf16[1920,128]{1,0:T(8,128)(2,1)S(1)}, bf16[1920,128]{1,0:T(8,128)(2,1)}, u32[]{:S(2)}) copy-start(bf16[1920,128]{1,0:T(8,128)(2,1)} %get-tuple-element.59) | copy-start | bytes 1474564
  14.9 54.3 %collective-permute-start.2 = (bf16[2,3,112,1024]{3,2,1,0:T(8,128)(2,1)}, bf16[2,3,112,1024]{3,2,1,0:T(8,128)(2,1)S(1)}, u32[]{:S(2)}, u32[]{:S(2)}) collective-permute-start(bf16[2,3,112,1024]{3,2,1,0:T(8,128)(2,1)} %get-tuple-element.56), channel_id=1, source_target_pairs={{0,6},{1,7},{2,4},{3,5},{4,2},{5,3},{6,0},{7,1},{8,14},{9,15},{10,... | collective-permute-start | bytes 4128776 | tf_op jit(solution)/shard_map/ppermute | solution.py:214
  15.1 20.4 %collective-permute-start.3 = (bf16[1920,128]{1,0:T(8,128)(2,1)S(1)}, bf16[1920,128]{1,0:T(8,128)(2,1)S(1)}, u32[]{:S(2)}, u32[]{:S(2)}) collective-permute-start(bf16[1920,128]{1,0:T(8,128)(2,1)S(1)} %copy-done.37), channel_id=1, source_target_pairs={{0,8},{8,0},{16,24},{24,16},{1,9},{9,1},{17,25},{25,17},{2,10},{10... | collective-permute-start | bytes 1474568 | tf_op jit(solution)/shard_map/ppermute | solution.py:214
  16.4 20.4 %collective-permute-start.4 = (bf16[1920,128]{1,0:T(8,128)(2,1)S(1)}, bf16[1920,128]{1,0:T(8,128)(2,1)S(1)}, u32[]{:S(2)}, u32[]{:S(2)}) collective-permute-start(bf16[1920,128]{1,0:T(8,128)(2,1)S(1)} %copy-done.36), channel_id=1, source_target_pairs={{0,16},{8,24},{16,0},{24,8},{1,17},{9,25},{17,1},{25,9},{2,18},{10... | collective-permute-start | bytes 1474568 | tf_op jit(solution)/shard_map/ppermute | solution.py:214
  35.5 24.5 %copy-start.4 = (bf16[1920,128]{1,0:T(8,128)(2,1)}, bf16[1920,128]{1,0:T(8,128)(2,1)S(1)}, u32[]{:S(2)}) copy-start(bf16[1920,128]{1,0:T(8,128)(2,1)S(1)} %collective-permute-done.3.refs_1_) | copy-start | bytes 1474564
  35.5 24.5 %collective-permute-start.5 = (bf16[1920,128]{1,0:T(8,128)(2,1)S(1)}, bf16[1920,128]{1,0:T(8,128)(2,1)S(1)}, u32[]{:S(2)}, u32[]{:S(2)}) collective-permute-start(bf16[1920,128]{1,0:T(8,128)(2,1)S(1)} %copy-done.35), channel_id=1, source_target_pairs={{0,24},{8,16},{16,8},{24,0},{1,25},{9,17},{17,9},{25,1},{2,26},{10... | collective-permute-start | bytes 1474568 | tf_op jit(solution)/shard_map/ppermute | solution.py:214
  36.7 23.2 %copy-start.5 = (bf16[1920,128]{1,0:T(8,128)(2,1)}, bf16[1920,128]{1,0:T(8,128)(2,1)S(1)}, u32[]{:S(2)}) copy-start(bf16[1920,128]{1,0:T(8,128)(2,1)S(1)} %collective-permute-done.4.refs_2_) | copy-start | bytes 1474564
  71.1 24.9 %copy-start.46 = (bf16[2,112,512]{2,1,0:T(8,128)(2,1)S(1)}, bf16[2,112,512]{2,1,0:T(8,128)(2,1)}, u32[]{:S(2)}) copy-start(bf16[2,112,512]{2,1,0:T(8,128)(2,1)} %get-tuple-element.78) | copy-start | bytes 688132
  71.2 28.4 %copy-start.45 = (bf16[2,112,512]{2,1,0:T(8,128)(2,1)S(1)}, bf16[2,112,512]{2,1,0:T(8,128)(2,1)}, u32[]{:S(2)}) copy-start(bf16[2,112,512]{2,1,0:T(8,128)(2,1)} %get-tuple-element.66) | copy-start | bytes 688132
  71.2 29.6 %copy-start.44 = (bf16[2,112,512]{2,1,0:T(8,128)(2,1)S(1)}, bf16[2,112,512]{2,1,0:T(8,128)(2,1)}, u32[]{:S(2)}) copy-start(bf16[2,112,512]{2,1,0:T(8,128)(2,1)} %get-tuple-element.67) | copy-start | bytes 688132
  71.2 33.0 %copy-start.43 = (bf16[2,112,512]{2,1,0:T(8,128)(2,1)S(1)}, bf16[2,112,512]{2,1,0:T(8,128)(2,1)}, u32[]{:S(2)}) copy-start(bf16[2,112,512]{2,1,0:T(8,128)(2,1)} %get-tuple-element.68) | copy-start | bytes 688132
  71.2 33.9 %copy-start.42 = (bf16[2,112,512]{2,1,0:T(8,128)(2,1)S(1)}, bf16[2,112,512]{2,1,0:T(8,128)(2,1)}, u32[]{:S(2)}) copy-start(bf16[2,112,512]{2,1,0:T(8,128)(2,1)} %get-tuple-element.69) | copy-start | bytes 688132
  71.2 35.7 %copy-start.41 = (bf16[2,112,512]{2,1,0:T(8,128)(2,1)S(1)}, bf16[2,112,512]{2,1,0:T(8,128)(2,1)}, u32[]{:S(2)}) copy-start(bf16[2,112,512]{2,1,0:T(8,128)(2,1)} %get-tuple-element.70) | copy-start | bytes 688132
  74.1 32.9 %collective-permute-start.6 = (bf16[4,3,112,1024]{3,2,1,0:T(8,128)(2,1)}, bf16[4,3,112,1024]{3,2,1,0:T(8,128)(2,1)S(1)}, u32[]{:S(2)}, u32[]{:S(2)}) collective-permute-start(bf16[4,3,112,1024]{3,2,1,0:T(8,128)(2,1)} %shard_map.117), channel_id=1, source_target_pairs={{0,1},{1,0},{2,3},{3,2},{4,5},{5,4},{6,7},{7,6},{8,9},{9,8},{10,11... | collective-permute-start | bytes 8257544 | tf_op jit(solution)/shard_map/ppermute | solution.py:214
  75.7 8.1 %collective-permute-start.7 = (bf16[2,112,512]{2,1,0:T(8,128)(2,1)S(1)}, bf16[2,112,512]{2,1,0:T(8,128)(2,1)S(1)}, u32[]{:S(2)}, u32[]{:S(2)}) collective-permute-start(bf16[2,112,512]{2,1,0:T(8,128)(2,1)S(1)} %copy-done.53), channel_id=1, source_target_pairs={{0,6},{1,7},{2,4},{3,5},{4,2},{5,3},{6,0},{7,1},{8,14},{9,15},{10,... | collective-permute-start | bytes 688136 | tf_op jit(solution)/shard_map/ppermute | solution.py:214
  77.9 10.9 %collective-permute-start.14 = (bf16[2,112,512]{2,1,0:T(8,128)(2,1)S(1)}, bf16[2,112,512]{2,1,0:T(8,128)(2,1)S(1)}, u32[]{:S(2)}, u32[]{:S(2)}) collective-permute-start(bf16[2,112,512]{2,1,0:T(8,128)(2,1)S(1)} %copy-done.52), channel_id=1, source_target_pairs={{0,6},{1,7},{2,4},{3,5},{4,2},{5,3},{6,0},{7,1},{8,14},{9,15},{10,... | collective-permute-start | bytes 688136 | tf_op jit(solution)/shard_map/ppermute | solution.py:214
  78.1 15.6 %collective-permute-start.15 = (bf16[2,112,512]{2,1,0:T(8,128)(2,1)S(1)}, bf16[2,112,512]{2,1,0:T(8,128)(2,1)S(1)}, u32[]{:S(2)}, u32[]{:S(2)}) collective-permute-start(bf16[2,112,512]{2,1,0:T(8,128)(2,1)S(1)} %copy-done.51), channel_id=1, source_target_pairs={{0,2},{1,3},{2,0},{3,1},{4,6},{5,7},{6,4},{7,5},{8,10},{9,11},{10,... | collective-permute-start | bytes 688136 | tf_op jit(solution)/shard_map/ppermute | solution.py:214
  79.3 16.8 %collective-permute-start.16 = (bf16[2,112,512]{2,1,0:T(8,128)(2,1)S(1)}, bf16[2,112,512]{2,1,0:T(8,128)(2,1)S(1)}, u32[]{:S(2)}, u32[]{:S(2)}) collective-permute-start(bf16[2,112,512]{2,1,0:T(8,128)(2,1)S(1)} %copy-done.50), channel_id=1, source_target_pairs={{0,4},{1,5},{2,6},{3,7},{4,0},{5,1},{6,2},{7,3},{8,12},{9,13},{10,... | collective-permute-start | bytes 688136 | tf_op jit(solution)/shard_map/ppermute | solution.py:214
  83.8 30.4 %copy-start.21 = (bf16[2,112,512]{2,1,0:T(8,128)(2,1)}, bf16[2,112,512]{2,1,0:T(8,128)(2,1)S(1)}, u32[]{:S(2)}) copy-start(bf16[2,112,512]{2,1,0:T(8,128)(2,1)S(1)} %collective-permute-done.7.refs_11_) | copy-start | bytes 688132
  83.8 15.7 %collective-permute-start.17 = (bf16[2,112,512]{2,1,0:T(8,128)(2,1)S(1)}, bf16[2,112,512]{2,1,0:T(8,128)(2,1)S(1)}, u32[]{:S(2)}, u32[]{:S(2)}) collective-permute-start(bf16[2,112,512]{2,1,0:T(8,128)(2,1)S(1)} %copy-done.49), channel_id=1, source_target_pairs={{0,3},{1,2},{2,1},{3,0},{4,7},{5,6},{6,5},{7,4},{8,11},{9,10},{10,... | collective-permute-start | bytes 688136 | tf_op jit(solution)/shard_map/ppermute | solution.py:214
  88.8 12.0 %collective-permute-start.18 = (bf16[2,112,512]{2,1,0:T(8,128)(2,1)S(1)}, bf16[2,112,512]{2,1,0:T(8,128)(2,1)S(1)}, u32[]{:S(2)}, u32[]{:S(2)}) collective-permute-start(bf16[2,112,512]{2,1,0:T(8,128)(2,1)S(1)} %copy-done.48), channel_id=1, source_target_pairs={{0,5},{1,4},{2,7},{3,6},{4,1},{5,0},{6,3},{7,2},{8,13},{9,12},{10,... | collective-permute-start | bytes 688136 | tf_op jit(solution)/shard_map/ppermute | solution.py:214
  93.7 10.4 %collective-permute-start.19 = (bf16[2,112,512]{2,1,0:T(8,128)(2,1)S(1)}, bf16[2,112,512]{2,1,0:T(8,128)(2,1)S(1)}, u32[]{:S(2)}, u32[]{:S(2)}) collective-permute-start(bf16[2,112,512]{2,1,0:T(8,128)(2,1)S(1)} %copy-done.47), channel_id=1, source_target_pairs={{0,7},{1,6},{2,5},{3,4},{4,3},{5,2},{6,1},{7,0},{8,15},{9,14},{10,... | collective-permute-start | bytes 688136 | tf_op jit(solution)/shard_map/ppermute | solution.py:214
  96.1 9.0 %collective-permute-start.20 = (bf16[2,112,512]{2,1,0:T(8,128)(2,1)S(1)}, bf16[2,112,512]{2,1,0:T(8,128)(2,1)S(1)}, u32[]{:S(2)}, u32[]{:S(2)}) collective-permute-start(bf16[2,112,512]{2,1,0:T(8,128)(2,1)S(1)} %copy-done.46), channel_id=1, source_target_pairs={{0,1},{1,0},{2,3},{3,2},{4,5},{5,4},{6,7},{7,6},{8,9},{9,8},{10,11... | collective-permute-start | bytes 688136 | tf_op jit(solution)/shard_map/ppermute | solution.py:214
  99.6 14.7 %collective-permute-start.8 = (bf16[2,112,512]{2,1,0:T(8,128)(2,1)S(1)}, bf16[2,112,512]{2,1,0:T(8,128)(2,1)S(1)}, u32[]{:S(2)}, u32[]{:S(2)}) collective-permute-start(bf16[2,112,512]{2,1,0:T(8,128)(2,1)S(1)} %copy-done.45), channel_id=1, source_target_pairs={{0,2},{1,3},{2,0},{3,1},{4,6},{5,7},{6,4},{7,5},{8,10},{9,11},{10,... | collective-permute-start | bytes 688136 | tf_op jit(solution)/shard_map/ppermute | solution.py:214
  100.8 14.4 %collective-permute-start.9 = (bf16[2,112,512]{2,1,0:T(8,128)(2,1)S(1)}, bf16[2,112,512]{2,1,0:T(8,128)(2,1)S(1)}, u32[]{:S(2)}, u32[]{:S(2)}) collective-permute-start(bf16[2,112,512]{2,1,0:T(8,128)(2,1)S(1)} %copy-done.44), channel_id=1, source_target_pairs={{0,4},{1,5},{2,6},{3,7},{4,0},{5,1},{6,2},{7,3},{8,12},{9,13},{10,... | collective-permute-start | bytes 688136 | tf_op jit(solution)/shard_map/ppermute | solution.py:214
  104.1 11.6 %collective-permute-start.10 = (bf16[2,112,512]{2,1,0:T(8,128)(2,1)S(1)}, bf16[2,112,512]{2,1,0:T(8,128)(2,1)S(1)}, u32[]{:S(2)}, u32[]{:S(2)}) collective-permute-start(bf16[2,112,512]{2,1,0:T(8,128)(2,1)S(1)} %copy-done.43), channel_id=1, source_target_pairs={{0,3},{1,2},{2,1},{3,0},{4,7},{5,6},{6,5},{7,4},{8,11},{9,10},{10,... | collective-permute-start | bytes 688136 | tf_op jit(solution)/shard_map/ppermute | solution.py:214
  105.1 11.9 %collective-permute-start.11 = (bf16[2,112,512]{2,1,0:T(8,128)(2,1)S(1)}, bf16[2,112,512]{2,1,0:T(8,128)(2,1)S(1)}, u32[]{:S(2)}, u32[]{:S(2)}) collective-permute-start(bf16[2,112,512]{2,1,0:T(8,128)(2,1)S(1)} %copy-done.42), channel_id=1, source_target_pairs={{0,5},{1,4},{2,7},{3,6},{4,1},{5,0},{6,3},{7,2},{8,13},{9,12},{10,... | collective-permute-start | bytes 688136 | tf_op jit(solution)/shard_map/ppermute | solution.py:214
  106.9 12.0 %collective-permute-start.12 = (bf16[2,112,512]{2,1,0:T(8,128)(2,1)S(1)}, bf16[2,112,512]{2,1,0:T(8,128)(2,1)S(1)}, u32[]{:S(2)}, u32[]{:S(2)}) collective-permute-start(bf16[2,112,512]{2,1,0:T(8,128)(2,1)S(1)} %copy-done.41), channel_id=1, source_target_pairs={{0,7},{1,6},{2,5},{3,4},{4,3},{5,2},{6,1},{7,0},{8,15},{9,14},{10,... | collective-permute-start | bytes 688136 | tf_op jit(solution)/shard_map/ppermute | solution.py:214
  114.3 13.5 %collective-permute-start.28 = (bf16[3,112,512]{2,1,0:T(8,128)(2,1)}, bf16[3,112,512]{2,1,0:T(8,128)(2,1)S(1)}, u32[]{:S(2)}, u32[]{:S(2)}) collective-permute-start(bf16[3,112,512]{2,1,0:T(8,128)(2,1)} %get-tuple-element.88), channel_id=1, source_target_pairs={{0,6},{1,7},{2,4},{3,5},{4,2},{5,3},{6,0},{7,1},{8,14},{9,15},{10,... | collective-permute-start | bytes 1032200 | tf_op jit(solution)/shard_map/ppermute | solution.py:214
  115.1 17.9 %collective-permute-start.29 = (bf16[3,112,512]{2,1,0:T(8,128)(2,1)}, bf16[3,112,512]{2,1,0:T(8,128)(2,1)S(1)}, u32[]{:S(2)}, u32[]{:S(2)}) collective-permute-start(bf16[3,112,512]{2,1,0:T(8,128)(2,1)} %get-tuple-element.89), channel_id=1, source_target_pairs={{0,2},{1,3},{2,0},{3,1},{4,6},{5,7},{6,4},{7,5},{8,10},{9,11},{10,... | collective-permute-start | bytes 1032200 | tf_op jit(solution)/shard_map/ppermute | solution.py:214
  115.7 18.7 %collective-permute-start.30 = (bf16[3,112,512]{2,1,0:T(8,128)(2,1)}, bf16[3,112,512]{2,1,0:T(8,128)(2,1)S(1)}, u32[]{:S(2)}, u32[]{:S(2)}) collective-permute-start(bf16[3,112,512]{2,1,0:T(8,128)(2,1)} %get-tuple-element.90), channel_id=1, source_target_pairs={{0,4},{1,5},{2,6},{3,7},{4,0},{5,1},{6,2},{7,3},{8,12},{9,13},{10,... | collective-permute-start | bytes 1032200 | tf_op jit(solution)/shard_map/ppermute | solution.py:214
  117.0 24.4 %collective-permute-start.31 = (bf16[3,112,512]{2,1,0:T(8,128)(2,1)}, bf16[3,112,512]{2,1,0:T(8,128)(2,1)S(1)}, u32[]{:S(2)}, u32[]{:S(2)}) collective-permute-start(bf16[3,112,512]{2,1,0:T(8,128)(2,1)} %get-tuple-element.91), channel_id=1, source_target_pairs={{0,3},{1,2},{2,1},{3,0},{4,7},{5,6},{6,5},{7,4},{8,11},{9,10},{10,... | collective-permute-start | bytes 1032200 | tf_op jit(solution)/shard_map/ppermute | solution.py:214
  119.0 1.5 collective-permute-start.13
  120.5 22.1 %collective-permute-start.32 = (bf16[3,112,512]{2,1,0:T(8,128)(2,1)}, bf16[3,112,512]{2,1,0:T(8,128)(2,1)S(1)}, u32[]{:S(2)}, u32[]{:S(2)}) collective-permute-start(bf16[3,112,512]{2,1,0:T(8,128)(2,1)} %get-tuple-element.92), channel_id=1, source_target_pairs={{0,5},{1,4},{2,7},{3,6},{4,1},{5,0},{6,3},{7,2},{8,13},{9,12},{10,... | collective-permute-start | bytes 1032200 | tf_op jit(solution)/shard_map/ppermute | solution.py:214
  127.7 36.2 %copy-start.14 = (bf16[3,112,512]{2,1,0:T(8,128)(2,1)}, bf16[3,112,512]{2,1,0:T(8,128)(2,1)S(1)}, u32[]{:S(2)}) copy-start(bf16[3,112,512]{2,1,0:T(8,128)(2,1)S(1)} %collective-permute-done.28.refs_1_) | copy-start | bytes 1032196
  127.8 20.8 %collective-permute-start.33 = (bf16[3,112,512]{2,1,0:T(8,128)(2,1)S(1)}, bf16[3,112,512]{2,1,0:T(8,128)(2,1)S(1)}, u32[]{:S(2)}, u32[]{:S(2)}) collective-permute-start(bf16[3,112,512]{2,1,0:T(8,128)(2,1)S(1)} %copy-done.39), channel_id=1, source_target_pairs={{0,7},{1,6},{2,5},{3,4},{4,3},{5,2},{6,1},{7,0},{8,15},{9,14},{10,... | collective-permute-start | bytes 1032200 | tf_op jit(solution)/shard_map/ppermute | solution.py:214
  133.1 30.9 %copy-start.15 = (bf16[3,112,512]{2,1,0:T(8,128)(2,1)}, bf16[3,112,512]{2,1,0:T(8,128)(2,1)S(1)}, u32[]{:S(2)}) copy-start(bf16[3,112,512]{2,1,0:T(8,128)(2,1)S(1)} %collective-permute-done.29.refs_2_) | copy-start | bytes 1032196
  133.1 16.3 %collective-permute-start.34 = (bf16[3,112,512]{2,1,0:T(8,128)(2,1)S(1)}, bf16[3,112,512]{2,1,0:T(8,128)(2,1)S(1)}, u32[]{:S(2)}, u32[]{:S(2)}) collective-permute-start(bf16[3,112,512]{2,1,0:T(8,128)(2,1)S(1)} %copy-done.38), channel_id=1, source_target_pairs={{0,1},{1,0},{2,3},{3,2},{4,5},{5,4},{6,7},{7,6},{8,9},{9,8},{10,11... | collective-permute-start | bytes 1032200 | tf_op jit(solution)/shard_map/ppermute | solution.py:214
  134.4 29.5 %copy-start.16 = (bf16[3,112,512]{2,1,0:T(8,128)(2,1)}, bf16[3,112,512]{2,1,0:T(8,128)(2,1)S(1)}, u32[]{:S(2)}) copy-start(bf16[3,112,512]{2,1,0:T(8,128)(2,1)S(1)} %collective-permute-done.30.refs_3_) | copy-start | bytes 1032196
  134.4 20.8 %collective-permute-start.21 = (bf16[3,112,512]{2,1,0:T(8,128)(2,1)}, bf16[3,112,512]{2,1,0:T(8,128)(2,1)S(1)}, u32[]{:S(2)}, u32[]{:S(2)}) collective-permute-start(bf16[3,112,512]{2,1,0:T(8,128)(2,1)} %get-tuple-element.81), channel_id=1, source_target_pairs={{0,6},{1,7},{2,4},{3,5},{4,2},{5,3},{6,0},{7,1},{8,14},{9,15},{10,... | collective-permute-start | bytes 1032200 | tf_op jit(solution)/shard_map/ppermute | solution.py:214
  141.4 21.2 %collective-permute-start.22 = (bf16[3,112,512]{2,1,0:T(8,128)(2,1)}, bf16[3,112,512]{2,1,0:T(8,128)(2,1)S(1)}, u32[]{:S(2)}, u32[]{:S(2)}) collective-permute-start(bf16[3,112,512]{2,1,0:T(8,128)(2,1)} %get-tuple-element.82), channel_id=1, source_target_pairs={{0,2},{1,3},{2,0},{3,1},{4,6},{5,7},{6,4},{7,5},{8,10},{9,11},{10,... | collective-permute-start | bytes 1032200 | tf_op jit(solution)/shard_map/ppermute | solution.py:214
  142.6 24.5 %collective-permute-start.23 = (bf16[3,112,512]{2,1,0:T(8,128)(2,1)}, bf16[3,112,512]{2,1,0:T(8,128)(2,1)S(1)}, u32[]{:S(2)}, u32[]{:S(2)}) collective-permute-start(bf16[3,112,512]{2,1,0:T(8,128)(2,1)} %get-tuple-element.83), channel_id=1, source_target_pairs={{0,4},{1,5},{2,6},{3,7},{4,0},{5,1},{6,2},{7,3},{8,12},{9,13},{10,... | collective-permute-start | bytes 1032200 | tf_op jit(solution)/shard_map/ppermute | solution.py:214
  148.5 22.4 %collective-permute-start.24 = (bf16[3,112,512]{2,1,0:T(8,128)(2,1)}, bf16[3,112,512]{2,1,0:T(8,128)(2,1)S(1)}, u32[]{:S(2)}, u32[]{:S(2)}) collective-permute-start(bf16[3,112,512]{2,1,0:T(8,128)(2,1)} %get-tuple-element.84), channel_id=1, source_target_pairs={{0,3},{1,2},{2,1},{3,0},{4,7},{5,6},{6,5},{7,4},{8,11},{9,10},{10,... | collective-permute-start | bytes 1032200 | tf_op jit(solution)/shard_map/ppermute | solution.py:214
  149.4 21.6 %collective-permute-start.25 = (bf16[3,112,512]{2,1,0:T(8,128)(2,1)}, bf16[3,112,512]{2,1,0:T(8,128)(2,1)S(1)}, u32[]{:S(2)}, u32[]{:S(2)}) collective-permute-start(bf16[3,112,512]{2,1,0:T(8,128)(2,1)} %get-tuple-element.85), channel_id=1, source_target_pairs={{0,5},{1,4},{2,7},{3,6},{4,1},{5,0},{6,3},{7,2},{8,13},{9,12},{10,... | collective-permute-start | bytes 1032200 | tf_op jit(solution)/shard_map/ppermute | solution.py:214
  155.2 22.3 %collective-permute-start.26 = (bf16[3,112,512]{2,1,0:T(8,128)(2,1)}, bf16[3,112,512]{2,1,0:T(8,128)(2,1)S(1)}, u32[]{:S(2)}, u32[]{:S(2)}) collective-permute-start(bf16[3,112,512]{2,1,0:T(8,128)(2,1)} %get-tuple-element.86), channel_id=1, source_target_pairs={{0,7},{1,6},{2,5},{3,4},{4,3},{5,2},{6,1},{7,0},{8,15},{9,14},{10,... | collective-permute-start | bytes 1032200 | tf_op jit(solution)/shard_map/ppermute | solution.py:214
  162.6 14.9 %collective-permute-start.27 = (bf16[3,112,512]{2,1,0:T(8,128)(2,1)}, bf16[3,112,512]{2,1,0:T(8,128)(2,1)S(1)}, u32[]{:S(2)}, u32[]{:S(2)}) collective-permute-start(bf16[3,112,512]{2,1,0:T(8,128)(2,1)} %get-tuple-element.87), channel_id=1, source_target_pairs={{0,1},{1,0},{2,3},{3,2},{4,5},{5,4},{6,7},{7,6},{8,9},{9,8},{10,11... | collective-permute-start | bytes 1032200 | tf_op jit(solution)/shard_map/ppermute | solution.py:214
  (41 other events, 351.8 us)

commit v5 on v4

--- a/solution.py
+++ b/solution.py
@@ -17,7 +17,7 @@
 BF = jnp.bfloat16
 F32 = jnp.float32
 CHUNK = 16
-LIMIT = 56 * 1024 * 1024
+LIMIT = 61 * 1024 * 1024
 FINE = 256
 SPLIT = (2, 2)
 ORDER = (0, 6, 2, 4, 3, 5, 7, 1)

time: 182 us -> 181 us (level)
    unnamed x108 -> x56, local copies, waits for them, and re-layouts: 5.07 us -> 3.26 us
where the time goes in v5:
time: 181 us; the launch traced here: 180 us
  waiting for transfers between devices  94.9 us (52%)
  Pallas kernels  40.7 us (22%)
  starting transfers between devices  40.7 us (22%)
  local copies, waits for them, and re-layouts  3.26 us (2%)
    ppermute x35, waiting for transfers between devices, swap(): lax.ppermute(array, axis, [(i, i ^ k) for i in range(lax.axis_size(axis))])  94.9 us
    ppermute x35, starting transfers between devices, swap(): lax.ppermute(array, axis, [(i, i ^ k) for i in range(lax.axis_size(axis))])  40.7 us
    pallas_call x2, Pallas kernels, fast_local(): call(functools.partial(update_kernel, n), 4, (width // block,), [mine] *...  11.7 us
    pallas_call x2, Pallas kernels, pack(): call(functools.partial(pack_kernel, items), 1, (len(ks),), [pl.BlockSpec(...  8.41 us
    pallas_call x1, Pallas kernels, fast_local(): call(functools.partial(grad_kernel, n, count, rows), 1, (n,), [whole(tall...  8.38 us
    pallas_call x2, Pallas kernels, fast_local(): call(functools.partial(unpack_kernel, begin), 1, (), [hbm] * (n + len(res...  6.15 us
  transfers between devices with their start and end apart: 35, of which 17 were waited for; matrix products, arithmetic and copies ran while one was open for 0% of the time, Pallas kernels for 17%

profile of v5, /device:TPU:17, one launch (start us, length us, event | category | flops | bytes accessed | tf_op | source)
XLA Modules:
  0.0 180.4 jit_solution(10653871408337278873)
XLA Ops:
  0.6 4.5 %shard_map.112 = (bf16[2,3,112,1024]{3,2,1,0:T(8,128)(2,1)}, bf16[2,3,112,1024]{3,2,1,0:T(8,128)(2,1)}) custom-call(s32[1]{0:T(128)} %bitcast.me.me_ref, f32[896,1024]{1,0:T(8,128)} %bitcast.11, bf16[896,1024]{1,0:T(8,128)(2,1)} %bitcast.15, bf16[896,1024]{1,0:T(8,128)(2,1)} %bitcast.19), custom_call_target="tpu_custom_call" | custom-call | tf_op jit(solution)/shard_map/pallas_call | solution.py:263
  5.1 1.2 collective-permute-start
  6.3 1.2 collective-permute-start.1
  7.6 3.3 %shard_map.113 = (bf16[1920,128]{1,0:T(8,128)(2,1)}, bf16[1920,128]{1,0:T(8,128)(2,1)}, bf16[1920,128]{1,0:T(8,128)(2,1)}, bf16[1920,128]{1,0:T(8,128)(2,1)}) custom-call(s32[1]{0:T(128)} %bitcast.4.group, s32[2]{0:T(128)} %bitcast.28, bf16[3584,128]{1,0:T(8,128)(2,1)} %bitcast.26, bf16[2,64,1024]{2,1,0:T(8,128)(2,1)} %bitcast.27, ...), custom_call_target="tpu_custom_call" | custom-call | tf_op jit(solution)/shard_map/pallas_call | solution.py:276
  10.9 3.9 %shard_map.114 = (bf16[2,3,112,1024]{3,2,1,0:T(8,128)(2,1)}, bf16[1,3,112,1024]{3,2,1,0:T(8,128)(2,1)}) custom-call(s32[1]{0:T(128)} %bitcast.me.me_ref, f32[896,1024]{1,0:T(8,128)} %bitcast.12, bf16[896,1024]{1,0:T(8,128)(2,1)} %bitcast.16, bf16[896,1024]{1,0:T(8,128)(2,1)} %bitcast.20, bf16[1920,128]{1,0:T(8,128)(2,1)} %get-tuple-element.53.refs_0_), custom_call_target="tpu_custom_call" | custom-call | tf_op jit(solution)/shard_map/pallas_call | solution.py:263
  15.0 1.3 collective-permute-start.3
  16.4 19.4 %collective-permute-done.3.refs_1_ = bf16[1920,128]{1,0:T(8,128)(2,1)} collective-permute-done((bf16[1920,128]{1,0:T(8,128)(2,1)}, bf16[1920,128]{1,0:T(8,128)(2,1)}, u32[]{:S(2)}, u32[]{:S(2)}) %collective-permute-start.3) | collective-permute-done | bytes 491552 | tf_op jit(solution)/shard_map/ppermute | solution.py:214
  35.7 1.3 collective-permute-done.4.refs_2_
  37.0 23.2 %collective-permute-done.5.refs_3_ = bf16[1920,128]{1,0:T(8,128)(2,1)} collective-permute-done((bf16[1920,128]{1,0:T(8,128)(2,1)}, bf16[1920,128]{1,0:T(8,128)(2,1)}, u32[]{:S(2)}, u32[]{:S(2)}) %collective-permute-start.5) | collective-permute-done | bytes 491552 | tf_op jit(solution)/shard_map/ppermute | solution.py:214
  60.2 8.4 %shard_map.115 = (bf16[2,112,512]{2,1,0:T(8,128)(2,1)}, bf16[2,112,512]{2,1,0:T(8,128)(2,1)}, bf16[2,112,512]{2,1,0:T(8,128)(2,1)}, bf16[2,112,512]{2,1,0:T(8,12...) custom-call(s32[1]{0:T(128)} %bitcast.me.me_ref, ...), custom_call_target="tpu_custom_call" | custom-call | tf_op jit(solution)/shard_map/pallas_call | solution.py:289
  70.1 2.7 %shard_map.117 = bf16[4,3,112,1024]{3,2,1,0:T(8,128)(2,1)} custom-call(bf16[1,3,112,1024]{3,2,1,0:T(8,128)(2,1)} %get-tuple-element.54.refs_0_, bf16[2,3,112,1024]{3,2,1,0:T(8,128)(2,1)} %get-tuple-element.61.refs_1_.refs_4_, bf16[2,3,112,1024]{3,2,1,0:T(8,128)(2,1)} %get-tuple-element.62.refs_2_.refs_6_, ...), custom_call_target="tpu_custom_call" | custom-call | tf_op jit(solution)/shard_map/pallas_call | solution.py:303
  72.8 1.6 collective-permute-start.6
  74.5 2.2 %collective-permute-start.7 = (bf16[2,112,512]{2,1,0:T(8,128)(2,1)}, bf16[2,112,512]{2,1,0:T(8,128)(2,1)S(1)}, u32[]{:S(2)}, u32[]{:S(2)}) collective-permute-start(bf16[2,112,512]{2,1,0:T(8,128)(2,1)} %get-tuple-element.65), channel_id=1, source_target_pairs={{0,6},{1,7},{2,4},{3,5},{4,2},{5,3},{6,0},{7,1},{8,14},{9,15},{10,... | collective-permute-start | bytes 688136 | tf_op jit(solution)/shard_map/ppermute | solution.py:214
  76.8 1.2 collective-permute-start.15
  78.1 1.2 collective-permute-start.16
  79.3 3.5 %collective-permute-done.7.refs_11_ = bf16[2,112,512]{2,1,0:T(8,128)(2,1)S(1)} collective-permute-done((bf16[2,112,512]{2,1,0:T(8,128)(2,1)}, bf16[2,112,512]{2,1,0:T(8,128)(2,1)S(1)}, u32[]{:S(2)}, u32[]{:S(2)}) %collective-permute-start.7) | collective-permute-done | bytes 229408 | tf_op jit(solution)/shard_map/ppermute | solution.py:214
  82.8 2.5 %collective-permute-start.17 = (bf16[2,112,512]{2,1,0:T(8,128)(2,1)}, bf16[2,112,512]{2,1,0:T(8,128)(2,1)S(1)}, u32[]{:S(2)}, u32[]{:S(2)}) collective-permute-start(bf16[2,112,512]{2,1,0:T(8,128)(2,1)} %get-tuple-element.75), channel_id=1, source_target_pairs={{0,3},{1,2},{2,1},{3,0},{4,7},{5,6},{6,5},{7,4},{8,11},{9,10},{10,... | collective-permute-start | bytes 688136 | tf_op jit(solution)/shard_map/ppermute | solution.py:214
  85.3 2.5 %collective-permute-done.14.refs_11_ = bf16[2,112,512]{2,1,0:T(8,128)(2,1)S(1)} collective-permute-done((bf16[2,112,512]{2,1,0:T(8,128)(2,1)}, bf16[2,112,512]{2,1,0:T(8,128)(2,1)S(1)}, u32[]{:S(2)}, u32[]{:S(2)}) %collective-permute-start.14) | collective-permute-done | bytes 229408 | tf_op jit(solution)/shard_map/ppermute | solution.py:214
  87.7 2.4 %collective-permute-start.18 = (bf16[2,112,512]{2,1,0:T(8,128)(2,1)}, bf16[2,112,512]{2,1,0:T(8,128)(2,1)S(1)}, u32[]{:S(2)}, u32[]{:S(2)}) collective-permute-start(bf16[2,112,512]{2,1,0:T(8,128)(2,1)} %get-tuple-element.76), channel_id=1, source_target_pairs={{0,5},{1,4},{2,7},{3,6},{4,1},{5,0},{6,3},{7,2},{8,13},{9,12},{10,... | collective-permute-start | bytes 688136 | tf_op jit(solution)/shard_map/ppermute | solution.py:214
  90.1 2.5 %collective-permute-done.15.refs_12_ = bf16[2,112,512]{2,1,0:T(8,128)(2,1)S(1)} collective-permute-done((bf16[2,112,512]{2,1,0:T(8,128)(2,1)}, bf16[2,112,512]{2,1,0:T(8,128)(2,1)S(1)}, u32[]{:S(2)}, u32[]{:S(2)}) %collective-permute-start.15) | collective-permute-done | bytes 229408 | tf_op jit(solution)/shard_map/ppermute | solution.py:214
  92.7 2.3 %collective-permute-start.19 = (bf16[2,112,512]{2,1,0:T(8,128)(2,1)}, bf16[2,112,512]{2,1,0:T(8,128)(2,1)S(1)}, u32[]{:S(2)}, u32[]{:S(2)}) collective-permute-start(bf16[2,112,512]{2,1,0:T(8,128)(2,1)} %get-tuple-element.77), channel_id=1, source_target_pairs={{0,7},{1,6},{2,5},{3,4},{4,3},{5,2},{6,1},{7,0},{8,15},{9,14},{10,... | collective-permute-start | bytes 688136 | tf_op jit(solution)/shard_map/ppermute | solution.py:214
  95.0 3.5 %collective-permute-done.17.refs_14_ = bf16[2,112,512]{2,1,0:T(8,128)(2,1)S(1)} collective-permute-done((bf16[2,112,512]{2,1,0:T(8,128)(2,1)}, bf16[2,112,512]{2,1,0:T(8,128)(2,1)S(1)}, u32[]{:S(2)}, u32[]{:S(2)}) %collective-permute-start.17) | collective-permute-done | bytes 229408 | tf_op jit(solution)/shard_map/ppermute | solution.py:214
  98.5 1.2 collective-permute-start.8
  99.7 3.1 %collective-permute-done.19.refs_16_ = bf16[2,112,512]{2,1,0:T(8,128)(2,1)S(1)} collective-permute-done((bf16[2,112,512]{2,1,0:T(8,128)(2,1)}, bf16[2,112,512]{2,1,0:T(8,128)(2,1)S(1)}, u32[]{:S(2)}, u32[]{:S(2)}) %collective-permute-start.19) | collective-permute-done | bytes 229408 | tf_op jit(solution)/shard_map/ppermute | solution.py:214
  102.9 1.4 collective-permute-start.10
  104.3 1.5 collective-permute-start.11
  107.4 5.8 %shard_map.118 = (bf16[3,112,512]{2,1,0:T(8,128)(2,1)}, bf16[3,112,512]{2,1,0:T(8,128)(2,1)}, bf16[3,112,512]{2,1,0:T(8,128)(2,1)}, bf16[3,112,512]{2,1,0:T(8,12...) custom-call(s32[1]{0:T(128)} %bitcast.me.me_ref, ...), custom_call_target="tpu_custom_call" | custom-call | tf_op jit(solution)/shard_map/pallas_call | solution.py:330
  114.4 1.5 collective-permute-start.30
  117.9 1.6 collective-permute-done.13.refs_17_
  119.5 1.5 collective-permute-start.32
  121.0 5.9 %shard_map.119 = (bf16[3,112,512]{2,1,0:T(8,128)(2,1)}, bf16[3,112,512]{2,1,0:T(8,128)(2,1)}, bf16[3,112,512]{2,1,0:T(8,128)(2,1)}, bf16[3,112,512]{2,1,0:T(8,12...) custom-call(s32[1]{0:T(128)} %bitcast.me.me_ref, ...), custom_call_target="tpu_custom_call" | custom-call | tf_op jit(solution)/shard_map/pallas_call | solution.py:330
  126.9 1.7 collective-permute-start.33
  128.6 3.4 %collective-permute-done.29.refs_2_ = bf16[3,112,512]{2,1,0:T(8,128)(2,1)S(1)} collective-permute-done((bf16[3,112,512]{2,1,0:T(8,128)(2,1)}, bf16[3,112,512]{2,1,0:T(8,128)(2,1)S(1)}, u32[]{:S(2)}, u32[]{:S(2)}) %collective-permute-start.29) | collective-permute-done | bytes 344096 | tf_op jit(solution)/shard_map/ppermute | solution.py:214
  132.1 1.3 collective-permute-start.34
  133.4 1.1 collective-permute-start.21
  134.5 5.8 %collective-permute-done.31.refs_4_ = bf16[3,112,512]{2,1,0:T(8,128)(2,1)S(1)} collective-permute-done((bf16[3,112,512]{2,1,0:T(8,128)(2,1)}, bf16[3,112,512]{2,1,0:T(8,128)(2,1)S(1)}, u32[]{:S(2)}, u32[]{:S(2)}) %collective-permute-start.31) | collective-permute-done | bytes 344096 | tf_op jit(solution)/shard_map/ppermute | solution.py:214
  140.3 1.2 collective-permute-start.22
  141.6 5.6 %collective-permute-done.33.refs_6_ = bf16[3,112,512]{2,1,0:T(8,128)(2,1)S(1)} collective-permute-done((bf16[3,112,512]{2,1,0:T(8,128)(2,1)S(1)}, bf16[3,112,512]{2,1,0:T(8,128)(2,1)S(1)}, u32[]{:S(2)}, u32[]{:S(2)}) %collective-permute-start.33) | collective-permute-done | bytes 344096 | tf_op jit(solution)/shard_map/ppermute | solution.py:214
  147.3 1.3 collective-permute-start.24
  148.6 1.7 collective-permute-start.25
  150.3 4.1 %collective-permute-done.21.refs_1_ = bf16[3,112,512]{2,1,0:T(8,128)(2,1)S(1)} collective-permute-done((bf16[3,112,512]{2,1,0:T(8,128)(2,1)}, bf16[3,112,512]{2,1,0:T(8,128)(2,1)S(1)}, u32[]{:S(2)}, u32[]{:S(2)}) %collective-permute-start.21) | collective-permute-done | bytes 344096 | tf_op jit(solution)/shard_map/ppermute | solution.py:214
  154.4 3.2 %collective-permute-start.26 = (bf16[3,112,512]{2,1,0:T(8,128)(2,1)}, bf16[3,112,512]{2,1,0:T(8,128)(2,1)S(1)}, u32[]{:S(2)}, u32[]{:S(2)}) collective-permute-start(bf16[3,112,512]{2,1,0:T(8,128)(2,1)} %get-tuple-element.86), channel_id=1, source_target_pairs={{0,7},{1,6},{2,5},{3,4},{4,3},{5,2},{6,1},{7,0},{8,15},{9,14},{10,... | collective-permute-start | bytes 1032200 | tf_op jit(solution)/shard_map/ppermute | solution.py:214
  157.5 4.1 %collective-permute-done.22.refs_2_ = bf16[3,112,512]{2,1,0:T(8,128)(2,1)S(1)} collective-permute-done((bf16[3,112,512]{2,1,0:T(8,128)(2,1)}, bf16[3,112,512]{2,1,0:T(8,128)(2,1)S(1)}, u32[]{:S(2)}, u32[]{:S(2)}) %collective-permute-start.22) | collective-permute-done | bytes 344096 | tf_op jit(solution)/shard_map/ppermute | solution.py:214
  161.6 1.3 collective-permute-start.27
  162.9 3.1 %shard_map.120 = (f32[896,1024]{1,0:T(8,128)}, bf16[896,1024]{1,0:T(8,128)(2,1)}, bf16[896,1024]{1,0:T(8,128)(2,1)}) custom-call(s32[1]{0:T(128)} %bitcast.me.me_ref, bf16[3,112,512]{2,1,0:T(8,128)(2,1)} %get-tuple-element.79.refs_18_.refs_0_, bf16[3,112,512]{2,1,0:T(8,128)(2,1)} %copy-done.10, bf16[3,112,512]{2,1,0:T(8,128)(2,1)} %copy-done.11, ...), custom_call_target="tpu_custom_call" | custom-call | tf_op jit(solution)/shard_map/pallas_call | solution.py:352
  166.0 3.9 %collective-permute-done.24.refs_4_ = bf16[3,112,512]{2,1,0:T(8,128)(2,1)S(1)} collective-permute-done((bf16[3,112,512]{2,1,0:T(8,128)(2,1)}, bf16[3,112,512]{2,1,0:T(8,128)(2,1)S(1)}, u32[]{:S(2)}, u32[]{:S(2)}) %collective-permute-start.24) | collective-permute-done | bytes 344096 | tf_op jit(solution)/shard_map/ppermute | solution.py:214
  169.9 6.6 %collective-permute-done.26.refs_6_ = bf16[3,112,512]{2,1,0:T(8,128)(2,1)S(1)} collective-permute-done((bf16[3,112,512]{2,1,0:T(8,128)(2,1)}, bf16[3,112,512]{2,1,0:T(8,128)(2,1)S(1)}, u32[]{:S(2)}, u32[]{:S(2)}) %collective-permute-start.26) | collective-permute-done | bytes 344096 | tf_op jit(solution)/shard_map/ppermute | solution.py:214
  177.3 3.1 %shard_map.121 = (f32[896,1024]{1,0:T(8,128)}, bf16[896,1024]{1,0:T(8,128)(2,1)}, bf16[896,1024]{1,0:T(8,128)(2,1)}) custom-call(s32[1]{0:T(128)} %bitcast.me.me_ref, bf16[3,112,512]{2,1,0:T(8,128)(2,1)} %get-tuple-element.80.refs_0_, bf16[3,112,512]{2,1,0:T(8,128)(2,1)} %copy-done.3, ...), custom_call_target="tpu_custom_call", output_to_operand_aliasing={{0}: (9, {}), {1}: (10, {}), {2}: (11, {})} | custom-call | tf_op jit(solution)/shard_map/pallas_call | solution.py:352
  (88 shorter events, 7.6 us)
Async XLA Ops:
  5.1 63.5 %collective-permute-start = (bf16[2,3,112,1024]{3,2,1,0:T(8,128)(2,1)}, bf16[2,3,112,1024]{3,2,1,0:T(8,128)(2,1)S(1)}, u32[]{:S(2)}, u32[]{:S(2)}) collective-permute-start(bf16[2,3,112,1024]{3,2,1,0:T(8,128)(2,1)} %get-tuple-element.55), channel_id=1, source_target_pairs={{0,2},{1,3},{2,0},{3,1},{4,6},{5,7},{6,4},{7,5},{8,10},{9,11},{10,... | collective-permute-start | bytes 4128776 | tf_op jit(solution)/shard_map/ppermute | solution.py:214
  6.3 62.3 %collective-permute-start.1 = (bf16[2,3,112,1024]{3,2,1,0:T(8,128)(2,1)}, bf16[2,3,112,1024]{3,2,1,0:T(8,128)(2,1)S(1)}, u32[]{:S(2)}, u32[]{:S(2)}) collective-permute-start(bf16[2,3,112,1024]{3,2,1,0:T(8,128)(2,1)} %get-tuple-element.52.refs_0_), channel_id=1, source_target_pairs={{0,4},{1,5},{2,6},{3,7},{4,0},{5,1},{6,2},{7,3},{8,12},{9,13},{10,... | collective-permute-start | bytes 4128776 | tf_op jit(solution)/shard_map/ppermute | solution.py:214
  14.8 53.8 %collective-permute-start.2 = (bf16[2,3,112,1024]{3,2,1,0:T(8,128)(2,1)}, bf16[2,3,112,1024]{3,2,1,0:T(8,128)(2,1)}, u32[]{:S(2)}, u32[]{:S(2)}) collective-permute-start(bf16[2,3,112,1024]{3,2,1,0:T(8,128)(2,1)} %get-tuple-element.56), channel_id=1, source_target_pairs={{0,6},{1,7},{2,4},{3,5},{4,2},{5,3},{6,0},{7,1},{8,14},{9,15},{10,... | collective-permute-start | bytes 4128776 | tf_op jit(solution)/shard_map/ppermute | solution.py:214
  15.0 20.7 %collective-permute-start.3 = (bf16[1920,128]{1,0:T(8,128)(2,1)}, bf16[1920,128]{1,0:T(8,128)(2,1)}, u32[]{:S(2)}, u32[]{:S(2)}) collective-permute-start(bf16[1920,128]{1,0:T(8,128)(2,1)} %get-tuple-element.57), channel_id=1, source_target_pairs={{0,8},{8,0},{16,24},{24,16},{1,9},{9,1},{17,25},{25,17},{2,10},{10... | collective-permute-start | bytes 1474568 | tf_op jit(solution)/shard_map/ppermute | solution.py:214
  16.3 20.7 %collective-permute-start.4 = (bf16[1920,128]{1,0:T(8,128)(2,1)}, bf16[1920,128]{1,0:T(8,128)(2,1)}, u32[]{:S(2)}, u32[]{:S(2)}) collective-permute-start(bf16[1920,128]{1,0:T(8,128)(2,1)} %get-tuple-element.58), channel_id=1, source_target_pairs={{0,16},{8,24},{16,0},{24,8},{1,17},{9,25},{17,1},{25,9},{2,18},{10... | collective-permute-start | bytes 1474568 | tf_op jit(solution)/shard_map/ppermute | solution.py:214
  35.7 24.5 %collective-permute-start.5 = (bf16[1920,128]{1,0:T(8,128)(2,1)}, bf16[1920,128]{1,0:T(8,128)(2,1)}, u32[]{:S(2)}, u32[]{:S(2)}) collective-permute-start(bf16[1920,128]{1,0:T(8,128)(2,1)} %get-tuple-element.59), channel_id=1, source_target_pairs={{0,24},{8,16},{16,8},{24,0},{1,25},{9,17},{17,9},{25,1},{2,26},{10... | collective-permute-start | bytes 1474568 | tf_op jit(solution)/shard_map/ppermute | solution.py:214
  72.8 33.0 %collective-permute-start.6 = (bf16[4,3,112,1024]{3,2,1,0:T(8,128)(2,1)}, bf16[4,3,112,1024]{3,2,1,0:T(8,128)(2,1)S(1)}, u32[]{:S(2)}, u32[]{:S(2)}) collective-permute-start(bf16[4,3,112,1024]{3,2,1,0:T(8,128)(2,1)} %shard_map.117), channel_id=1, source_target_pairs={{0,1},{1,0},{2,3},{3,2},{4,5},{5,4},{6,7},{7,6},{8,9},{9,8},{10,11... | collective-permute-start | bytes 8257544 | tf_op jit(solution)/shard_map/ppermute | solution.py:214
  74.5 8.3 %collective-permute-start.7 = (bf16[2,112,512]{2,1,0:T(8,128)(2,1)}, bf16[2,112,512]{2,1,0:T(8,128)(2,1)S(1)}, u32[]{:S(2)}, u32[]{:S(2)}) collective-permute-start(bf16[2,112,512]{2,1,0:T(8,128)(2,1)} %get-tuple-element.65), channel_id=1, source_target_pairs={{0,6},{1,7},{2,4},{3,5},{4,2},{5,3},{6,0},{7,1},{8,14},{9,15},{10,... | collective-permute-start | bytes 688136 | tf_op jit(solution)/shard_map/ppermute | solution.py:214
  76.7 11.1 %collective-permute-start.14 = (bf16[2,112,512]{2,1,0:T(8,128)(2,1)}, bf16[2,112,512]{2,1,0:T(8,128)(2,1)S(1)}, u32[]{:S(2)}, u32[]{:S(2)}) collective-permute-start(bf16[2,112,512]{2,1,0:T(8,128)(2,1)} %get-tuple-element.72), channel_id=1, source_target_pairs={{0,6},{1,7},{2,4},{3,5},{4,2},{5,3},{6,0},{7,1},{8,14},{9,15},{10,... | collective-permute-start | bytes 688136 | tf_op jit(solution)/shard_map/ppermute | solution.py:214
  76.8 15.8 %collective-permute-start.15 = (bf16[2,112,512]{2,1,0:T(8,128)(2,1)}, bf16[2,112,512]{2,1,0:T(8,128)(2,1)S(1)}, u32[]{:S(2)}, u32[]{:S(2)}) collective-permute-start(bf16[2,112,512]{2,1,0:T(8,128)(2,1)} %get-tuple-element.73), channel_id=1, source_target_pairs={{0,2},{1,3},{2,0},{3,1},{4,6},{5,7},{6,4},{7,5},{8,10},{9,11},{10,... | collective-permute-start | bytes 688136 | tf_op jit(solution)/shard_map/ppermute | solution.py:214
  78.1 17.0 %collective-permute-start.16 = (bf16[2,112,512]{2,1,0:T(8,128)(2,1)}, bf16[2,112,512]{2,1,0:T(8,128)(2,1)S(1)}, u32[]{:S(2)}, u32[]{:S(2)}) collective-permute-start(bf16[2,112,512]{2,1,0:T(8,128)(2,1)} %get-tuple-element.74), channel_id=1, source_target_pairs={{0,4},{1,5},{2,6},{3,7},{4,0},{5,1},{6,2},{7,3},{8,12},{9,13},{10,... | collective-permute-start | bytes 688136 | tf_op jit(solution)/shard_map/ppermute | solution.py:214
  82.8 30.4 %copy-start.17 = (bf16[2,112,512]{2,1,0:T(8,128)(2,1)}, bf16[2,112,512]{2,1,0:T(8,128)(2,1)S(1)}, u32[]{:S(2)}) copy-start(bf16[2,112,512]{2,1,0:T(8,128)(2,1)S(1)} %collective-permute-done.7.refs_11_) | copy-start | bytes 688132
  82.8 15.7 %collective-permute-start.17 = (bf16[2,112,512]{2,1,0:T(8,128)(2,1)}, bf16[2,112,512]{2,1,0:T(8,128)(2,1)S(1)}, u32[]{:S(2)}, u32[]{:S(2)}) collective-permute-start(bf16[2,112,512]{2,1,0:T(8,128)(2,1)} %get-tuple-element.75), channel_id=1, source_target_pairs={{0,3},{1,2},{2,1},{3,0},{4,7},{5,6},{6,5},{7,4},{8,11},{9,10},{10,... | collective-permute-start | bytes 688136 | tf_op jit(solution)/shard_map/ppermute | solution.py:214
  87.7 18.1 %copy-start.18 = (bf16[2,112,512]{2,1,0:T(8,128)(2,1)}, bf16[2,112,512]{2,1,0:T(8,128)(2,1)S(1)}, u32[]{:S(2)}) copy-start(bf16[2,112,512]{2,1,0:T(8,128)(2,1)S(1)} %collective-permute-done.14.refs_11_) | copy-start | bytes 688132
  87.7 12.0 %collective-permute-start.18 = (bf16[2,112,512]{2,1,0:T(8,128)(2,1)}, bf16[2,112,512]{2,1,0:T(8,128)(2,1)S(1)}, u32[]{:S(2)}, u32[]{:S(2)}) collective-permute-start(bf16[2,112,512]{2,1,0:T(8,128)(2,1)} %get-tuple-element.76), channel_id=1, source_target_pairs={{0,5},{1,4},{2,7},{3,6},{4,1},{5,0},{6,3},{7,2},{8,13},{9,12},{10,... | collective-permute-start | bytes 688136 | tf_op jit(solution)/shard_map/ppermute | solution.py:214
  92.7 13.1 %copy-start.19 = (bf16[2,112,512]{2,1,0:T(8,128)(2,1)}, bf16[2,112,512]{2,1,0:T(8,128)(2,1)S(1)}, u32[]{:S(2)}) copy-start(bf16[2,112,512]{2,1,0:T(8,128)(2,1)S(1)} %collective-permute-done.15.refs_12_) | copy-start | bytes 688132
  92.7 10.2 %collective-permute-start.19 = (bf16[2,112,512]{2,1,0:T(8,128)(2,1)}, bf16[2,112,512]{2,1,0:T(8,128)(2,1)S(1)}, u32[]{:S(2)}, u32[]{:S(2)}) collective-permute-start(bf16[2,112,512]{2,1,0:T(8,128)(2,1)} %get-tuple-element.77), channel_id=1, source_target_pairs={{0,7},{1,6},{2,5},{3,4},{4,3},{5,2},{6,1},{7,0},{8,15},{9,14},{10,... | collective-permute-start | bytes 688136 | tf_op jit(solution)/shard_map/ppermute | solution.py:214
  95.0 10.8 %copy-start.20 = (bf16[2,112,512]{2,1,0:T(8,128)(2,1)}, bf16[2,112,512]{2,1,0:T(8,128)(2,1)S(1)}, u32[]{:S(2)}) copy-start(bf16[2,112,512]{2,1,0:T(8,128)(2,1)S(1)} %collective-permute-done.16.refs_13_) | copy-start | bytes 688132
  95.0 9.2 %collective-permute-start.20 = (bf16[2,112,512]{2,1,0:T(8,128)(2,1)}, bf16[2,112,512]{2,1,0:T(8,128)(2,1)S(1)}, u32[]{:S(2)}, u32[]{:S(2)}) collective-permute-start(bf16[2,112,512]{2,1,0:T(8,128)(2,1)} %get-tuple-element.78), channel_id=1, source_target_pairs={{0,1},{1,0},{2,3},{3,2},{4,5},{5,4},{6,7},{7,6},{8,9},{9,8},{10,11... | collective-permute-start | bytes 688136 | tf_op jit(solution)/shard_map/ppermute | solution.py:214
  98.5 7.3 %copy-start.21 = (bf16[2,112,512]{2,1,0:T(8,128)(2,1)}, bf16[2,112,512]{2,1,0:T(8,128)(2,1)S(1)}, u32[]{:S(2)}) copy-start(bf16[2,112,512]{2,1,0:T(8,128)(2,1)S(1)} %collective-permute-done.17.refs_14_) | copy-start | bytes 688132
  98.5 14.7 %collective-permute-start.8 = (bf16[2,112,512]{2,1,0:T(8,128)(2,1)}, bf16[2,112,512]{2,1,0:T(8,128)(2,1)}, u32[]{:S(2)}, u32[]{:S(2)}) collective-permute-start(bf16[2,112,512]{2,1,0:T(8,128)(2,1)} %get-tuple-element.66), channel_id=1, source_target_pairs={{0,2},{1,3},{2,0},{3,1},{4,6},{5,7},{6,4},{7,5},{8,10},{9,11},{10,... | collective-permute-start | bytes 688136 | tf_op jit(solution)/shard_map/ppermute | solution.py:214
  99.7 14.2 %collective-permute-start.9 = (bf16[2,112,512]{2,1,0:T(8,128)(2,1)}, bf16[2,112,512]{2,1,0:T(8,128)(2,1)}, u32[]{:S(2)}, u32[]{:S(2)}) collective-permute-start(bf16[2,112,512]{2,1,0:T(8,128)(2,1)} %get-tuple-element.67), channel_id=1, source_target_pairs={{0,4},{1,5},{2,6},{3,7},{4,0},{5,1},{6,2},{7,3},{8,12},{9,13},{10,... | collective-permute-start | bytes 688136 | tf_op jit(solution)/shard_map/ppermute | solution.py:214
  102.9 11.6 %collective-permute-start.10 = (bf16[2,112,512]{2,1,0:T(8,128)(2,1)}, bf16[2,112,512]{2,1,0:T(8,128)(2,1)}, u32[]{:S(2)}, u32[]{:S(2)}) collective-permute-start(bf16[2,112,512]{2,1,0:T(8,128)(2,1)} %get-tuple-element.68), channel_id=1, source_target_pairs={{0,3},{1,2},{2,1},{3,0},{4,7},{5,6},{6,5},{7,4},{8,11},{9,10},{10,... | collective-permute-start | bytes 688136 | tf_op jit(solution)/shard_map/ppermute | solution.py:214
  104.3 11.6 %collective-permute-start.11 = (bf16[2,112,512]{2,1,0:T(8,128)(2,1)}, bf16[2,112,512]{2,1,0:T(8,128)(2,1)}, u32[]{:S(2)}, u32[]{:S(2)}) collective-permute-start(bf16[2,112,512]{2,1,0:T(8,128)(2,1)} %get-tuple-element.69), channel_id=1, source_target_pairs={{0,5},{1,4},{2,7},{3,6},{4,1},{5,0},{6,3},{7,2},{8,13},{9,12},{10,... | collective-permute-start | bytes 688136 | tf_op jit(solution)/shard_map/ppermute | solution.py:214
  105.9 11.9 %collective-permute-start.12 = (bf16[2,112,512]{2,1,0:T(8,128)(2,1)}, bf16[2,112,512]{2,1,0:T(8,128)(2,1)}, u32[]{:S(2)}, u32[]{:S(2)}) collective-permute-start(bf16[2,112,512]{2,1,0:T(8,128)(2,1)} %get-tuple-element.70), channel_id=1, source_target_pairs={{0,7},{1,6},{2,5},{3,4},{4,3},{5,2},{6,1},{7,0},{8,15},{9,14},{10,... | collective-permute-start | bytes 688136 | tf_op jit(solution)/shard_map/ppermute | solution.py:214
  113.2 13.7 %collective-permute-start.28 = (bf16[3,112,512]{2,1,0:T(8,128)(2,1)}, bf16[3,112,512]{2,1,0:T(8,128)(2,1)S(1)}, u32[]{:S(2)}, u32[]{:S(2)}) collective-permute-start(bf16[3,112,512]{2,1,0:T(8,128)(2,1)} %get-tuple-element.88), channel_id=1, source_target_pairs={{0,6},{1,7},{2,4},{3,5},{4,2},{5,3},{6,0},{7,1},{8,14},{9,15},{10,... | collective-permute-start | bytes 1032200 | tf_op jit(solution)/shard_map/ppermute | solution.py:214
  114.0 18.1 %collective-permute-start.29 = (bf16[3,112,512]{2,1,0:T(8,128)(2,1)}, bf16[3,112,512]{2,1,0:T(8,128)(2,1)S(1)}, u32[]{:S(2)}, u32[]{:S(2)}) collective-permute-start(bf16[3,112,512]{2,1,0:T(8,128)(2,1)} %get-tuple-element.89), channel_id=1, source_target_pairs={{0,2},{1,3},{2,0},{3,1},{4,6},{5,7},{6,4},{7,5},{8,10},{9,11},{10,... | collective-permute-start | bytes 1032200 | tf_op jit(solution)/shard_map/ppermute | solution.py:214
  114.4 18.9 %collective-permute-start.30 = (bf16[3,112,512]{2,1,0:T(8,128)(2,1)}, bf16[3,112,512]{2,1,0:T(8,128)(2,1)S(1)}, u32[]{:S(2)}, u32[]{:S(2)}) collective-permute-start(bf16[3,112,512]{2,1,0:T(8,128)(2,1)} %get-tuple-element.90), channel_id=1, source_target_pairs={{0,4},{1,5},{2,6},{3,7},{4,0},{5,1},{6,2},{7,3},{8,12},{9,13},{10,... | collective-permute-start | bytes 1032200 | tf_op jit(solution)/shard_map/ppermute | solution.py:214
  115.9 24.4 %collective-permute-start.31 = (bf16[3,112,512]{2,1,0:T(8,128)(2,1)}, bf16[3,112,512]{2,1,0:T(8,128)(2,1)S(1)}, u32[]{:S(2)}, u32[]{:S(2)}) collective-permute-start(bf16[3,112,512]{2,1,0:T(8,128)(2,1)} %get-tuple-element.91), channel_id=1, source_target_pairs={{0,3},{1,2},{2,1},{3,0},{4,7},{5,6},{6,5},{7,4},{8,11},{9,10},{10,... | collective-permute-start | bytes 1032200 | tf_op jit(solution)/shard_map/ppermute | solution.py:214
  117.8 1.7 collective-permute-start.13
  119.5 22.1 %collective-permute-start.32 = (bf16[3,112,512]{2,1,0:T(8,128)(2,1)}, bf16[3,112,512]{2,1,0:T(8,128)(2,1)S(1)}, u32[]{:S(2)}, u32[]{:S(2)}) collective-permute-start(bf16[3,112,512]{2,1,0:T(8,128)(2,1)} %get-tuple-element.92), channel_id=1, source_target_pairs={{0,5},{1,4},{2,7},{3,6},{4,1},{5,0},{6,3},{7,2},{8,13},{9,12},{10,... | collective-permute-start | bytes 1032200 | tf_op jit(solution)/shard_map/ppermute | solution.py:214
  121.0 11.1 %copy-start.26 = (bf16[3,112,512]{2,1,0:T(8,128)(2,1)S(1)}, bf16[3,112,512]{2,1,0:T(8,128)(2,1)}, u32[]{:S(2)}) copy-start(bf16[3,112,512]{2,1,0:T(8,128)(2,1)} %get-tuple-element.94) | copy-start | bytes 1032196
  126.9 36.0 %copy-start.10 = (bf16[3,112,512]{2,1,0:T(8,128)(2,1)}, bf16[3,112,512]{2,1,0:T(8,128)(2,1)S(1)}, u32[]{:S(2)}) copy-start(bf16[3,112,512]{2,1,0:T(8,128)(2,1)S(1)} %collective-permute-done.28.refs_1_) | copy-start | bytes 1032196
  126.9 20.3 %collective-permute-start.33 = (bf16[3,112,512]{2,1,0:T(8,128)(2,1)S(1)}, bf16[3,112,512]{2,1,0:T(8,128)(2,1)S(1)}, u32[]{:S(2)}, u32[]{:S(2)}) collective-permute-start(bf16[3,112,512]{2,1,0:T(8,128)(2,1)S(1)} %copy-done.27), channel_id=1, source_target_pairs={{0,7},{1,6},{2,5},{3,4},{4,3},{5,2},{6,1},{7,0},{8,15},{9,14},{10,... | collective-permute-start | bytes 1032200 | tf_op jit(solution)/shard_map/ppermute | solution.py:214
  132.1 16.5 %collective-permute-start.34 = (bf16[3,112,512]{2,1,0:T(8,128)(2,1)S(1)}, bf16[3,112,512]{2,1,0:T(8,128)(2,1)S(1)}, u32[]{:S(2)}, u32[]{:S(2)}) collective-permute-start(bf16[3,112,512]{2,1,0:T(8,128)(2,1)S(1)} %copy-done.26), channel_id=1, source_target_pairs={{0,1},{1,0},{2,3},{3,2},{4,5},{5,4},{6,7},{7,6},{8,9},{9,8},{10,11... | collective-permute-start | bytes 1032200 | tf_op jit(solution)/shard_map/ppermute | solution.py:214
  133.4 7.0 %copy-start.12 = (bf16[3,112,512]{2,1,0:T(8,128)(2,1)}, bf16[3,112,512]{2,1,0:T(8,128)(2,1)S(1)}, u32[]{:S(2)}) copy-start(bf16[3,112,512]{2,1,0:T(8,128)(2,1)S(1)} %collective-permute-done.30.refs_3_) | copy-start | bytes 1032196
  133.4 21.0 %collective-permute-start.21 = (bf16[3,112,512]{2,1,0:T(8,128)(2,1)}, bf16[3,112,512]{2,1,0:T(8,128)(2,1)S(1)}, u32[]{:S(2)}, u32[]{:S(2)}) collective-permute-start(bf16[3,112,512]{2,1,0:T(8,128)(2,1)} %get-tuple-element.81), channel_id=1, source_target_pairs={{0,6},{1,7},{2,4},{3,5},{4,2},{5,3},{6,0},{7,1},{8,14},{9,15},{10,... | collective-permute-start | bytes 1032200 | tf_op jit(solution)/shard_map/ppermute | solution.py:214
  140.3 21.3 %collective-permute-start.22 = (bf16[3,112,512]{2,1,0:T(8,128)(2,1)}, bf16[3,112,512]{2,1,0:T(8,128)(2,1)S(1)}, u32[]{:S(2)}, u32[]{:S(2)}) collective-permute-start(bf16[3,112,512]{2,1,0:T(8,128)(2,1)} %get-tuple-element.82), channel_id=1, source_target_pairs={{0,2},{1,3},{2,0},{3,1},{4,6},{5,7},{6,4},{7,5},{8,10},{9,11},{10,... | collective-permute-start | bytes 1032200 | tf_op jit(solution)/shard_map/ppermute | solution.py:214
  141.6 24.4 %collective-permute-start.23 = (bf16[3,112,512]{2,1,0:T(8,128)(2,1)}, bf16[3,112,512]{2,1,0:T(8,128)(2,1)S(1)}, u32[]{:S(2)}, u32[]{:S(2)}) collective-permute-start(bf16[3,112,512]{2,1,0:T(8,128)(2,1)} %get-tuple-element.83), channel_id=1, source_target_pairs={{0,4},{1,5},{2,6},{3,7},{4,0},{5,1},{6,2},{7,3},{8,12},{9,13},{10,... | collective-permute-start | bytes 1032200 | tf_op jit(solution)/shard_map/ppermute | solution.py:214
  147.3 22.6 %collective-permute-start.24 = (bf16[3,112,512]{2,1,0:T(8,128)(2,1)}, bf16[3,112,512]{2,1,0:T(8,128)(2,1)S(1)}, u32[]{:S(2)}, u32[]{:S(2)}) collective-permute-start(bf16[3,112,512]{2,1,0:T(8,128)(2,1)} %get-tuple-element.84), channel_id=1, source_target_pairs={{0,3},{1,2},{2,1},{3,0},{4,7},{5,6},{6,5},{7,4},{8,11},{9,10},{10,... | collective-permute-start | bytes 1032200 | tf_op jit(solution)/shard_map/ppermute | solution.py:214
  148.6 21.3 %collective-permute-start.25 = (bf16[3,112,512]{2,1,0:T(8,128)(2,1)}, bf16[3,112,512]{2,1,0:T(8,128)(2,1)S(1)}, u32[]{:S(2)}, u32[]{:S(2)}) collective-permute-start(bf16[3,112,512]{2,1,0:T(8,128)(2,1)} %get-tuple-element.85), channel_id=1, source_target_pairs={{0,5},{1,4},{2,7},{3,6},{4,1},{5,0},{6,3},{7,2},{8,13},{9,12},{10,... | collective-permute-start | bytes 1032200 | tf_op jit(solution)/shard_map/ppermute | solution.py:214
  154.4 22.1 %copy-start.3 = (bf16[3,112,512]{2,1,0:T(8,128)(2,1)}, bf16[3,112,512]{2,1,0:T(8,128)(2,1)S(1)}, u32[]{:S(2)}) copy-start(bf16[3,112,512]{2,1,0:T(8,128)(2,1)S(1)} %collective-permute-done.21.refs_1_) | copy-start | bytes 1032196
  154.4 22.1 %collective-permute-start.26 = (bf16[3,112,512]{2,1,0:T(8,128)(2,1)}, bf16[3,112,512]{2,1,0:T(8,128)(2,1)S(1)}, u32[]{:S(2)}, u32[]{:S(2)}) collective-permute-start(bf16[3,112,512]{2,1,0:T(8,128)(2,1)} %get-tuple-element.86), channel_id=1, source_target_pairs={{0,7},{1,6},{2,5},{3,4},{4,3},{5,2},{6,1},{7,0},{8,15},{9,14},{10,... | collective-permute-start | bytes 1032200 | tf_op jit(solution)/shard_map/ppermute | solution.py:214
  161.6 14.9 %copy-start.4 = (bf16[3,112,512]{2,1,0:T(8,128)(2,1)}, bf16[3,112,512]{2,1,0:T(8,128)(2,1)S(1)}, u32[]{:S(2)}) copy-start(bf16[3,112,512]{2,1,0:T(8,128)(2,1)S(1)} %collective-permute-done.22.refs_2_) | copy-start | bytes 1032196
  161.6 14.9 %collective-permute-start.27 = (bf16[3,112,512]{2,1,0:T(8,128)(2,1)}, bf16[3,112,512]{2,1,0:T(8,128)(2,1)S(1)}, u32[]{:S(2)}, u32[]{:S(2)}) collective-permute-start(bf16[3,112,512]{2,1,0:T(8,128)(2,1)} %get-tuple-element.87), channel_id=1, source_target_pairs={{0,1},{1,0},{2,3},{3,2},{4,5},{5,4},{6,7},{7,6},{8,9},{9,8},{10,11... | collective-permute-start | bytes 1032200 | tf_op jit(solution)/shard_map/ppermute | solution.py:214
  166.0 10.5 %copy-start.5 = (bf16[3,112,512]{2,1,0:T(8,128)(2,1)}, bf16[3,112,512]{2,1,0:T(8,128)(2,1)S(1)}, u32[]{:S(2)}) copy-start(bf16[3,112,512]{2,1,0:T(8,128)(2,1)S(1)} %collective-permute-done.23.refs_3_) | copy-start | bytes 1032196
  169.9 6.7 %copy-start.6 = (bf16[3,112,512]{2,1,0:T(8,128)(2,1)}, bf16[3,112,512]{2,1,0:T(8,128)(2,1)S(1)}, u32[]{:S(2)}) copy-start(bf16[3,112,512]{2,1,0:T(8,128)(2,1)S(1)} %collective-permute-done.24.refs_4_) | copy-start | bytes 1032196
  169.9 6.7 %copy-start.7 = (bf16[3,112,512]{2,1,0:T(8,128)(2,1)}, bf16[3,112,512]{2,1,0:T(8,128)(2,1)S(1)}, u32[]{:S(2)}) copy-start(bf16[3,112,512]{2,1,0:T(8,128)(2,1)S(1)} %collective-permute-done.25.refs_5_) | copy-start | bytes 1032196
  (15 other events, 39.2 us)
